TPU v7x, 32 devices: a whole 2x2x4 slice. The times are simulated.
32 devices in a mesh: groups: 2 (over y), expert: 4 (over z), replica: 4 (over x, core).
Axes of the slice: x: 2, y: 2, z: 4, core: 2. Of those that a mesh axis runs over, the one named last changes fastest.
Arguments:
- tokens: bfloat16 [4096, 1024], P(('groups', 'expert', 'replica')), parts along dimension 0, may hold values from -6 to 6
- expert_ids: int32 [4096, 6], P(('groups', 'expert', 'replica')), parts along dimension 0, may hold values from 0 to 15, all different within a row; in each aligned block of 128 rows (0 to 127, 128 to 255, ...) at most 64 rows name the same one
- gate_probs: bfloat16 [4096, 6], P(('groups', 'expert', 'replica')), parts along dimension 0, may hold values from 0.099609375 to 0.59765625
- cotangent: bfloat16 [4096, 1024], P(('groups', 'expert', 'replica')), parts along dimension 0, may hold values from -1.5 to 1.5
- gate_up: bfloat16 [1024, 16, 1536], P(None, 'expert'), may hold values from -0.1875 to 0.1875
- down_weights: bfloat16 [768, 16, 1024], P(None, 'expert'), may hold values from -0.21875 to 0.21875
Outputs:
- combined: bfloat16 [4096, 1024], P(('groups', 'expert', 'replica')), parts along dimension 0
- token_gradient: bfloat16 [4096, 1024], P(('groups', 'expert', 'replica')), parts along dimension 0
- prob_gradient: float32 [4096, 6], P(('groups', 'expert', 'replica')), parts along dimension 0
- gate_up_gradient: float32 [2048, 16, 1536], P(('groups', 'replica'), 'expert'), parts along dimension 0
- down_gradient: float32 [1536, 16, 1024], P(('groups', 'replica'), 'expert'), parts along dimension 0
There are 2 independent parts, one for each index of `groups`. A program takes and returns all parts, laid end to end along the dimension named above; an argument that names none is the same for every part. Nothing has to cross between parts.
Inputs may be any that keep to these rules, and one draw needn't show every extreme that they name: `expert_ids`: each row names 6 different experts. Within the rows of one device (aligned blocks of 128 rows) no expert is named by more than 64 rows, and in some block one expert is named by exactly 64 rows.
All inputs are finite; a program needn't handle non-finite values.
Results may differ from a plain program's by a relative error of at most 0.0064.
Values may be sent and summed in bfloat16 or wider, within the bound.
No kernel may reach another device: no remote copies, remote signals or barrier semaphores. Data moves between devices by JAX's collectives and lax.ppermute only.
A program may use at most 128 MiB of HBM per device.

v0:
```python
import jax
import jax.numpy as jnp
from jax import lax
from jax.sharding import PartitionSpec as P

EXPERTS = 16
CAP = 64


def slot_table(expert_ids, experts, capacity):
    flat_ids = expert_ids.reshape(-1)
    assigned = flat_ids.shape[0]
    onehot = (flat_ids[:, None] == jnp.arange(experts, dtype=jnp.int32)[None, :]).astype(jnp.int32)
    before = jnp.cumsum(onehot, axis=0) - onehot
    slot_index = jnp.sum(before * onehot, axis=1)
    position = (flat_ids * capacity + slot_index).astype(jnp.int32)
    slot_owner = (
        jnp.full((experts * capacity,), assigned, jnp.int32)
        .at[position]
        .set(jnp.arange(assigned, dtype=jnp.int32))
    )
    return (position, slot_owner)


def expert_forward(received, gate_up, down_weights):
    local_count = gate_up.shape[1]
    blocks = received.reshape(
        received.shape[0] // local_count, local_count, received.shape[1], received.shape[2]
    )
    pre_act = jnp.einsum("secd,def->secf", blocks, gate_up, preferred_element_type=jnp.float32)
    middle = pre_act.shape[-1] // 2
    hidden = (jax.nn.silu(pre_act[..., :middle]) * pre_act[..., middle:]).astype(jnp.bfloat16)
    outputs = jnp.einsum(
        "secf,fed->secd", hidden, down_weights, preferred_element_type=jnp.float32
    ).astype(jnp.bfloat16)
    return (outputs.reshape(received.shape), pre_act, hidden)


def on_device(tokens, expert_ids, gate_probs, cotangent, gate_up, down_weights):
    tok_count, model_width = tokens.shape
    per_patch = expert_ids.shape[1]
    local_count = gate_up.shape[1]
    sources = EXPERTS // local_count
    position, slot_owner = slot_table(expert_ids, EXPERTS, CAP)
    all_tokens, all_ids = (
        lax.all_gather(tokens, "expert", axis=0, tiled=True),
        lax.all_gather(expert_ids, "expert", axis=0, tiled=True),
    )
    first_expert = lax.axis_index("expert") * local_count
    owner_tables = jax.vmap(lambda choose: slot_table(choose, EXPERTS, CAP)[1])(
        all_ids.reshape(sources, tok_count, per_patch)
    )
    mine = lax.dynamic_slice_in_dim(
        owner_tables.reshape(sources, EXPERTS, CAP), first_expert, local_count, 1
    ).reshape(sources, local_count * CAP)
    source_zeros = jnp.zeros((sources, 1, model_width), jnp.bfloat16)
    source_tokens = jnp.concatenate(
        [all_tokens.reshape(sources, tok_count, model_width), source_zeros], axis=1
    )
    received = jax.vmap(lambda values, owners: values[owners // per_patch])(
        source_tokens, mine
    ).reshape(EXPERTS, CAP, model_width)
    outputs, pre_act, hidden = expert_forward(received, gate_up, down_weights)
    returned = lax.all_to_all(outputs, "expert", split_axis=0, concat_axis=0, tiled=True)
    picked = (
        returned.reshape(EXPERTS * CAP, model_width)[position]
        .reshape(tok_count, per_patch, model_width)
        .astype(jnp.float32)
    )
    probs_float = gate_probs.astype(jnp.float32)
    combined = jnp.sum(probs_float[:, :, None] * picked, axis=1).astype(jnp.bfloat16)
    cot_float = cotangent.astype(jnp.float32)
    prob_gradient = jnp.sum(cot_float[:, None, :] * picked, axis=2)
    all_cot, all_probs = (
        lax.all_gather(cotangent, "expert", axis=0, tiled=True),
        lax.all_gather(gate_probs, "expert", axis=0, tiled=True),
    )
    source_cot = jnp.concatenate(
        [all_cot.reshape(sources, tok_count, model_width), source_zeros], axis=1
    )
    zero_probs = jnp.zeros((sources, 1), jnp.bfloat16)
    source_probs = jnp.concatenate(
        [all_probs.reshape(sources, tok_count * per_patch), zero_probs], axis=1
    )
    cot_rows = jax.vmap(lambda values, owners: values[owners // per_patch])(source_cot, mine)
    prob_rows = jax.vmap(lambda values, owners: values[owners])(source_probs, mine)
    cot_received = (
        (prob_rows[:, :, None].astype(jnp.float32) * cot_rows.astype(jnp.float32))
        .astype(jnp.bfloat16)
        .reshape(EXPERTS, CAP, model_width)
    )
    block_shape = (sources, local_count, CAP, model_width)
    slot_inputs = received.reshape(block_shape)
    slot_cotangent = cot_received.reshape(block_shape)
    middle = pre_act.shape[-1] // 2
    gate_part = pre_act[..., :middle]
    up_part = pre_act[..., middle:]
    hidden_grad = jnp.einsum(
        "secd,fed->secf", slot_cotangent, down_weights, preferred_element_type=jnp.float32
    )
    sigmoid_gate = jax.nn.sigmoid(gate_part)
    pre_gradient = jnp.concatenate(
        [
            hidden_grad * up_part * sigmoid_gate * (1.0 + gate_part * (1.0 - sigmoid_gate)),
            hidden_grad * gate_part * sigmoid_gate,
        ],
        axis=-1,
    ).astype(jnp.bfloat16)
    input_grads = jnp.einsum(
        "secf,def->secd", pre_gradient, gate_up, preferred_element_type=jnp.float32
    ).astype(jnp.bfloat16)
    returned_grads = lax.all_to_all(
        input_grads.reshape(EXPERTS, CAP, model_width),
        "expert",
        split_axis=0,
        concat_axis=0,
        tiled=True,
    )
    token_rows = returned_grads.reshape(EXPERTS * CAP, model_width)[position].reshape(
        tok_count, per_patch, model_width
    )
    token_gradient = jnp.sum(token_rows.astype(jnp.float32), axis=1).astype(jnp.bfloat16)
    full_inner = jnp.einsum(
        "secd,secf->def", slot_inputs, pre_gradient, preferred_element_type=jnp.float32
    )
    full_down = jnp.einsum(
        "secf,secd->fed", hidden, slot_cotangent, preferred_element_type=jnp.float32
    )
    gate_up_gradient, down_gradient = (
        lax.psum_scatter(full_inner, "replica", scatter_dimension=0, tiled=True),
        lax.psum_scatter(full_down, "replica", scatter_dimension=0, tiled=True),
    )
    return (combined, token_gradient, prob_gradient, gate_up_gradient, down_gradient)


def solution(mesh):
    placed = (
        P(("groups", "expert", "replica"), None),
        P(("groups", "expert", "replica"), None),
        P(("groups", "expert", "replica"), None),
        P(("groups", "expert", "replica"), None),
        P(None, "expert", None),
        P(None, "expert", None),
    )
    return jax.shard_map(
        on_device,
        mesh=mesh,
        in_specs=placed,
        out_specs=(
            P(("groups", "expert", "replica"), None),
            P(("groups", "expert", "replica"), None),
            P(("groups", "expert", "replica"), None),
            P(("groups", "replica"), "expert", None),
            P(("groups", "replica"), "expert", None),
        ),
        check_vma=False,
    )
```

profile of v0, /device:TPU:0, one launch (start us, length us, event | category | flops | bytes accessed | tf_op | source)
XLA Modules:
  0.0 558.3 jit_solution(15946966605619337818)
XLA Ops:
  8.7 15.0 %all_gather.13 = s32[512,6]{0,1:T(8,128)S(1)} all-gather(s32[128,6]{0,1:T(8,128)} %param.7), channel_id=1, replica_groups=mesh['groups'=2,'expert'=4,'replica'=4] {'expert'}, dimensions={0}, use_global_device_ids=true | all-gather | bytes 15360 | tf_op jit(solution)/shard_map/all_gather | solution.py:47
  24.2 12.1 %all_gather.14 = bf16[512,6]{0,1:T(8,128)(2,1)S(1)} all-gather(bf16[128,6]{0,1:T(8,128)(2,1)} %param.8), channel_id=1, replica_groups=mesh['groups'=2,'expert'=4,'replica'=4] {'expert'}, dimensions={0}, use_global_device_ids=true | all-gather | bytes 7680 | tf_op jit(solution)/shard_map/all_gather | solution.py:76
  36.8 6.8 %reduce-window.14 = s32[4,16,6,128]{3,1,2,0:T(8,128)S(1)} reduce-window(s32[4,16,6,128]{3,1,2,0:T(8,128)S(1)} %fusion.28, s32[]{:T(128)} %constant.19.clone.1), window={size=1x1x1x128 pad=0_0x0_0x0_0x127_0}, to_apply=%region_0.0 | reduce-window | flops 6242304 | bytes 393220 | tf_op jit(solution)/shard_map/reduce-window
  44.7 11.8 %scatter_custom_fusion = s32[4096]{0:T(1024)S(1)} fusion(s32[3072]{0:T(1024)S(1)} %reshape.287, s32[3072]{0:T(1024)S(1)} %reshape.289, s32[]{:T(128)} %constant.17.clone.1), kind=kCustom, calls=%fused_computation.62 | custom fusion | bytes 16388
  56.7 9.2 %gather_fusion.3 = bf16[1024]{0:T(1024)(128)(2,1)S(1)} fusion(bf16[4,769]{1,0:T(4,128)(2,1)S(1)} %concatenate.14, s32[1024]{0:T(1024)S(1)} %bitcast.103), kind=kCustom, calls=%fused_computation.3 | custom fusion | bytes 12288 | tf_op jit(solution)/shard_map/vmap()/gather | solution.py:86
  66.0 2.0 copy.48
  69.5 2.0 copy.65
  72.3 15.2 %gather_fusion.4 = bf16[1024,1024]{1,0:T(8,128)(2,1)} fusion(bf16[4,129,1024]{2,0,1:T(4,128)(2,1)S(1)} %concatenate.15, s32[1024]{0:T(1024)S(1)} %bitcast.100), kind=kCustom, calls=%fused_computation.4 | custom fusion | bytes 4202496 | tf_op jit(solution)/shard_map/vmap()/gather | solution.py:85
  87.5 9.9 %gather_fusion.2 = bf16[1024,1024]{1,0:T(8,128)(2,1)S(1)} fusion(bf16[4,129,1024]{2,0,1:T(4,128)(2,1)S(1)} %concatenate.13, s32[1024]{0:T(1024)S(1)} %bitcast.101), kind=kCustom, calls=%fused_computation.2 | custom fusion | bytes 4202496 | tf_op jit(solution)/shard_map/vmap()/gather | solution.py:60
  97.4 9.2 %fusion.8 = f32[4,4,64,1536]{3,2,0,1:T(8,128)S(1)} fusion(bf16[1024,4,1536,1]{2,1,0,3:T(4,128)(2,1)} %bitcast.113, bf16[4,4,64,1024]{3,2,1,0:T(8,128)(2,1)S(1)} %bitcast.106), kind=kOutput, calls=%fused_computation.15 | convolution fusion | flops 3221225472 | bytes 20971520 | tf_op jit(solution)/shard_map/secd,def->secf/dot_general | solution.py:30
  106.7 10.2 %fusion.14 = (bf16[4,4,64,768]{3,2,0,1:T(8,128)(2,1)}, bf16[4,4,64,768]{3,2,0,1:T(8,128)(2,1)}, bf16[4,4,64,768]{3,2,0,1:T(8,128)(2,1)S(1)}) fusion(f32[4,4,64,1536]{3,2,0,1:T(8,128)S(1)} %fusion.8, bf16[768,4,1024,1]{2,1,0,3:T(4,128)(2,1)} %bitcast.115, f32[4,4,64]{2,0,1:T(4,128)S(1)} %copy.64, bf16[4,4,64,1024]{3,2,1,0:T(8,128)(2,1)S(1)} %bitcast.108), kind=kOutput, calls=%fused_computation.26 | convolution fusion | flops 1626341376 | bytes 19402752 | tf_op jit(solution)/shard_map/secd,fed->secf/dot_general | solution.py:98
  118.0 6.5 %convolution_bitcast_fusion.1 = f32[768,4,1024]{0,2,1:T(8,128)} fusion(bf16[4,4,64,768]{3,2,0,1:T(8,128)(2,1)S(1)} %get-tuple-element.24, f32[4,4,64]{2,0,1:T(4,128)S(1)} %copy.64, bf16[4,4,64,1024]{3,2,1,0:T(8,128)(2,1)S(1)} %bitcast.109), kind=kOutput, calls=%fused_computation.16 | convolution fusion | flops 1613758464 | bytes 16257024 | tf_op jit(solution)/shard_map/secf,secd->fed/dot_general | solution.py:126
  124.5 15.4 %copy.71 = f32[768,4,1024]{2,1,0:T(4,128)} copy(f32[768,4,1024]{0,2,1:T(8,128)} %convolution_bitcast_fusion.1) | data formatting | bytes 25165824 | tf_op jit(solution)/shard_map/secf,secd->fed/transpose | solution.py:126
  140.0 13.2 %convolution_bitcast_fusion = f32[1024,4,1536]{0,2,1:T(8,128)} fusion(bf16[4,4,64,768]{3,2,0,1:T(8,128)(2,1)} %get-tuple-element.23, bf16[4,4,64,768]{3,2,0,1:T(8,128)(2,1)} %get-tuple-element.22, bf16[4,4,64,1024]{3,2,1,0:T(8,128)(2,1)S(1)} %bitcast.107), kind=kOutput, calls=%fused_computation.6 | convolution fusion | flops 3227516928 | bytes 30408704 | tf_op jit(solution)/shard_map/secd,secf->def/dot_general | solution.py:123
  153.2 9.7 %convert_bitcast_fusion = bf16[4,4,64,1024]{3,2,0,1:T(8,128)(2,1)S(1)} fusion(bf16[1024,4,1536,1]{2,1,0,3:T(4,128)(2,1)} %bitcast.114, bf16[4,4,64,768]{3,2,0,1:T(8,128)(2,1)} %get-tuple-element.23, bf16[4,4,64,768]{3,2,0,1:T(8,128)(2,1)} %get-tuple-element.22), kind=kOutput, calls=%fused_computation.31 | convolution fusion | flops 3228565504 | bytes 17825792 | tf_op jit(solution)/shard_map/secf,def->secd/dot_general | solution.py:109
  162.9 1.6 copy.69
  164.5 3.6 all-to-all-start.1
  168.2 7.4 %convert_bitcast_fusion.1 = bf16[4,4,64,1024]{3,2,0,1:T(8,128)(2,1)S(1)} fusion(bf16[4,4,64,768]{3,2,0,1:T(8,128)(2,1)} %copy-done.7, bf16[768,4,1024,1]{2,1,0,3:T(4,128)(2,1)} %bitcast.116), kind=kOutput, calls=%fused_computation.32 | convolution fusion | flops 1611661312 | bytes 9961472 | tf_op jit(solution)/shard_map/secf,fed->secd/dot_general | solution.py:33
  177.0 39.5 %all-to-all-done.1 = bf16[16,64,1024]{2,1,0:T(8,128)(2,1)S(1)} async-done(((bf16[16,64,1024]{2,1,0:T(8,128)(2,1)}), bf16[16,64,1024]{2,1,0:T(8,128)(2,1)S(1)}, u32[]{:S(2)}, u32[]{:S(2)}) %all-to-all-start.1) | async-done | bytes 2097184 | tf_op jit(solution)/shard_map/all_to_all | solution.py:112
  216.5 4.7 all-to-all-start
  222.1 1.7 reduce-window.16
  225.5 3.6 gather_fusion.1
  229.0 2.5 reshape.244
  231.5 2.2 reduce_sum.57
  233.7 35.3 %all-to-all-done = bf16[16,64,1024]{2,1,0:T(8,128)(2,1)} async-done(((bf16[16,64,1024]{2,1,0:T(8,128)(2,1)}), bf16[16,64,1024]{2,1,0:T(8,128)(2,1)}, u32[]{:S(2)}, u32[]{:S(2)}) %all-to-all-start) | async-done | bytes 2097184 | tf_op jit(solution)/shard_map/all_to_all | solution.py:64
  269.0 5.7 %gather_fusion = bf16[768,1024]{1,0:T(8,128)(2,1)S(1)} fusion(bf16[1024,1024]{1,0:T(8,128)(2,1)} %bitcast.10, s32[1024]{0:T(1024)S(1)} %pad_clamp_fusion), kind=kCustom, calls=%fused_computation | custom fusion | bytes 3148800 | tf_op jit(solution)/shard_map/gather | solution.py:66
  274.7 2.2 reshape.250
  276.9 4.8 multiply_reduce_fusion
  282.4 77.9 %all-reduce.6.cloned.1.call-done = f32[768,4,1024]{2,1,0:T(4,128)} async-done(((f32[768,4,1024]{2,1,0:T(4,128)}), f32[768,4,1024]{2,1,0:T(4,128)}) %all-reduce.6.cloned.1.call-update) | async-done | bytes 12582928
  360.3 4.2 constant_dynamic-slice_fusion
  364.5 178.9 %reduce-scatter.2.cloned.1.call-done = f32[256,4,1536]{0,2,1:T(8,128)} async-done(((f32[1024,4,1536]{0,2,1:T(8,128)}), f32[256,4,1536]{0,2,1:T(8,128)}) %reduce-scatter.2.cloned.1.call-update) | async-done | bytes 6291472 | tf_op jit(solution)/shard_map/reduce_scatter | solution.py:130
  543.4 7.9 %copy.73 = f32[256,4,1536]{2,1,0:T(4,128)} copy(f32[256,4,1536]{0,2,1:T(8,128)} %reduce-scatter.2.cloned.1.call-done) | data formatting | bytes 12582912
  (77 shorter events, 11.2 us)
Async XLA Ops:
  7.2 37.3 %copy-start.5 = (s32[2]{0:T(128)S(1)}, s32[2]{0:T(128)}, u32[]{:S(2)}) copy-start(s32[2]{0:T(128)} %constant.62) | copy-start | bytes 28
  7.2 37.4 %copy-start.4 = (s32[2]{0:T(128)S(1)}, s32[2]{0:T(128)}, u32[]{:S(2)}) copy-start(s32[2]{0:T(128)} %constant.65) | copy-start | bytes 28
  7.2 58.8 %all-gather.3.cloned.1.call-start = ((), (), s32[]{:S(2)}) async-start(), calls=%async_computation.3 | async-start | bytes 1310720 | tf_op jit(solution)/shard_map/all_gather | solution.py:46
  7.9 61.5 %all-gather.5.cloned.1.call-start = ((), (), s32[]{:S(2)}) async-start(), calls=%async_computation.4 | async-start | bytes 1310720 | tf_op jit(solution)/shard_map/all_gather | solution.py:75
  8.7 351.6 %all-reduce.6.cloned.1.call-start = ((), (), s32[]{:S(2)}) async-start(), calls=%async_computation.6 | async-start | bytes 25165824
  97.4 9.3 %copy-start = (bf16[1024,1024]{1,0:T(8,128)(2,1)S(1)}, bf16[1024,1024]{1,0:T(8,128)(2,1)}, u32[]{:S(2)}) copy-start(bf16[1024,1024]{1,0:T(8,128)(2,1)} %gather_fusion.4) | copy-start | bytes 6291460
  116.9 1.1 copy-start.7
  140.0 403.4 %reduce-scatter.2.cloned.1.call-start = ((), (), s32[]{:S(2)}) async-start(), calls=%async_computation.5 | async-start | bytes 31457280 | tf_op jit(solution)/shard_map/reduce_scatter | solution.py:130
  164.5 52.0 %all-to-all-start.1 = ((bf16[16,64,1024]{2,1,0:T(8,128)(2,1)}), bf16[16,64,1024]{2,1,0:T(8,128)(2,1)S(1)}, u32[]{:S(2)}, u32[]{:S(2)}) async-start(bf16[16,64,1024]{2,1,0:T(8,128)(2,1)} %bitcast.105), calls=%async_computation.1 | async-start | bytes 4194304 | tf_op jit(solution)/shard_map/all_to_all | solution.py:112
  177.0 44.2 %copy-start.2 = (s32[128,6]{0,1:T(8,128)S(1)}, s32[128,6]{0,1:T(8,128)}, u32[]{:S(2)}) copy-start(s32[128,6]{0,1:T(8,128)} %param.7) | copy-start | bytes 9220
  177.0 44.6 %copy-start.3 = (bf16[128,6]{0,1:T(8,128)(2,1)S(1)}, bf16[128,6]{0,1:T(8,128)(2,1)}, u32[]{:S(2)}) copy-start(bf16[128,6]{0,1:T(8,128)(2,1)} %param.8) | copy-start | bytes 4612
  177.0 44.7 %copy-start.1 = (bf16[128,1024]{1,0:T(8,128)(2,1)S(1)}, bf16[128,1024]{1,0:T(8,128)(2,1)}, u32[]{:S(2)}) copy-start(bf16[128,1024]{1,0:T(8,128)(2,1)} %param.9) | copy-start | bytes 786436
  177.0 47.1 %copy-start.6 = (u32[32]{0:T(128)S(1)}, u32[32]{0:T(128)}, u32[]{:S(2)}) copy-start(u32[32]{0:T(128)} %constant.111) | copy-start | bytes 388
  216.5 52.5 %all-to-all-start = ((bf16[16,64,1024]{2,1,0:T(8,128)(2,1)}), bf16[16,64,1024]{2,1,0:T(8,128)(2,1)}, u32[]{:S(2)}, u32[]{:S(2)}) async-start(bf16[16,64,1024]{2,1,0:T(8,128)(2,1)} %bitcast.104), calls=%async_computation | async-start | bytes 4194304 | tf_op jit(solution)/shard_map/all_to_all | solution.py:64
Sparse Core Ops, SparseCore 0:
  9.6 30.7 all-gather.2
  42.0 27.4 all-gather.4
  140.1 220.1 all-reduce.5
  362.7 180.6 reduce-scatter.1
where the time goes:
time: 567 us; the launch traced here: 558 us
  waiting for transfers between devices  334 us (59%)
  local copies, waits for them, and re-layouts  101 us (18%)
  matrix products  56.2 us (10%)
  blocking collectives  27.1 us (5%)
  other arithmetic  16.1 us (3%)
  between operations  15.2 us (3%)
  starting transfers between devices  8.51 us (2%)
    reduce_scatter x1, waiting for transfers between devices, on_device(): lax.psum_scatter(full_inner, 'replica', scatter_dimension=0, tiled=True)  179 us
    unnamed x5, waiting for transfers between devices  79.3 us
    all_to_all x1, waiting for transfers between devices, on_device(): lax.all_to_all(input_grads.reshape(EXPERTS, CAP, model_width), 'expert',...  39.5 us
    all_to_all x1, waiting for transfers between devices, on_device(): lax.all_to_all(outputs, 'expert', split_axis=0, concat_axis=0, tiled=True)  35.3 us
    unnamed x26, local copies, waits for them, and re-layouts  26.5 us
    gather x2, local copies, waits for them, and re-layouts, on_device(): values[owners // per_patch]  25 us
    transpose x1, local copies, waits for them, and re-layouts, on_device(): jnp.einsum('secf,secd->fed', hidden, slot_cotangent, preferred_element_ty...  15.4 us
    all_gather x1, blocking collectives, on_device(): lax.all_gather(expert_ids, 'expert', axis=0, tiled=True)  15 us
  transfers between devices with their start and end apart: 6, of which 5 were waited for; matrix products, arithmetic and copies ran while one was open for 17% of the time, Pallas kernels for 0%

commit v1 on v0

v1 whole, which is shorter than its diff:
```python
import functools

import jax
import jax.numpy as jnp
from jax import lax
from jax.experimental import pallas as pl
from jax.experimental.pallas import tpu as pltpu
from jax.sharding import PartitionSpec as P

CAP = 64
HALVES = 2
VMEM_LIMIT = 56 * 1024 * 1024
BF = jnp.bfloat16
F32 = jnp.float32


def mm(a, b):
    return jnp.dot(a, b, preferred_element_type=F32)


def mm_t0(a, b):
    return lax.dot_general(a, b, (((0,), (0,)), ((), ())), preferred_element_type=F32)


def mm_t1(a, b):
    return lax.dot_general(a, b, (((1,), (1,)), ((), ())), preferred_element_type=F32)


def full(shape):
    return pl.BlockSpec(shape, lambda e, s: (0,) * len(shape))


def per_expert(shape):
    return pl.BlockSpec((1,) + tuple(shape[1:]), lambda e, s: (e,) + (0,) * (len(shape) - 1))


def params():
    return pltpu.CompilerParams(vmem_limit_bytes=VMEM_LIMIT)


def table_kernel(experts, ids_ref, probs_ref, out_ref):
    count, top = ids_ref.shape
    row = lax.broadcasted_iota(jnp.int32, (count, count), 0)
    col = lax.broadcasted_iota(jnp.int32, (count, count), 1)
    eye = (row == col).astype(F32).astype(BF)
    ids = mm_t0(ids_ref[...].astype(F32).astype(BF), eye)
    probs = mm_t0(probs_ref[...], eye)
    expert = lax.broadcasted_iota(jnp.int32, (experts, count), 0).astype(F32)
    member = jnp.zeros((experts, count), F32)
    weight = jnp.zeros((experts, count), F32)
    for k in range(top):
        hit = ids[k : k + 1, :] == expert
        member = member + hit.astype(F32)
        weight = weight + jnp.where(hit, probs[k : k + 1, :], 0.0)
    earlier = (row < col).astype(F32).astype(BF)
    rank = mm(member.astype(BF), earlier)
    out_ref[:experts, :] = jnp.where(member > 0.0, rank, -1.0).astype(BF)
    out_ref[experts:, :] = weight.astype(BF)


def make_table(ids, probs, experts):
    return pl.pallas_call(
        functools.partial(table_kernel, experts),
        out_shape=jax.ShapeDtypeStruct((2 * experts, ids.shape[0]), BF),
        compiler_params=params(),
    )(ids, probs)


def masks(table, first, local):
    experts, count = table.shape[0] // 2, table.shape[1]
    named = lax.broadcasted_iota(jnp.int32, (CAP, experts), 1)
    pick = jnp.concatenate([(named == first + i).astype(F32) for i in range(local)], axis=0).astype(BF)
    slot = lax.broadcasted_iota(jnp.int32, (CAP, count), 0).astype(F32)
    slot = jnp.concatenate([slot] * local, axis=0)
    hit = mm(pick, table[:experts, :]) == slot
    weight = jnp.where(hit, mm(pick, table[experts:, :]), 0.0)
    return hit.astype(F32), weight


def scatter_slots(dst, values, d, local):
    for i in range(local):
        dst[i, d * CAP : (d + 1) * CAP, :] = values[i * CAP : (i + 1) * CAP, :]


def forward_kernel(n, local, scal, *refs):
    toks, tabs, (wgu, wd), (x_ref, gu_ref, h_ref, o_ref), combs = (
        refs[:n], refs[n : 2 * n], refs[2 * n : 2 * n + 2], refs[2 * n + 2 : 2 * n + 6], refs[2 * n + 6 :],
    )
    e = pl.program_id(0)
    first = scal[0]

    @pl.when(e == 0)
    def _():
        for d in range(n):
            hit, _w = masks(tabs[d][...], first, local)
            scatter_slots(x_ref, mm(hit.astype(BF), toks[d][...]).astype(BF), d, local)

    pre = mm(x_ref[e], wgu[0])
    gu_ref[0] = pre
    middle = pre.shape[-1] // 2
    hidden = (jax.nn.silu(pre[:, :middle]) * pre[:, middle:]).astype(BF)
    h_ref[0] = hidden
    out = mm(hidden, wd[0]).astype(BF)
    for d in range(n):
        o_ref[d, pl.ds(pl.multiple_of(e * CAP, CAP), CAP), :] = out[d * CAP : (d + 1) * CAP, :]

    @pl.when(e == local - 1)
    def _():
        for d in range(n):
            _h, weight = masks(tabs[d][...], first, local)
            combs[d][...] = mm_t0(weight.astype(BF), o_ref[d]).astype(BF)


def forward(scal, toks, tabs, wgu, wd):
    n, (local, width, two_f) = len(toks), wgu.shape
    count, rows, ff = toks[0].shape[0], n * CAP, two_f // 2
    outs = [
        (jax.ShapeDtypeStruct((local, rows, width), BF), full((local, rows, width))),
        (jax.ShapeDtypeStruct((local, rows, two_f), F32), per_expert((local, rows, two_f))),
        (jax.ShapeDtypeStruct((local, rows, ff), BF), per_expert((local, rows, ff))),
        (jax.ShapeDtypeStruct((n, local * CAP, width), BF), full((n, local * CAP, width))),
    ] + [(jax.ShapeDtypeStruct((count, width), BF), full((count, width)))] * n
    res = pl.pallas_call(
        functools.partial(forward_kernel, n, local),
        grid_spec=pltpu.PrefetchScalarGridSpec(
            num_scalar_prefetch=1,
            grid=(local,),
            in_specs=[full(a.shape) for a in (*toks, *tabs)] + [per_expert(wgu.shape), per_expert(wd.shape)],
            out_specs=[o[1] for o in outs],
        ),
        out_shape=[o[0] for o in outs],
        compiler_params=params(),
        cost_estimate=pl.CostEstimate(
            flops=6 * local * rows * width * ff, bytes_accessed=40 << 20, transcendentals=local * rows * ff
        ),
    )(scal, *toks, *tabs, wgu, wd)
    return res[0], res[1], res[2], res[3], list(res[4:])


def act_gradient(pre, hidden_grad):
    middle = pre.shape[-1] // 2
    g, u = pre[:, :middle], pre[:, middle:]
    s = jax.nn.sigmoid(g)
    return jnp.concatenate(
        [hidden_grad * u * s * (1.0 + g * (1.0 - s)), hidden_grad * g * s], axis=-1
    ).astype(BF)


def backward_kernel(n, local, scal, *refs):
    cots, tabs, (gu_ref, o_ref, wgu, wd), (pg_ref, gs_ref) = (
        refs[:n], refs[n : 2 * n], refs[2 * n : 2 * n + 4], refs[2 * n + 4 : 2 * n + 6],
    )
    tokgs, pgms, dx_ref = refs[2 * n + 6 : 3 * n + 6], refs[3 * n + 6 : 4 * n + 6], refs[4 * n + 6]
    e = pl.program_id(0)
    first = scal[0]

    @pl.when(e == 0)
    def _():
        for d in range(n):
            hit, weight = masks(tabs[d][...], first, local)
            slots = mm(hit.astype(BF), cots[d][...])
            scale = jnp.sum(weight, axis=1, keepdims=True)
            scatter_slots(gs_ref, (scale * slots).astype(BF), d, local)
            dots = jnp.sum(slots * o_ref[d].astype(F32), axis=1, keepdims=True)
            spread = hit * dots
            for i in range(local):
                pgms[d][i : i + 1, :] = jnp.sum(spread[i * CAP : (i + 1) * CAP, :], axis=0, keepdims=True)

    hidden_grad = mm_t1(gs_ref[e], wd[0])
    pg = act_gradient(gu_ref[0], hidden_grad)
    pg_ref[0] = pg
    dx = mm_t1(pg, wgu[0]).astype(BF)
    for d in range(n):
        dx_ref[d, pl.ds(pl.multiple_of(e * CAP, CAP), CAP), :] = dx[d * CAP : (d + 1) * CAP, :]

    @pl.when(e == local - 1)
    def _():
        for d in range(n):
            hit, _w = masks(tabs[d][...], first, local)
            tokgs[d][...] = mm_t0(hit.astype(BF), dx_ref[d]).astype(BF)


def backward(scal, cots, tabs, gu, o, wgu, wd):
    n, (local, width, two_f) = len(cots), wgu.shape
    count, rows, ff = cots[0].shape[0], n * CAP, two_f // 2
    outs = (
        [
            (jax.ShapeDtypeStruct((local, rows, two_f), BF), per_expert((local, rows, two_f))),
            (jax.ShapeDtypeStruct((local, rows, width), BF), full((local, rows, width))),
        ]
        + [(jax.ShapeDtypeStruct((count, width), BF), full((count, width)))] * n
        + [(jax.ShapeDtypeStruct((local, count), F32), full((local, count)))] * n
    )
    res = pl.pallas_call(
        functools.partial(backward_kernel, n, local),
        grid_spec=pltpu.PrefetchScalarGridSpec(
            num_scalar_prefetch=1,
            grid=(local,),
            in_specs=[full(a.shape) for a in (*cots, *tabs)]
            + [per_expert(gu.shape), full(o.shape), per_expert(wgu.shape), per_expert(wd.shape)],
            out_specs=[o_[1] for o_ in outs],
            scratch_shapes=[pltpu.VMEM((n, local * CAP, width), BF)],
        ),
        out_shape=[o_[0] for o_ in outs],
        compiler_params=params(),
        cost_estimate=pl.CostEstimate(
            flops=6 * local * rows * width * ff, bytes_accessed=40 << 20, transcendentals=local * rows * ff
        ),
    )(scal, *cots, *tabs, gu, o, wgu, wd)
    return res[0], res[1], list(res[2 : 2 + n]), list(res[2 + n :])


def weight_kernel(n, local, low, experts, scal, *refs):
    toks, cots = refs[:n], refs[n : 2 * n]
    tab_ref, x_ref, h_ref, pg_ref, gs_ref, wgu, wd = refs[2 * n : 2 * n + 7]
    rest = refs[2 * n + 7 :]
    gates, downs = rest[:low], rest[low : 2 * low]
    xo, go, ho, acc_g, acc_d = rest[2 * low :]
    e = pl.program_id(0)
    first, hi, lo = scal[0], scal[1], scal[2]

    @pl.when(e == 0)
    def _():
        for d in range(n):
            hit, weight = masks(tab_ref[d * 2 * experts : (d + 1) * 2 * experts, :], first, local)
            scatter_slots(xo, mm(hit.astype(BF), toks[d][...]).astype(BF), d, local)
            scatter_slots(go, mm(weight.astype(BF), cots[d][...]).astype(BF), d, local)

    pre = mm(xo[e], wgu[0])
    middle = pre.shape[-1] // 2
    ho[...] = (jax.nn.silu(pre[:, :middle]) * pre[:, middle:]).astype(BF)
    pg = act_gradient(pre, mm_t1(go[e], wd[0]))
    half_d, half_f = acc_g.shape[0], acc_d.shape[0]
    cols = pl.ds(pl.multiple_of(hi * half_d, half_d), half_d)
    acc_g[...] = mm_t0(x_ref[0, :, cols], pg_ref[0]) + mm_t0(xo[e, :, cols], pg)
    cols = pl.ds(pl.multiple_of(hi * half_f, half_f), half_f)
    acc_d[...] = mm_t0(h_ref[0, :, cols], gs_ref[0]) + mm_t0(ho[:, cols], go[e])
    for j in range(low):
        block = lax.rem(lo + j, low)
        for acc, dst in ((acc_g, gates[j]), (acc_d, downs[j])):
            size = acc.shape[0] // low
            dst[0] = acc[pl.ds(pl.multiple_of(block * size, size), size), :].astype(dst.dtype)


def weight_gradients(scal, low, toks, cots, tab, x, h, pg, gs, wgu, wd):
    n, (local, width, two_f) = len(toks), wgu.shape
    rows, ff = n * CAP, two_f // 2
    half_d, half_f = width // HALVES, ff // HALVES
    outs = []
    for size, lanes in ((half_d // low, two_f), (half_f // low, width)):
        for j in range(low):
            shape = (local, size, lanes)
            outs.append((jax.ShapeDtypeStruct(shape, BF if j else F32), per_expert(shape)))
    res = pl.pallas_call(
        functools.partial(weight_kernel, n, local, low, tab.shape[0] // (2 * n)),
        grid_spec=pltpu.PrefetchScalarGridSpec(
            num_scalar_prefetch=1,
            grid=(local,),
            in_specs=[full(a.shape) for a in (*toks, *cots, tab)]
            + [per_expert(a.shape) for a in (x, h, pg, gs, wgu, wd)],
            out_specs=[o[1] for o in outs],
            scratch_shapes=[
                pltpu.VMEM((local, rows, width), BF),
                pltpu.VMEM((local, rows, width), BF),
                pltpu.VMEM((rows, ff), BF),
                pltpu.VMEM((half_d, two_f), F32),
                pltpu.VMEM((half_f, width), F32),
            ],
        ),
        out_shape=[o[0] for o in outs],
        compiler_params=params(),
        cost_estimate=pl.CostEstimate(
            flops=12 * local * rows * width * ff, bytes_accessed=50 << 20, transcendentals=local * rows * ff
        ),
    )(scal, *toks, *cots, tab, x, h, pg, gs, wgu, wd)
    return res[:low], res[low:]


def on_device(n, replicas, tokens, expert_ids, gate_probs, cotangent, gate_up, down_weights):
    local = gate_up.shape[1]
    experts = n * local
    low = replicas // HALVES
    z, r = lax.axis_index("expert"), lax.axis_index("replica")
    scal = jnp.stack([z * local, r // low, r % low]).astype(jnp.int32)
    ring = [(i, (i + 1) % n) for i in range(n)]
    across = [(i, (i + low) % replicas) for i in range(replicas)]

    table = make_table(expert_ids, gate_probs, experts)
    toks, tabs, cots = [tokens], [table], [cotangent]
    for _ in range(n - 1):
        toks.append(lax.ppermute(toks[-1], "expert", ring))
        tabs.append(lax.ppermute(tabs[-1], "expert", ring))
        cots.append(lax.ppermute(cots[-1], "expert", ring))
    other_toks = [lax.ppermute(t, "replica", across) for t in toks]
    other_cots = [lax.ppermute(t, "replica", across) for t in cots]
    other_tab = lax.ppermute(jnp.concatenate(tabs, axis=0), "replica", across)

    wgu = jnp.transpose(gate_up, (1, 0, 2))
    wd = jnp.transpose(down_weights, (1, 0, 2))
    x, gu, h, o, combs = forward(scal, toks, tabs, wgu, wd)
    pg, gs, tokgs, pgms = backward(scal, cots, tabs, gu, o, wgu, wd)

    def ring_sum(parts):
        total = parts[1]
        for d in range(2, n + 1):
            total = lax.ppermute(total, "expert", ring)
            total = (total.astype(F32) + parts[d % n].astype(F32)).astype(BF)
        return total

    combined = ring_sum(combs)
    token_gradient = ring_sum(tokgs)
    gates, downs = weight_gradients(scal, low, other_toks, other_cots, other_tab, x, h, pg, gs, wgu, wd)
    sums = []
    for blocks in (gates, downs):
        total = blocks[0]
        for j in range(1, low):
            step = [(i, i // low * low + (i % low + j) % low) for i in range(replicas)]
            total = total + lax.ppermute(blocks[j], "replica", step).astype(F32)
        sums.append(jnp.transpose(total, (1, 0, 2)))

    found = [pgms[0]]
    for d in range(1, n):
        found.append(lax.ppermute(pgms[d], "expert", [(i, (i - d) % n) for i in range(n)]))
    prob_gradient = jnp.zeros(expert_ids.shape, F32)
    for d in range(n):
        for i in range(local):
            name = lax.rem(z + d, n) * local + i
            prob_gradient = prob_gradient + jnp.where(expert_ids == name, found[d][i][:, None], 0.0)
    return (combined, token_gradient, prob_gradient, sums[0], sums[1])


def solution(mesh):
    rows = P(("groups", "expert", "replica"), None)
    weights = P(None, "expert", None)
    shares = P(("groups", "replica"), "expert", None)
    return jax.shard_map(
        functools.partial(on_device, mesh.shape["expert"], mesh.shape["replica"]),
        mesh=mesh,
        in_specs=(rows, rows, rows, rows, weights, weights),
        out_specs=(rows, rows, rows, shares, shares),
        check_vma=False,
    )
```

time: 567 us -> 191 us (0.34); the launches traced: 558 us -> 190 us
  waiting for transfers between devices: 334 us -> 62.9 us
  local copies, waits for them, and re-layouts: 101 us -> 32.4 us
  Pallas kernels: 0 us -> 59.8 us
  matrix products: 56.2 us -> 0 us
  blocking collectives: 27.1 us -> 0 us
  starting transfers between devices: 8.51 us -> 23.8 us
  between operations: 15.2 us -> 0.99 us
  other arithmetic: 16.1 us -> 10.2 us
    reduce_scatter x1 -> x0, waiting for transfers between devices: 179 us -> none  [on_device(): lax.psum_scatter(full_inner, 'replica', scatter_dimension=0, tiled=True)]
    unnamed x5 -> x0, waiting for transfers between devices: 79.3 us -> none
    all_to_all x2 -> x0, waiting for transfers between devices: 74.7 us -> none  [the longest x1 39.5 us: on_device(): lax.all_to_all(input_grads.reshape(EXPERTS, CAP, model_width), 'expert',...]
    ppermute x0 -> x29, waiting for transfers between devices: none -> 62.9 us  [the longest x6 20.9 us: ring_sum(): total = lax.ppermute(total, 'expert', ring)]
    pallas_call x0 -> x4, Pallas kernels: none -> 59.8 us  [the longest x1 22.6 us: weight_gradients(): pl.pallas_call(functools.partial(weight_kernel, n, local, low, tab.shape[...]
    dot_general x6 -> x0, matrix products: 56.2 us -> none  [the longest x1 13.2 us: on_device(): jnp.einsum('secd,secf->def', slot_inputs, pre_gradient, preferred_element...]
    gather x5 -> x0, local copies, waits for them, and re-layouts: 43.5 us -> none  [the longest x2 25 us: on_device(): values[owners // per_patch]]
    all_gather x2 -> x0, blocking collectives: 27.1 us -> none  [the longest x1 15 us: on_device(): lax.all_gather(expert_ids, 'expert', axis=0, tiled=True)]
  transfers between devices with their start and end apart: 6 -> 29, of which waited for: 5 -> 12; matrix products, arithmetic and copies ran while one was open for 17% -> 17% of each run, Pallas kernels for 0% -> 20%
where the time goes in v1:
time: 191 us; the launch traced here: 190 us
  waiting for transfers between devices  62.9 us (33%)
  Pallas kernels  59.8 us (31%)
  local copies, waits for them, and re-layouts  32.4 us (17%)
  starting transfers between devices  23.8 us (12%)
  other arithmetic  10.2 us (5%)
    unnamed x66, local copies, waits for them, and re-layouts  32.3 us
    pallas_call x1, Pallas kernels, weight_gradients(): pl.pallas_call(functools.partial(weight_kernel, n, local, low, tab.shape[...  22.6 us
    ppermute x6, waiting for transfers between devices, ring_sum(): total = lax.ppermute(total, 'expert', ring)  20.9 us
    pallas_call x1, Pallas kernels, backward(): pl.pallas_call(functools.partial(backward_kernel, n, local), grid_spec=pl...  18.6 us
    pallas_call x1, Pallas kernels, forward(): pl.pallas_call(functools.partial(forward_kernel, n, local), grid_spec=plt...  16.8 us
    ppermute x3, waiting for transfers between devices, on_device(): toks.append(lax.ppermute(toks[-1], 'expert', ring))  13.4 us
    ppermute x3, waiting for transfers between devices, on_device(): lax.ppermute(pgms[d], 'expert', [(i, (i - d) % n) for i in range(n)])  11.4 us
    ppermute x3, waiting for transfers between devices, on_device(): tabs.append(lax.ppermute(tabs[-1], 'expert', ring))  7.69 us
  transfers between devices with their start and end apart: 29, of which 12 were waited for; matrix products, arithmetic and copies ran while one was open for 17% of the time, Pallas kernels for 20%

profile of v1, /device:TPU:0, one launch (start us, length us, event | category | flops | bytes accessed | tf_op | source)
XLA Modules:
  0.0 190.1 jit_solution(17669782141954633609)
XLA Ops:
  0.6 3.1 %collective-permute-start = (bf16[128,1024]{1,0:T(8,128)(2,1)}, bf16[128,1024]{1,0:T(8,128)(2,1)S(1)}, u32[]{:S(2)}, u32[]{:S(2)}) collective-permute-start(bf16[128,1024]{1,0:T(8,128)(2,1)} %refs_0_.2), channel_id=1, source_target_pairs={{0,4},{4,8},{8,12},{12,0},{1,5},{5,9},{9,13},{13,1},{2,6},{6,10},{... | collective-permute-start | bytes 786440 | tf_op jit(solution)/shard_map/ppermute | solution.py:291
  3.7 1.6 collective-permute-start.9
  5.3 7.8 %collective-permute-done.refs_1_ = bf16[128,1024]{1,0:T(8,128)(2,1)S(1)} collective-permute-done((bf16[128,1024]{1,0:T(8,128)(2,1)}, bf16[128,1024]{1,0:T(8,128)(2,1)S(1)}, u32[]{:S(2)}, u32[]{:S(2)}) %collective-permute-start) | collective-permute-done | bytes 262176 | tf_op jit(solution)/shard_map/ppermute | solution.py:291
  13.1 5.6 %collective-permute-done.9.refs_1_ = bf16[128,1024]{1,0:T(8,128)(2,1)S(1)} collective-permute-done((bf16[128,1024]{1,0:T(8,128)(2,1)}, bf16[128,1024]{1,0:T(8,128)(2,1)S(1)}, u32[]{:S(2)}, u32[]{:S(2)}) %collective-permute-start.9) | collective-permute-done | bytes 262176 | tf_op jit(solution)/shard_map/ppermute | solution.py:293
  18.7 5.6 %collective-permute-done.1.refs_2_ = bf16[128,1024]{1,0:T(8,128)(2,1)S(1)} collective-permute-done((bf16[128,1024]{1,0:T(8,128)(2,1)S(1)}, bf16[128,1024]{1,0:T(8,128)(2,1)S(1)}, u32[]{:S(2)}, u32[]{:S(2)}) %collective-permute-start.1) | collective-permute-done | bytes 262176 | tf_op jit(solution)/shard_map/ppermute | solution.py:291
  24.4 1.6 copy.11.ids_ref
  25.9 1.4 copy.12.probs_ref
  27.3 1.7 shard_map.101.refs_4_
  29.1 1.6 collective-permute-start.3
  30.6 4.3 %collective-permute-done.3.refs_5_ = bf16[32,128]{1,0:T(8,128)(2,1)S(1)} collective-permute-done((bf16[32,128]{1,0:T(8,128)(2,1)}, bf16[32,128]{1,0:T(8,128)(2,1)S(1)}, u32[]{:S(2)}, u32[]{:S(2)}) %collective-permute-start.3) | collective-permute-done | bytes 8224 | tf_op jit(solution)/shard_map/ppermute | solution.py:292
  34.9 1.5 collective-permute-start.18
  36.9 3.4 %collective-permute-done.4.refs_6_ = bf16[32,128]{1,0:T(8,128)(2,1)S(1)} collective-permute-done((bf16[32,128]{1,0:T(8,128)(2,1)S(1)}, bf16[32,128]{1,0:T(8,128)(2,1)S(1)}, u32[]{:S(2)}, u32[]{:S(2)}) %collective-permute-start.4) | collective-permute-done | bytes 8224 | tf_op jit(solution)/shard_map/ppermute | solution.py:292
  40.9 12.6 %copy.19 = bf16[1024,4,1536]{2,0,1:T(8,128)(2,1)} copy(bf16[1024,4,1536]{2,1,0:T(4,128)(2,1)} %param.10) | data formatting | bytes 25165824 | tf_op args[4]
  53.6 4.8 %copy.20 = bf16[768,4,1024]{2,0,1:T(8,128)(2,1)} copy(bf16[768,4,1024]{2,1,0:T(4,128)(2,1)S(1)} %bitcast.52) | data formatting | bytes 12582912 | tf_op args[5]
  58.5 1.6 collective-permute-start.26
  61.3 16.8 %shard_map.102 = (bf16[4,256,1024]{2,1,0:T(8,128)(2,1)}, f32[4,256,1536]{2,1,0:T(8,128)}, bf16[4,256,768]{2,1,0:T(8,128)(2,1)}, bf16[4,256,1024]{2,1,0:T(8,128)(...) custom-call(s32[3]{0:T(128)} %pad_add_fusion.scal, ...), custom_call_target="tpu_custom_call" | custom-call | flops 4831838208 | bytes 41943040 | tf_op jit(solution)/shard_map/pallas_call | solution.py:123
  78.2 1.6 collective-permute-start.23
  80.3 1.5 collective-permute-start.24
  82.3 1.5 collective-permute-start.25
  83.9 18.6 %shard_map.103 = (bf16[4,256,1536]{2,1,0:T(8,128)(2,1)}, bf16[4,256,1024]{2,1,0:T(8,128)(2,1)}, bf16[128,1024]{1,0:T(8,128)(2,1)}, bf16[128,1024]{1,0:T(8,128)(2...) custom-call(s32[3]{0:T(128)} %pad_add_fusion.scal, ...), custom_call_target="tpu_custom_call" | custom-call | flops 4831838208 | bytes 41943040 | tf_op jit(solution)/shard_map/pallas_call | solution.py:194
  103.7 2.8 %collective-permute-done.25.refs_7_ = bf16[128,1024]{1,0:T(8,128)(2,1)S(1)} collective-permute-done((bf16[128,1024]{1,0:T(8,128)(2,1)S(1)}, bf16[128,1024]{1,0:T(8,128)(2,1)S(1)}, u32[]{:S(2)}, u32[]{:S(2)}) %collective-permute-start.25) | collective-permute-done | bytes 262176 | tf_op jit(solution)/shard_map/ppermute | solution.py:295
  107.3 22.6 %shard_map.104 = (f32[4,256,1536]{2,1,0:T(8,128)}, bf16[4,256,1536]{2,1,0:T(8,128)(2,1)}, f32[4,192,1024]{2,1,0:T(8,128)}, bf16[4,192,1024]{2,1,0:T(8,128)(2,1)}) custom-call(s32[3]{0:T(128)} %pad_add_fusion.scal, bf16[128,1024]{1,0:T(8,128)(2,1)} %collective-permute-done.18.refs_0_, bf16[128,1024]{1,0:T(8,128)(2,1)} %copy-done.16, ...), custom_call_target="tpu_custom_call" | custom-call | flops 9663676416 | bytes 52428800 | tf_op jit(solution)/shard_map/pallas_call | solution.py:254
  130.6 3.1 %collective-permute-start.12 = (bf16[128,1024]{1,0:T(8,128)(2,1)}, bf16[128,1024]{1,0:T(8,128)(2,1)S(1)}, u32[]{:S(2)}, u32[]{:S(2)}) collective-permute-start(bf16[128,1024]{1,0:T(8,128)(2,1)} %get-tuple-element.33), channel_id=1, source_target_pairs={{0,4},{4,8},{8,12},{12,0},{1,5},{5,9},{9,13},{13,1},{2,6},{6,10},{... | collective-permute-start | bytes 786440 | tf_op jit(solution)/shard_map/ppermute | solution.py:306
  135.0 11.4 %collective-permute-done.17 = f32[4,128]{1,0:T(4,128)S(1)} collective-permute-done((f32[4,128]{1,0:T(4,128)S(1)}, f32[4,128]{1,0:T(4,128)S(1)}, u32[]{:S(2)}, u32[]{:S(2)}) %collective-permute-start.17) | collective-permute-done | bytes 2080 | tf_op jit(solution)/shard_map/ppermute | solution.py:323
  146.4 1.7 collective-permute-start.15
  150.8 9.5 %collective-permute-done.7 = bf16[128,1024]{1,0:T(8,128)(2,1)S(1)} collective-permute-done((bf16[128,1024]{1,0:T(8,128)(2,1)S(1)}, bf16[128,1024]{1,0:T(8,128)(2,1)S(1)}, u32[]{:S(2)}, u32[]{:S(2)}) %collective-permute-start.7) | collective-permute-done | bytes 262176 | tf_op jit(solution)/shard_map/ppermute | solution.py:306
  161.6 4.1 %collective-permute-done.13 = bf16[128,1024]{1,0:T(8,128)(2,1)S(1)} collective-permute-done((bf16[128,1024]{1,0:T(8,128)(2,1)S(1)}, bf16[128,1024]{1,0:T(8,128)(2,1)S(1)}, u32[]{:S(2)}, u32[]{:S(2)}) %collective-permute-start.13) | collective-permute-done | bytes 262176 | tf_op jit(solution)/shard_map/ppermute | solution.py:306
  167.4 4.1 %collective-permute-done.8 = bf16[128,1024]{1,0:T(8,128)(2,1)S(1)} collective-permute-done((bf16[128,1024]{1,0:T(8,128)(2,1)S(1)}, bf16[128,1024]{1,0:T(8,128)(2,1)S(1)}, u32[]{:S(2)}, u32[]{:S(2)}) %collective-permute-start.8) | collective-permute-done | bytes 262176 | tf_op jit(solution)/shard_map/ppermute | solution.py:306
  172.3 3.2 %collective-permute-done.14 = bf16[128,1024]{1,0:T(8,128)(2,1)S(1)} collective-permute-done((bf16[128,1024]{1,0:T(8,128)(2,1)S(1)}, bf16[128,1024]{1,0:T(8,128)(2,1)S(1)}, u32[]{:S(2)}, u32[]{:S(2)}) %collective-permute-start.14) | collective-permute-done | bytes 262176 | tf_op jit(solution)/shard_map/ppermute | solution.py:306
  176.8 3.7 %copy.16 = f32[192,4,1024]{2,1,0:T(4,128)} copy(f32[192,4,1024]{2,0,1:T(8,128)S(1)} %add_bitcast_fusion.1) | data formatting | bytes 6291456
  180.5 2.8 %add_bitcast_fusion = f32[256,4,1536]{2,0,1:T(8,128)S(1)} fusion(f32[4,256,1536]{2,1,0:T(8,128)S(1)} %bitcast.54, bf16[4,256,1536]{2,1,0:T(8,128)(2,1)} %collective-permute-done.27), kind=kLoop, calls=%fused_computation.2 | loop fusion | flops 3145728 | bytes 15728640 | tf_op jit(solution)/shard_map/transpose | solution.py:319
  183.3 6.7 %copy.15 = f32[256,4,1536]{2,1,0:T(4,128)} copy(f32[256,4,1536]{2,0,1:T(8,128)S(1)} %add_bitcast_fusion) | data formatting | bytes 12582912
  (113 shorter events, 15.2 us)
Async XLA Ops:
  0.6 12.4 %collective-permute-start = (bf16[128,1024]{1,0:T(8,128)(2,1)}, bf16[128,1024]{1,0:T(8,128)(2,1)S(1)}, u32[]{:S(2)}, u32[]{:S(2)}) collective-permute-start(bf16[128,1024]{1,0:T(8,128)(2,1)} %refs_0_.2), channel_id=1, source_target_pairs={{0,4},{4,8},{8,12},{12,0},{1,5},{5,9},{9,13},{13,1},{2,6},{6,10},{... | collective-permute-start | bytes 786440 | tf_op jit(solution)/shard_map/ppermute | solution.py:291
  3.7 15.0 %collective-permute-start.9 = (bf16[128,1024]{1,0:T(8,128)(2,1)}, bf16[128,1024]{1,0:T(8,128)(2,1)S(1)}, u32[]{:S(2)}, u32[]{:S(2)}) collective-permute-start(bf16[128,1024]{1,0:T(8,128)(2,1)} %refs_0_.3), channel_id=1, source_target_pairs={{0,4},{4,8},{8,12},{12,0},{1,5},{5,9},{9,13},{13,1},{2,6},{6,10},{... | collective-permute-start | bytes 786440 | tf_op jit(solution)/shard_map/ppermute | solution.py:293
  13.1 47.0 %copy-start.6 = (bf16[128,1024]{1,0:T(8,128)(2,1)}, bf16[128,1024]{1,0:T(8,128)(2,1)S(1)}, u32[]{:S(2)}) copy-start(bf16[128,1024]{1,0:T(8,128)(2,1)S(1)} %collective-permute-done.refs_1_) | copy-start | bytes 786436
  13.1 11.2 %collective-permute-start.1 = (bf16[128,1024]{1,0:T(8,128)(2,1)S(1)}, bf16[128,1024]{1,0:T(8,128)(2,1)S(1)}, u32[]{:S(2)}, u32[]{:S(2)}) collective-permute-start(bf16[128,1024]{1,0:T(8,128)(2,1)S(1)} %collective-permute-done.refs_1_), channel_id=1, source_target_pairs={{0,4},{4,8},{8,12},{12,0},{1,5},{5,9},{9,13},{13,1},{2,6},{6,10},{... | collective-permute-start | bytes 786440 | tf_op jit(solution)/shard_map/ppermute | solution.py:291
  18.7 59.5 %copy-start.1 = (bf16[128,1024]{1,0:T(8,128)(2,1)}, bf16[128,1024]{1,0:T(8,128)(2,1)S(1)}, u32[]{:S(2)}) copy-start(bf16[128,1024]{1,0:T(8,128)(2,1)S(1)} %collective-permute-done.9.refs_1_) | copy-start | bytes 786436
  18.7 41.4 %collective-permute-start.10 = (bf16[128,1024]{1,0:T(8,128)(2,1)S(1)}, bf16[128,1024]{1,0:T(8,128)(2,1)S(1)}, u32[]{:S(2)}, u32[]{:S(2)}) collective-permute-start(bf16[128,1024]{1,0:T(8,128)(2,1)S(1)} %collective-permute-done.9.refs_1_), channel_id=1, source_target_pairs={{0,4},{4,8},{8,12},{12,0},{1,5},{5,9},{9,13},{13,1},{2,6},{6,10},{... | collective-permute-start | bytes 786440 | tf_op jit(solution)/shard_map/ppermute | solution.py:293
  24.3 36.3 %collective-permute-start.2 = (bf16[128,1024]{1,0:T(8,128)(2,1)S(1)}, bf16[128,1024]{1,0:T(8,128)(2,1)S(1)}, u32[]{:S(2)}, u32[]{:S(2)}) collective-permute-start(bf16[128,1024]{1,0:T(8,128)(2,1)S(1)} %collective-permute-done.1.refs_2_), channel_id=1, source_target_pairs={{0,4},{4,8},{8,12},{12,0},{1,5},{5,9},{9,13},{13,1},{2,6},{6,10},{... | collective-permute-start | bytes 786440 | tf_op jit(solution)/shard_map/ppermute | solution.py:291
  29.1 5.8 %collective-permute-start.3 = (bf16[32,128]{1,0:T(8,128)(2,1)}, bf16[32,128]{1,0:T(8,128)(2,1)S(1)}, u32[]{:S(2)}, u32[]{:S(2)}) collective-permute-start(bf16[32,128]{1,0:T(8,128)(2,1)} %shard_map.101.refs_4_), channel_id=1, source_target_pairs={{0,4},{4,8},{8,12},{12,0},{1,5},{5,9},{9,13},{13,1},{2,6},{6,10},{... | collective-permute-start | bytes 24584 | tf_op jit(solution)/shard_map/ppermute | solution.py:292
  34.9 5.4 %collective-permute-start.4 = (bf16[32,128]{1,0:T(8,128)(2,1)S(1)}, bf16[32,128]{1,0:T(8,128)(2,1)S(1)}, u32[]{:S(2)}, u32[]{:S(2)}) collective-permute-start(bf16[32,128]{1,0:T(8,128)(2,1)S(1)} %collective-permute-done.3.refs_5_), channel_id=1, source_target_pairs={{0,4},{4,8},{8,12},{12,0},{1,5},{5,9},{9,13},{13,1},{2,6},{6,10},{... | collective-permute-start | bytes 24584 | tf_op jit(solution)/shard_map/ppermute | solution.py:292
  34.9 44.9 %collective-permute-start.18 = (bf16[128,1024]{1,0:T(8,128)(2,1)}, bf16[128,1024]{1,0:T(8,128)(2,1)}, u32[]{:S(2)}, u32[]{:S(2)}) collective-permute-start(bf16[128,1024]{1,0:T(8,128)(2,1)} %refs_0_.2), channel_id=1, source_target_pairs={{0,2},{1,3},{2,0},{3,1},{4,6},{5,7},{6,4},{7,5},{8,10},{9,11},{10,... | collective-permute-start | bytes 786440 | tf_op jit(solution)/shard_map/ppermute | solution.py:294
  36.4 43.9 %collective-permute-start.22 = (bf16[128,1024]{1,0:T(8,128)(2,1)}, bf16[128,1024]{1,0:T(8,128)(2,1)}, u32[]{:S(2)}, u32[]{:S(2)}) collective-permute-start(bf16[128,1024]{1,0:T(8,128)(2,1)} %refs_0_.3), channel_id=1, source_target_pairs={{0,2},{1,3},{2,0},{3,1},{4,6},{5,7},{6,4},{7,5},{8,10},{9,11},{10,... | collective-permute-start | bytes 786440 | tf_op jit(solution)/shard_map/ppermute | solution.py:295
  40.4 18.1 %collective-permute-start.5 = (bf16[32,128]{1,0:T(8,128)(2,1)S(1)}, bf16[32,128]{1,0:T(8,128)(2,1)S(1)}, u32[]{:S(2)}, u32[]{:S(2)}) collective-permute-start(bf16[32,128]{1,0:T(8,128)(2,1)S(1)} %collective-permute-done.4.refs_6_), channel_id=1, source_target_pairs={{0,4},{4,8},{8,12},{12,0},{1,5},{5,9},{9,13},{13,1},{2,6},{6,10},{... | collective-permute-start | bytes 24584 | tf_op jit(solution)/shard_map/ppermute | solution.py:292
  58.5 19.7 %collective-permute-start.26 = (bf16[128,128]{1,0:T(8,128)(2,1)S(1)}, bf16[128,128]{1,0:T(8,128)(2,1)S(1)}, u32[]{:S(2)}, u32[]{:S(2)}) collective-permute-start(bf16[128,128]{1,0:T(8,128)(2,1)S(1)} %pad_maximum_fusion), channel_id=1, source_target_pairs={{0,2},{1,3},{2,0},{3,1},{4,6},{5,7},{6,4},{7,5},{8,10},{9,11},{10,... | collective-permute-start | bytes 98312 | tf_op jit(solution)/shard_map/ppermute | solution.py:296
  60.1 21.8 %collective-permute-start.19 = (bf16[128,1024]{1,0:T(8,128)(2,1)S(1)}, bf16[128,1024]{1,0:T(8,128)(2,1)S(1)}, u32[]{:S(2)}, u32[]{:S(2)}) collective-permute-start(bf16[128,1024]{1,0:T(8,128)(2,1)S(1)} %collective-permute-done.refs_1_), channel_id=1, source_target_pairs={{0,2},{1,3},{2,0},{3,1},{4,6},{5,7},{6,4},{7,5},{8,10},{9,11},{10,... | collective-permute-start | bytes 786440 | tf_op jit(solution)/shard_map/ppermute | solution.py:294
  60.6 21.7 %collective-permute-start.11 = (bf16[128,1024]{1,0:T(8,128)(2,1)S(1)}, bf16[128,1024]{1,0:T(8,128)(2,1)S(1)}, u32[]{:S(2)}, u32[]{:S(2)}) collective-permute-start(bf16[128,1024]{1,0:T(8,128)(2,1)S(1)} %collective-permute-done.10.refs_2_), channel_id=1, source_target_pairs={{0,4},{4,8},{8,12},{12,0},{1,5},{5,9},{9,13},{13,1},{2,6},{6,10},{... | collective-permute-start | bytes 786440 | tf_op jit(solution)/shard_map/ppermute | solution.py:293
  78.2 24.3 %collective-permute-start.23 = (bf16[128,1024]{1,0:T(8,128)(2,1)S(1)}, bf16[128,1024]{1,0:T(8,128)(2,1)S(1)}, u32[]{:S(2)}, u32[]{:S(2)}) collective-permute-start(bf16[128,1024]{1,0:T(8,128)(2,1)S(1)} %collective-permute-done.9.refs_1_), channel_id=1, source_target_pairs={{0,2},{1,3},{2,0},{3,1},{4,6},{5,7},{6,4},{7,5},{8,10},{9,11},{10,... | collective-permute-start | bytes 786440 | tf_op jit(solution)/shard_map/ppermute | solution.py:295
  79.8 22.7 %collective-permute-start.20 = (bf16[128,1024]{1,0:T(8,128)(2,1)S(1)}, bf16[128,1024]{1,0:T(8,128)(2,1)S(1)}, u32[]{:S(2)}, u32[]{:S(2)}) collective-permute-start(bf16[128,1024]{1,0:T(8,128)(2,1)S(1)} %copy-done.3), channel_id=1, source_target_pairs={{0,2},{1,3},{2,0},{3,1},{4,6},{5,7},{6,4},{7,5},{8,10},{9,11},{10,... | collective-permute-start | bytes 786440 | tf_op jit(solution)/shard_map/ppermute | solution.py:294
  80.3 22.2 %collective-permute-start.24 = (bf16[128,1024]{1,0:T(8,128)(2,1)S(1)}, bf16[128,1024]{1,0:T(8,128)(2,1)S(1)}, u32[]{:S(2)}, u32[]{:S(2)}) collective-permute-start(bf16[128,1024]{1,0:T(8,128)(2,1)S(1)} %collective-permute-done.10.refs_2_), channel_id=1, source_target_pairs={{0,2},{1,3},{2,0},{3,1},{4,6},{5,7},{6,4},{7,5},{8,10},{9,11},{10,... | collective-permute-start | bytes 786440 | tf_op jit(solution)/shard_map/ppermute | solution.py:295
  81.8 21.9 %collective-permute-start.21 = (bf16[128,1024]{1,0:T(8,128)(2,1)}, bf16[128,1024]{1,0:T(8,128)(2,1)S(1)}, u32[]{:S(2)}, u32[]{:S(2)}) collective-permute-start(bf16[128,1024]{1,0:T(8,128)(2,1)} %copy-done.5), channel_id=1, source_target_pairs={{0,2},{1,3},{2,0},{3,1},{4,6},{5,7},{6,4},{7,5},{8,10},{9,11},{10,... | collective-permute-start | bytes 786440 | tf_op jit(solution)/shard_map/ppermute | solution.py:294
  82.3 24.2 %collective-permute-start.25 = (bf16[128,1024]{1,0:T(8,128)(2,1)S(1)}, bf16[128,1024]{1,0:T(8,128)(2,1)S(1)}, u32[]{:S(2)}, u32[]{:S(2)}) collective-permute-start(bf16[128,1024]{1,0:T(8,128)(2,1)S(1)} %collective-permute-done.11.refs_3_), channel_id=1, source_target_pairs={{0,2},{1,3},{2,0},{3,1},{4,6},{5,7},{6,4},{7,5},{8,10},{9,11},{10,... | collective-permute-start | bytes 786440 | tf_op jit(solution)/shard_map/ppermute | solution.py:295
  107.3 64.3 %copy-start.8 = (bf16[128,1024]{1,0:T(8,128)(2,1)S(1)}, bf16[128,1024]{1,0:T(8,128)(2,1)}, u32[]{:S(2)}) copy-start(bf16[128,1024]{1,0:T(8,128)(2,1)} %get-tuple-element.30) | copy-start | bytes 786436
  129.9 50.6 %collective-permute-start.27 = (bf16[4,256,1536]{2,1,0:T(8,128)(2,1)}, bf16[4,256,1536]{2,1,0:T(8,128)(2,1)}, u32[]{:S(2)}, u32[]{:S(2)}) collective-permute-start(bf16[4,256,1536]{2,1,0:T(8,128)(2,1)} %get-tuple-element.46), channel_id=1, source_target_pairs={{0,1},{1,0},{2,3},{3,2},{4,5},{5,4},{6,7},{7,6},{8,9},{9,8},{10,11... | collective-permute-start | bytes 9437192 | tf_op jit(solution)/shard_map/ppermute | solution.py:318
  130.0 18.1 %collective-permute-start.6 = (bf16[128,1024]{1,0:T(8,128)(2,1)}, bf16[128,1024]{1,0:T(8,128)(2,1)S(1)}, u32[]{:S(2)}, u32[]{:S(2)}) collective-permute-start(bf16[128,1024]{1,0:T(8,128)(2,1)} %get-tuple-element.27), channel_id=1, source_target_pairs={{0,4},{4,8},{8,12},{12,0},{1,5},{5,9},{9,13},{13,1},{2,6},{6,10},{... | collective-permute-start | bytes 786440 | tf_op jit(solution)/shard_map/ppermute | solution.py:306
  130.6 18.9 %collective-permute-start.12 = (bf16[128,1024]{1,0:T(8,128)(2,1)}, bf16[128,1024]{1,0:T(8,128)(2,1)S(1)}, u32[]{:S(2)}, u32[]{:S(2)}) collective-permute-start(bf16[128,1024]{1,0:T(8,128)(2,1)} %get-tuple-element.33), channel_id=1, source_target_pairs={{0,4},{4,8},{8,12},{12,0},{1,5},{5,9},{9,13},{13,1},{2,6},{6,10},{... | collective-permute-start | bytes 786440 | tf_op jit(solution)/shard_map/ppermute | solution.py:306
  133.8 12.7 %collective-permute-start.17 = (f32[4,128]{1,0:T(4,128)S(1)}, f32[4,128]{1,0:T(4,128)S(1)}, u32[]{:S(2)}, u32[]{:S(2)}) collective-permute-start(f32[4,128]{1,0:T(4,128)S(1)} %copy-done.25), channel_id=1, source_target_pairs={{0,4},{4,8},{8,12},{12,0},{1,5},{5,9},{9,13},{13,1},{2,6},{6,10},{... | collective-permute-start | bytes 6152 | tf_op jit(solution)/shard_map/ppermute | solution.py:323
  134.7 13.4 %collective-permute-start.16 = (f32[4,128]{1,0:T(4,128)S(1)}, f32[4,128]{1,0:T(4,128)S(1)}, u32[]{:S(2)}, u32[]{:S(2)}) collective-permute-start(f32[4,128]{1,0:T(4,128)S(1)} %copy-done.24), channel_id=1, source_target_pairs={{0,8},{4,12},{8,0},{12,4},{1,9},{5,13},{9,1},{13,5},{2,10},{6,14},... | collective-permute-start | bytes 6152 | tf_op jit(solution)/shard_map/ppermute | solution.py:323
  146.4 4.3 %collective-permute-start.15 = (f32[4,128]{1,0:T(4,128)S(1)}, f32[4,128]{1,0:T(4,128)S(1)}, u32[]{:S(2)}, u32[]{:S(2)}) collective-permute-start(f32[4,128]{1,0:T(4,128)S(1)} %copy-done.23), channel_id=1, source_target_pairs={{0,12},{4,0},{8,4},{12,8},{1,13},{5,1},{9,5},{13,9},{2,14},{6,2},{... | collective-permute-start | bytes 6152 | tf_op jit(solution)/shard_map/ppermute | solution.py:323
  149.2 11.1 %collective-permute-start.7 = (bf16[128,1024]{1,0:T(8,128)(2,1)S(1)}, bf16[128,1024]{1,0:T(8,128)(2,1)S(1)}, u32[]{:S(2)}, u32[]{:S(2)}) collective-permute-start(bf16[128,1024]{1,0:T(8,128)(2,1)S(1)} %add_convert_fusion.5), channel_id=1, source_target_pairs={{0,4},{4,8},{8,12},{12,0},{1,5},{5,9},{9,13},{13,1},{2,6},{6,10},{... | collective-permute-start | bytes 786440 | tf_op jit(solution)/shard_map/ppermute | solution.py:306
  149.6 26.7 %collective-permute-start.28 = (bf16[4,192,1024]{2,1,0:T(8,128)(2,1)}, bf16[4,192,1024]{2,1,0:T(8,128)(2,1)S(1)}, u32[]{:S(2)}, u32[]{:S(2)}) collective-permute-start(bf16[4,192,1024]{2,1,0:T(8,128)(2,1)} %get-tuple-element.48), channel_id=1, source_target_pairs={{0,1},{1,0},{2,3},{3,2},{4,5},{5,4},{6,7},{7,6},{8,9},{9,8},{10,11... | collective-permute-start | bytes 4718600 | tf_op jit(solution)/shard_map/ppermute | solution.py:318
  150.6 15.0 %collective-permute-start.13 = (bf16[128,1024]{1,0:T(8,128)(2,1)S(1)}, bf16[128,1024]{1,0:T(8,128)(2,1)S(1)}, u32[]{:S(2)}, u32[]{:S(2)}) collective-permute-start(bf16[128,1024]{1,0:T(8,128)(2,1)S(1)} %add_convert_fusion.2), channel_id=1, source_target_pairs={{0,4},{4,8},{8,12},{12,0},{1,5},{5,9},{9,13},{13,1},{2,6},{6,10},{... | collective-permute-start | bytes 786440 | tf_op jit(solution)/shard_map/ppermute | solution.py:306
  161.3 10.2 %collective-permute-start.8 = (bf16[128,1024]{1,0:T(8,128)(2,1)S(1)}, bf16[128,1024]{1,0:T(8,128)(2,1)S(1)}, u32[]{:S(2)}, u32[]{:S(2)}) collective-permute-start(bf16[128,1024]{1,0:T(8,128)(2,1)S(1)} %add_convert_fusion.4), channel_id=1, source_target_pairs={{0,4},{4,8},{8,12},{12,0},{1,5},{5,9},{9,13},{13,1},{2,6},{6,10},{... | collective-permute-start | bytes 786440 | tf_op jit(solution)/shard_map/ppermute | solution.py:306
  166.6 8.8 %collective-permute-start.14 = (bf16[128,1024]{1,0:T(8,128)(2,1)S(1)}, bf16[128,1024]{1,0:T(8,128)(2,1)S(1)}, u32[]{:S(2)}, u32[]{:S(2)}) collective-permute-start(bf16[128,1024]{1,0:T(8,128)(2,1)S(1)} %add_convert_fusion.1), channel_id=1, source_target_pairs={{0,4},{4,8},{8,12},{12,0},{1,5},{5,9},{9,13},{13,1},{2,6},{6,10},{... | collective-permute-start | bytes 786440 | tf_op jit(solution)/shard_map/ppermute | solution.py:306
  (27 other events, 479.3 us)

commit v2 on v0

v2 whole, which is shorter than its diff:
```python
import functools

import jax
import jax.numpy as jnp
from jax import lax
from jax.experimental import pallas as pl
from jax.experimental.pallas import tpu as pltpu
from jax.sharding import PartitionSpec as P

CAP = 64
HALVES = 2
VMEM_LIMIT = 56 * 1024 * 1024
BF = jnp.bfloat16
F32 = jnp.float32


def mm(a, b):
    return jnp.dot(a, b, preferred_element_type=F32)


def mm_t0(a, b):
    return lax.dot_general(a, b, (((0,), (0,)), ((), ())), preferred_element_type=F32)


def mm_t1(a, b):
    return lax.dot_general(a, b, (((1,), (1,)), ((), ())), preferred_element_type=F32)


def full(shape):
    return pl.BlockSpec(shape, lambda e, s: (0,) * len(shape))


def per_expert(shape):
    return pl.BlockSpec((1,) + tuple(shape[1:]), lambda e, s: (e,) + (0,) * (len(shape) - 1))


def params():
    return pltpu.CompilerParams(vmem_limit_bytes=VMEM_LIMIT)


def pack_kernel(ids_ref, probs_ref, tok_ref, cot_ref, out_ref):
    top, count = ids_ref.shape
    experts = out_ref.shape[0] - 2 * count
    out_ref[:count, :] = tok_ref[...]
    out_ref[count : 2 * count, :] = cot_ref[...]
    ids, probs = ids_ref[...], probs_ref[...].astype(F32)
    expert = lax.broadcasted_iota(jnp.int32, (experts, count), 0)
    member = jnp.zeros((experts, count), F32)
    weight = jnp.zeros((experts, count), F32)
    for k in range(top):
        hit = ids[k : k + 1, :] == expert
        member = member + hit.astype(F32)
        weight = weight + jnp.where(hit, probs[k : k + 1, :], 0.0)
    row = lax.broadcasted_iota(jnp.int32, (count, count), 0)
    col = lax.broadcasted_iota(jnp.int32, (count, count), 1)
    rank = mm(member.astype(BF), (row < col).astype(F32).astype(BF))
    slot = jnp.where(member > 0.0, rank, -1.0)
    rest = jnp.zeros((experts, out_ref.shape[1] - 2 * count), F32)
    out_ref[2 * count :, :] = jnp.concatenate([slot, weight, rest], axis=1).astype(BF)


def pack(ids, probs, tokens, cot, experts):
    count, width = tokens.shape
    return pl.pallas_call(
        pack_kernel,
        out_shape=jax.ShapeDtypeStruct((2 * count + experts, width), BF),
        compiler_params=pltpu.CompilerParams(vmem_limit_bytes=8 * 1024 * 1024),
    )(ids.T, probs.T, tokens, cot)


def masks(pay, count, first, local):
    experts = pay.shape[0] - 2 * count
    named = lax.broadcasted_iota(jnp.int32, (CAP, experts), 1)
    pick = jnp.concatenate([(named == first + i).astype(F32) for i in range(local)], axis=0).astype(BF)
    slot = lax.broadcasted_iota(jnp.int32, (CAP, count), 0).astype(F32)
    slot = jnp.concatenate([slot] * local, axis=0)
    hit = mm(pick, pay[2 * count :, :count]) == slot
    weight = jnp.where(hit, mm(pick, pay[2 * count :, count : 2 * count]), 0.0)
    return hit.astype(F32), weight


def scatter_slots(dst, values, d, local):
    for i in range(local):
        dst[i, d * CAP : (d + 1) * CAP, :] = values[i * CAP : (i + 1) * CAP, :]


def act_gradient(pre, hidden_grad):
    middle = pre.shape[-1] // 2
    g, u = pre[:, :middle], pre[:, middle:]
    s = jax.nn.sigmoid(g)
    return jnp.concatenate(
        [hidden_grad * u * s * (1.0 + g * (1.0 - s)), hidden_grad * g * s], axis=-1
    ).astype(BF)


def stage_kernel(m, local, count, own, after, scal, *refs):
    pays, (wgu, wd) = refs[:m], refs[m : m + 2]
    refs = refs[m + 2 + after :]
    x_ref, h_ref, pg_ref, gs_ref = refs[:4]
    refs = refs[4:]
    if own:
        sums, (hit_s, wt_s, cs, o_s, dx_s, dots_s) = refs[:m], refs[m:]
    e = pl.program_id(0)
    here = pl.ds(pl.multiple_of(e * CAP, CAP), CAP)

    @pl.when(e == 0)
    def _():
        for d in range(m):
            hit, weight = masks(pays[d], count, scal[0], local)
            hit_b = hit.astype(BF)
            scatter_slots(x_ref, mm(hit_b, pays[d][:count, :]).astype(BF), d, local)
            if own:
                hit_s[d] = hit_b
                wt_s[d] = weight.astype(BF)
                slots = mm(hit_b, pays[d][count : 2 * count, :])
                scatter_slots(cs, slots.astype(BF), d, local)
                slots = jnp.sum(weight, axis=1, keepdims=True) * slots
            else:
                slots = mm(weight.astype(BF), pays[d][count : 2 * count, :])
            scatter_slots(gs_ref, slots.astype(BF), d, local)

    pre = mm(x_ref[e], wgu[0])
    middle = pre.shape[-1] // 2
    hidden = (jax.nn.silu(pre[:, :middle]) * pre[:, middle:]).astype(BF)
    h_ref[0] = hidden
    pg = act_gradient(pre, mm_t1(gs_ref[e], wd[0]))
    pg_ref[0] = pg
    if own:
        out = mm(hidden, wd[0]).astype(BF)
        dots = jnp.sum(cs[e].astype(F32) * out.astype(F32), axis=1, keepdims=True)
        dx = mm_t1(pg, wgu[0]).astype(BF)
        for d in range(m):
            part = slice(d * CAP, (d + 1) * CAP)
            o_s[d, here, :] = out[part]
            dx_s[d, here, :] = dx[part]
            spread = hit_s[d, here, :].astype(F32) * dots[part]
            dots_s[d, pl.ds(e, 1), :] = jnp.sum(spread, axis=0, keepdims=True)

        @pl.when(e == local - 1)
        def _():
            for d in range(m):
                sums[d][:count, :] = mm_t0(wt_s[d], o_s[d]).astype(BF)
                sums[d][count : 2 * count, :] = mm_t0(hit_s[d], dx_s[d]).astype(BF)
                experts, width = sums[d].shape[0] - 2 * count, sums[d].shape[1]
                row = lax.broadcasted_iota(jnp.int32, (experts, count), 0)
                dots = jnp.zeros((experts, count), F32)
                for i in range(local):
                    dots = dots + jnp.where(row == scal[0] + i, dots_s[d, i : i + 1, :], 0.0)
                upper = dots.astype(BF).astype(F32)
                rest = jnp.zeros((experts, width - 2 * count), F32)
                sums[d][2 * count :, :] = jnp.concatenate([upper, dots - upper, rest], axis=1).astype(BF)


def stage(scal, pays, count, wgu, wd, own, after=()):
    m, (local, width, two_f) = len(pays), wgu.shape
    rows, ff = m * CAP, two_f // 2
    outs = [
        (jax.ShapeDtypeStruct((local, rows, width), BF), full((local, rows, width))),
        (jax.ShapeDtypeStruct((local, rows, ff), BF), per_expert((local, rows, ff))),
        (jax.ShapeDtypeStruct((local, rows, two_f), BF), per_expert((local, rows, two_f))),
        (jax.ShapeDtypeStruct((local, rows, width), BF), full((local, rows, width))),
    ]
    scratch = []
    if own:
        outs += [(jax.ShapeDtypeStruct(a.shape, BF), full(a.shape)) for a in pays]
        scratch = [
            pltpu.VMEM((m, local * CAP, count), BF),
            pltpu.VMEM((m, local * CAP, count), BF),
            pltpu.VMEM((local, rows, width), BF),
            pltpu.VMEM((m, local * CAP, width), BF),
            pltpu.VMEM((m, local * CAP, width), BF),
            pltpu.VMEM((m, local, count), F32),
        ]
    res = pl.pallas_call(
        functools.partial(stage_kernel, m, local, count, own, len(after)),
        grid_spec=pltpu.PrefetchScalarGridSpec(
            num_scalar_prefetch=1,
            grid=(local,),
            in_specs=[full(a.shape) for a in pays]
            + [per_expert(wgu.shape), per_expert(wd.shape)]
            + [pl.BlockSpec(memory_space=pl.ANY)] * len(after),
            out_specs=[o[1] for o in outs],
            scratch_shapes=scratch,
        ),
        out_shape=[o[0] for o in outs],
        compiler_params=params(),
        cost_estimate=pl.CostEstimate(
            flops=(48 if own else 34) * local * rows * width * ff, bytes_accessed=24 << 20, transcendentals=local * rows * ff
        ),
    )(scal, *pays, wgu, wd, *after)
    return res[:4], list(res[4:])


def send_kernel(parts, low, scal, *refs):
    xs, hs, pgs, gss = (refs[k * parts : (k + 1) * parts] for k in range(4))
    gates, downs, own_down, acc_d = refs[4 * parts : 4 * parts + low - 1], refs[4 * parts + low - 1 : -2], refs[-2], refs[-1]
    lo = scal[2]
    pg = jnp.concatenate([p[0] for p in pgs], axis=0)
    size = xs[0].shape[-1] // low
    for j in range(1, low):
        cols = pl.ds(pl.multiple_of(lax.rem(lo + j, low) * size, size), size)
        gates[j - 1][0] = mm_t0(jnp.concatenate([x[0, :, cols] for x in xs], axis=0), pg).astype(BF)
    h = jnp.concatenate([h_[0] for h_ in hs], axis=0)
    acc_d[...] = mm_t0(h, jnp.concatenate([g[0] for g in gss], axis=0))
    size = acc_d.shape[0] // low
    for j in range(low):
        block = acc_d[pl.ds(pl.multiple_of(lax.rem(lo + j, low) * size, size), size), :]
        if j:
            downs[j - 1][0] = block.astype(BF)
        else:
            own_down[0] = block


def send_blocks(scal, low, stages, start, local, after=()):
    xs, hs, pgs, gss = zip(*stages)
    width = xs[0].shape[-1]
    ff = hs[0].shape[-1]
    half_d, half_f = width // HALVES, ff // HALVES
    of_half = lambda a, size: pl.BlockSpec((1, a.shape[1], size), lambda e, s: (e + start, 0, s[1]))
    whole = lambda a: pl.BlockSpec((1,) + a.shape[1:], lambda e, s: (e + start, 0, 0))
    gate_shape, down_shape = (local, half_d // low, 2 * ff), (local, half_f // low, width)
    outs = [jax.ShapeDtypeStruct(gate_shape, BF)] * (low - 1)
    outs += [jax.ShapeDtypeStruct(down_shape, BF)] * (low - 1) + [jax.ShapeDtypeStruct(down_shape, F32)]
    k = len(after)
    body = functools.partial(send_kernel, len(stages), low)
    res = pl.pallas_call(
        lambda s, *refs: body(s, *refs[k:]),
        grid_spec=pltpu.PrefetchScalarGridSpec(
            num_scalar_prefetch=1,
            grid=(local,),
            in_specs=[pl.BlockSpec(memory_space=pl.ANY)] * k
            + [of_half(x, half_d) for x in xs]
            + [of_half(h, half_f) for h in hs]
            + [whole(a) for a in (*pgs, *gss)],
            out_specs=[per_expert(o.shape) for o in outs],
            scratch_shapes=[pltpu.VMEM((half_f, width), F32)],
        ),
        out_shape=outs,
        compiler_params=params(),
        cost_estimate=pl.CostEstimate(
            flops=36 * local * xs[0].shape[1] * width * ff, bytes_accessed=24 << 20, transcendentals=0
        ),
    )(scal, *after, *xs, *hs, *pgs, *gss)
    return res[: low - 1], res[low - 1 : 2 * low - 2], res[-1]


def keep_kernel(parts, pieces, low, scal, *refs):
    xs, pgs, refs = refs[:parts], refs[parts : 2 * parts], refs[2 * parts :]
    gate_ref, down_ref = refs[-2:]
    each = gate_ref.shape[1] // pieces
    got = [refs[k * (2 * low - 1) : (k + 1) * (2 * low - 1)] for k in range(pieces)]
    size = xs[0].shape[-1] // low
    cols = pl.ds(pl.multiple_of(scal[2] * size, size), size)
    for e in range(gate_ref.shape[1]):
        total = mm_t0(
            jnp.concatenate([x[e, :, cols] for x in xs], axis=0), jnp.concatenate([p[e] for p in pgs], axis=0)
        )
        arrived = got[e // each]
        gate_ref[:, e, :] = total + sum(g[e % each].astype(F32) for g in arrived[: low - 1])
        down_ref[:, e, :] = arrived[-1][e % each] + sum(g[e % each].astype(F32) for g in arrived[low - 1 : -1])


def keep_blocks(scal, low, stages, pieces, after=()):
    xs, _, pgs, _ = zip(*stages)
    local, rows, width = xs[0].shape
    two_f = pgs[0].shape[-1]
    half_d = width // HALVES
    steps = 4
    lanes = lambda a: pl.BlockSpec(a.shape[:-1] + (a.shape[-1] // steps,), lambda c, s: (0, 0, c))
    outs = [
        jax.ShapeDtypeStruct((half_d // low, local, two_f), F32),
        jax.ShapeDtypeStruct((pieces[0][-1].shape[1], local, width), F32),
    ]
    k = len(after)
    body = functools.partial(keep_kernel, len(stages), len(pieces), low)
    arrived = [a for piece in pieces for a in piece]
    return pl.pallas_call(
        lambda s, *refs: body(s, *refs[k:]),
        grid_spec=pltpu.PrefetchScalarGridSpec(
            num_scalar_prefetch=1,
            grid=(steps,),
            in_specs=[pl.BlockSpec(memory_space=pl.ANY)] * k
            + [pl.BlockSpec((local, rows, half_d), lambda c, s: (0, 0, s[1]))] * len(xs)
            + [lanes(a) for a in (*pgs, *arrived)],
            out_specs=[lanes(o) for o in outs],
        ),
        out_shape=outs,
        compiler_params=params(),
        cost_estimate=pl.CostEstimate(
            flops=16 * local * rows * width * two_f, bytes_accessed=24 << 20, transcendentals=0
        ),
    )(scal, *after, *xs, *pgs, *arrived)


def on_device(n, replicas, tokens, expert_ids, gate_probs, cotangent, gate_up, down_weights):
    local, count = gate_up.shape[1], tokens.shape[0]
    low = replicas // HALVES
    z, r = lax.axis_index("expert"), lax.axis_index("replica")
    scal = jnp.stack([z * local, r // low, r % low]).astype(jnp.int32)
    ring = [(i, (i + 1) % n) for i in range(n)]
    across = [(i, (i + low) % replicas) for i in range(replicas)]

    pays = [pack(expert_ids, gate_probs, tokens, cotangent, n * local)]
    others = []
    wgu = jnp.transpose(gate_up, (1, 0, 2))
    wd = jnp.transpose(down_weights, (1, 0, 2))
    for d in range(n):
        others.append(lax.ppermute(pays[d], "replica", across))
        if d < n - 1:
            pays.append(lax.ppermute(pays[d], "expert", ring))
            if d == 0:
                pays[1], others[0], wgu, wd = lax.optimization_barrier((pays[1], others[0], wgu, wd))
    near = n // 2
    own_a, sums_a = stage(scal, pays[:near], count, wgu, wd, True)
    other_a, _ = stage(scal, others[:near], count, wgu, wd, False, (sums_a[0], pays[near]))
    own_b, sums_b = stage(scal, pays[near:], count, wgu, wd, True, (other_a[3],))
    sums = sums_a + sums_b

    def add(got, mine):
        return (got.astype(F32) + mine.astype(F32)).astype(BF)

    totals = [sums[1]]
    for d in range(2, n):
        totals.append(add(lax.ppermute(totals[-1], "expert", ring), sums[d]))
    other_b, _ = stage(scal, others[near:], count, wgu, wd, False, (totals[n // 2 - 1],))
    stages = (own_a, other_a, own_b, other_b)
    steps = [[(i, i // low * low + (i % low + j) % low) for i in range(replicas)] for j in range(1, low)]
    pieces, before = [], ()
    for start in range(0, local, -(-local // 2)):
        gates, downs, own_down = send_blocks(scal, low, stages, start, -(-local // 2), before)
        gates = [lax.ppermute(b, "replica", s) for b, s in zip(gates, steps)]
        downs = [lax.ppermute(b, "replica", s) for b, s in zip(downs, steps)]
        pieces.append((*gates, *downs, own_down))
        before = (totals[-1],)
    arrived = lax.ppermute(totals[-1], "expert", ring)
    gate_up_gradient, down_gradient = keep_blocks(scal, low, stages, pieces)
    arrived, gate_up_gradient, down_gradient = lax.optimization_barrier((arrived, gate_up_gradient, down_gradient))
    combined, token_gradient = add(arrived[:count], sums[0][:count]), add(arrived[count : 2 * count], sums[0][count : 2 * count])
    dots = arrived[2 * count :, : 2 * count].astype(F32) + sums[0][2 * count :, : 2 * count].astype(F32)
    dots = dots[:, :count] + dots[:, count:]
    named = expert_ids.T[:, None, :] == jnp.arange(n * local, dtype=jnp.int32)[None, :, None]
    prob_gradient = jnp.sum(jnp.where(named, dots[None], 0.0), axis=1).T
    return (combined, token_gradient, prob_gradient, gate_up_gradient, down_gradient)


def solution(mesh):
    rows = P(("groups", "expert", "replica"), None)
    weights = P(None, "expert", None)
    shares = P(("groups", "replica"), "expert", None)
    return jax.shard_map(
        functools.partial(on_device, mesh.shape["expert"], mesh.shape["replica"]),
        mesh=mesh,
        in_specs=(rows, rows, rows, rows, weights, weights),
        out_specs=(rows, rows, rows, shares, shares),
        check_vma=False,
    )
```

time: 567 us -> 141 us (0.25); the launches traced: 558 us -> 141 us
  waiting for transfers between devices: 334 us -> 18.2 us
  Pallas kernels: 0 us -> 81.3 us
  local copies, waits for them, and re-layouts: 101 us -> 22.9 us
  matrix products: 56.2 us -> 0 us
  blocking collectives: 27.1 us -> 0 us
  between operations: 15.2 us -> 0.84 us
  other arithmetic: 16.1 us -> 4.53 us
    reduce_scatter x1 -> x0, waiting for transfers between devices: 179 us -> none  [on_device(): lax.psum_scatter(full_inner, 'replica', scatter_dimension=0, tiled=True)]
    pallas_call x0 -> x8, Pallas kernels: none -> 81.3 us  [the longest x4 56.3 us: stage(): pl.pallas_call(functools.partial(stage_kernel, m, local, count, own, len(...]
    unnamed x5 -> x0, waiting for transfers between devices: 79.3 us -> none
    all_to_all x2 -> x0, waiting for transfers between devices: 74.7 us -> none  [the longest x1 39.5 us: on_device(): lax.all_to_all(input_grads.reshape(EXPERTS, CAP, model_width), 'expert',...]
    dot_general x6 -> x0, matrix products: 56.2 us -> none  [the longest x1 13.2 us: on_device(): jnp.einsum('secd,secf->def', slot_inputs, pre_gradient, preferred_element...]
    gather x5 -> x0, local copies, waits for them, and re-layouts: 43.5 us -> none  [the longest x2 25 us: on_device(): values[owners // per_patch]]
    all_gather x2 -> x0, blocking collectives: 27.1 us -> none  [the longest x1 15 us: on_device(): lax.all_gather(expert_ids, 'expert', axis=0, tiled=True)]
    ppermute x0 -> x14, waiting for transfers between devices: none -> 18.2 us  [the longest x3 11.4 us: on_device(): pays.append(lax.ppermute(pays[d], 'expert', ring))]
  transfers between devices with their start and end apart: 6 -> 14, of which waited for: 5 -> 3; matrix products, arithmetic and copies ran while one was open for 17% -> 12% of each run, Pallas kernels for 0% -> 53%
where the time goes in v2:
time: 141 us
  Pallas kernels  81.3 us (58%)
  local copies, waits for them, and re-layouts  22.9 us (16%)
  waiting for transfers between devices  18.2 us (13%)
  starting transfers between devices  12.9 us (9%)
  other arithmetic  4.53 us (3%)
    pallas_call x4, Pallas kernels, stage(): pl.pallas_call(functools.partial(stage_kernel, m, local, count, own, len(...  56.3 us
    unnamed x50, local copies, waits for them, and re-layouts  22.9 us
    pallas_call x2, Pallas kernels, send_blocks(): pl.pallas_call(lambda s, *refs: body(s, *refs[k:]), grid_spec=pltpu.Prefe...  12.8 us
    pallas_call x1, Pallas kernels, keep_blocks(): pl.pallas_call(lambda s, *refs: body(s, *refs[k:]), grid_spec=pltpu.Prefe...  12.1 us
    ppermute x3, waiting for transfers between devices, on_device(): pays.append(lax.ppermute(pays[d], 'expert', ring))  11.4 us
    ppermute x2, waiting for transfers between devices, on_device(): downs = [lax.ppermute(b, 'replica', s) for b, s in zip(downs, steps)]  6.85 us
    ppermute x4, starting transfers between devices, on_device(): others.append(lax.ppermute(pays[d], 'replica', across))  6.54 us
    ppermute x3, starting transfers between devices, on_device(): pays.append(lax.ppermute(pays[d], 'expert', ring))  3.38 us
  transfers between devices with their start and end apart: 14, of which 3 were waited for; matrix products, arithmetic and copies ran while one was open for 12% of the time, Pallas kernels for 53%

profile of v2, /device:TPU:0, one launch (start us, length us, event | category | flops | bytes accessed | tf_op | source)
XLA Modules:
  0.0 140.7 jit_solution(4718827791425345976)
XLA Ops:
  0.6 0.9 copy-done.1
  1.6 0.9 copy-done.2
  2.5 0.7 copy-done.3
  3.2 0.7 copy-done.5
  4.0 2.9 %collective-permute-start.1 = (bf16[272,1024]{1,0:T(8,128)(2,1)S(1)}, bf16[272,1024]{1,0:T(8,128)(2,1)S(1)}, u32[]{:S(2)}, u32[]{:S(2)}) collective-permute-start(bf16[272,1024]{1,0:T(8,128)(2,1)S(1)} %shard_map.101.refs_0_), channel_id=1, source_target_pairs={{0,2},{1,3},{2,0},{3,1},{4,6},{5,7},{6,4},{7,5},{8,10},{9,11},{10,... | collective-permute-start | bytes 1671176 | tf_op jit(solution)/shard_map/ppermute | solution.py:308
  7.0 1.6 %collective-permute-start = (bf16[272,1024]{1,0:T(8,128)(2,1)S(1)}, bf16[272,1024]{1,0:T(8,128)(2,1)S(1)}, u32[]{:S(2)}, u32[]{:S(2)}) collective-permute-start(bf16[272,1024]{1,0:T(8,128)(2,1)S(1)} %shard_map.101.refs_0_), channel_id=1, source_target_pairs={{0,4},{4,8},{8,12},{12,0},{1,5},{5,9},{9,13},{13,1},{2,6},{6,10},{... | collective-permute-start | bytes 1671176 | tf_op jit(solution)/shard_map/ppermute | solution.py:310
  8.6 7.8 %copy.18 = bf16[768,4,1024]{2,0,1:T(8,128)(2,1)} copy(bf16[768,4,1024]{2,1,0:T(4,128)(2,1)} %param.11) | data formatting | bytes 12582912 | tf_op args[5]
  16.3 7.5 %copy.17 = bf16[1024,4,1536]{2,0,1:T(8,128)(2,1)} copy(bf16[1024,4,1536]{2,1,0:T(4,128)(2,1)S(1)} %copy-done.6) | data formatting | bytes 25165824 | tf_op args[4]
  23.9 0.6 pad_add_fusion.scal.s
  24.5 0.6 collective-permute-start.5
  25.1 1.6 %collective-permute-start.3 = (bf16[272,1024]{1,0:T(8,128)(2,1)S(1)}, bf16[272,1024]{1,0:T(8,128)(2,1)S(1)}, u32[]{:S(2)}, u32[]{:S(2)}) collective-permute-start(bf16[272,1024]{1,0:T(8,128)(2,1)S(1)} %collective-permute-done.refs_1_), channel_id=1, source_target_pairs={{0,4},{4,8},{8,12},{12,0},{1,5},{5,9},{9,13},{13,1},{2,6},{6,10},{... | collective-permute-start | bytes 1671176 | tf_op jit(solution)/shard_map/ppermute | solution.py:310
  26.7 16.4 %shard_map.102 = (bf16[4,128,1024]{2,1,0:T(8,128)(2,1)}, bf16[4,128,768]{2,1,0:T(8,128)(2,1)}, bf16[4,128,1536]{2,1,0:T(8,128)(2,1)}, bf16[4,128,1024]{2,1,0:T(8...) custom-call(s32[3]{0:T(128)} %pad_add_fusion.scal.s, bf16[272,1024]{1,0:T(8,128)(2,1)} %copy-done, ...), custom_call_target="tpu_custom_call" | custom-call | flops 19327352832 | bytes 25165824 | tf_op jit(solution)/shard_map/pallas_call | solution.py:174
  43.1 1.6 %collective-permute-start.2 = (bf16[272,1024]{1,0:T(8,128)(2,1)}, bf16[272,1024]{1,0:T(8,128)(2,1)S(1)}, u32[]{:S(2)}, u32[]{:S(2)}) collective-permute-start(bf16[272,1024]{1,0:T(8,128)(2,1)} %get-tuple-element.43), channel_id=1, source_target_pairs={{0,4},{4,8},{8,12},{12,0},{1,5},{5,9},{9,13},{13,1},{2,6},{6,10},{... | collective-permute-start | bytes 1671176 | tf_op jit(solution)/shard_map/ppermute | solution.py:324
  44.7 1.5 %collective-permute-start.8 = (bf16[272,1024]{1,0:T(8,128)(2,1)S(1)}, bf16[272,1024]{1,0:T(8,128)(2,1)S(1)}, u32[]{:S(2)}, u32[]{:S(2)}) collective-permute-start(bf16[272,1024]{1,0:T(8,128)(2,1)S(1)} %collective-permute-done.3.refs_5_.refs_0_), channel_id=1, source_target_pairs={{0,2},{1,3},{2,0},{3,1},{4,6},{5,7},{6,4},{7,5},{8,10},{9,11},{10,... | collective-permute-start | bytes 1671176 | tf_op jit(solution)/shard_map/ppermute | solution.py:308
  46.4 0.8 copy-done.22
  47.2 11.7 %shard_map.103 = (bf16[4,128,1024]{2,1,0:T(8,128)(2,1)}, bf16[4,128,768]{2,1,0:T(8,128)(2,1)}, bf16[4,128,1536]{2,1,0:T(8,128)(2,1)}, bf16[4,128,1024]{2,1,0:T(8,128)(2,1)}) custom-call(s32[3]{0:T(128)} %pad_add_fusion.scal.s, bf16[272,1024]{1,0:T(8,128)(2,1)} %copy-done.17, bf16[272,1024]{1,0:T(8,128)(2,1)} %copy-done.22, bf16[4,1024,1536]{2,1,0:T(8,128)(2,1)} %bitcast.16, ...), custom_call_target="tpu_custom_call" | custom-call | flops 13690208256 | bytes 25165824 | tf_op jit(solution)/shard_map/pallas_call | solution.py:174
  59.0 11.4 %collective-permute-done.4.refs_1_ = bf16[272,1024]{1,0:T(8,128)(2,1)S(1)} collective-permute-done((bf16[272,1024]{1,0:T(8,128)(2,1)S(1)}, bf16[272,1024]{1,0:T(8,128)(2,1)S(1)}, u32[]{:S(2)}, u32[]{:S(2)}) %collective-permute-start.4) | collective-permute-done | bytes 557088 | tf_op jit(solution)/shard_map/ppermute | solution.py:310
  70.3 1.5 %collective-permute-start.9 = (bf16[272,1024]{1,0:T(8,128)(2,1)S(1)}, bf16[272,1024]{1,0:T(8,128)(2,1)S(1)}, u32[]{:S(2)}, u32[]{:S(2)}) collective-permute-start(bf16[272,1024]{1,0:T(8,128)(2,1)S(1)} %collective-permute-done.4.refs_1_), channel_id=1, source_target_pairs={{0,2},{1,3},{2,0},{3,1},{4,6},{5,7},{6,4},{7,5},{8,10},{9,11},{10,... | collective-permute-start | bytes 1671176 | tf_op jit(solution)/shard_map/ppermute | solution.py:308
  71.8 16.4 %shard_map.104 = (bf16[4,128,1024]{2,1,0:T(8,128)(2,1)}, bf16[4,128,768]{2,1,0:T(8,128)(2,1)}, bf16[4,128,1536]{2,1,0:T(8,128)(2,1)}, bf16[4,128,1024]{2,1,0:T(8...) custom-call(s32[3]{0:T(128)} %pad_add_fusion.scal.s, bf16[272,1024]{1,0:T(8,128)(2,1)} %copy-done.19, ...), custom_call_target="tpu_custom_call" | custom-call | flops 19327352832 | bytes 25165824 | tf_op jit(solution)/shard_map/pallas_call | solution.py:174
  88.3 1.3 add_convert_fusion.1.refs_4_
  90.6 0.8 copy-done.23
  91.5 11.8 %shard_map.105 = (bf16[4,128,1024]{2,1,0:T(8,128)(2,1)}, bf16[4,128,768]{2,1,0:T(8,128)(2,1)}, bf16[4,128,1536]{2,1,0:T(8,128)(2,1)}, bf16[4,128,1024]{2,1,0:T(8,128)(2,1)}) custom-call(s32[3]{0:T(128)} %pad_add_fusion.scal.s, bf16[272,1024]{1,0:T(8,128)(2,1)} %copy-done.20, bf16[272,1024]{1,0:T(8,128)(2,1)} %copy-done.23, bf16[4,1024,1536]{2,1,0:T(8,128)(2,1)} %bitcast.18, ...), custom_call_target="tpu_custom_call" | custom-call | flops 13690208256 | bytes 25165824 | tf_op jit(solution)/shard_map/pallas_call | solution.py:174
  103.2 6.4 %shard_map.106 = (bf16[2,256,1536]{2,1,0:T(8,128)(2,1)}, bf16[2,192,1024]{2,1,0:T(8,128)(2,1)}, f32[2,192,1024]{2,1,0:T(8,128)}) custom-call(s32[3]{0:T(128)} %pad_add_fusion.scal.s, bf16[4,128,1024]{2,1,0:T(8,128)(2,1)} %get-tuple-element.49.refs_0_.refs_1_, bf16[4,128,1024]{2,1,0:T(8,128)(2,1)} %get-tuple-element.50.refs_1_.refs_2_, ...), custom_call_target="tpu_custom_call" | custom-call | flops 7247757312 | bytes 25165824 | tf_op jit(solution)/shard_map/pallas_call | solution.py:226
  109.7 1.1 add_convert_fusion.refs_0_
  110.7 6.4 %shard_map.107 = (bf16[2,256,1536]{2,1,0:T(8,128)(2,1)}, bf16[2,192,1024]{2,1,0:T(8,128)(2,1)}, f32[2,192,1024]{2,1,0:T(8,128)}) custom-call(s32[3]{0:T(128)} %pad_add_fusion.scal.s, bf16[272,1024]{1,0:T(8,128)(2,1)} %add_convert_fusion.refs_0_, bf16[4,128,1024]{2,1,0:T(8,128)(2,1)} %get-tuple-element.49.refs_0_.refs_1_, ...), custom_call_target="tpu_custom_call" | custom-call | flops 7247757312 | bytes 25165824 | tf_op jit(solution)/shard_map/pallas_call | solution.py:226
  118.3 6.2 %collective-permute-done.13.refs_12_ = bf16[2,192,1024]{2,1,0:T(8,128)(2,1)S(1)} collective-permute-done((bf16[2,192,1024]{2,1,0:T(8,128)(2,1)}, bf16[2,192,1024]{2,1,0:T(8,128)(2,1)S(1)}, u32[]{:S(2)}, u32[]{:S(2)}) %collective-permute-start.13) | collective-permute-done | bytes 786464 | tf_op jit(solution)/shard_map/ppermute | solution.py:332
  124.5 0.7 collective-permute-done.11.refs_9_
  125.2 0.9 copy-done.16
  126.0 0.6 copy-done.12
  127.0 12.1 %shard_map.108 = (f32[256,4,1536]{2,1,0:T(4,128)}, f32[192,4,1024]{2,1,0:T(4,128)}) custom-call(s32[3]{0:T(128)} %pad_add_fusion.scal.s, bf16[4,128,1024]{2,1,0:T(8,128)(2,1)} %get-tuple-element.49.refs_0_.refs_1_, bf16[4,128,1024]{2,1,0:T(8,128)(2,1)} %get-tuple-element.50.refs_1_.refs_2_, bf16[4,128,1024]{2,1,0:T(8,128)(2,1)} %get-tuple-element.51.refs_2_.refs_3_, ...), custom_call_target="tpu_custom_call" | custom-call | flops 12884901888 | bytes 25165824 | tf_op jit(solution)/shard_map/pallas_call | solution.py:277
  139.1 1.0 add_convert_fusion.2
  140.1 0.6 select_reduce_fusion
  (61 shorter events, 3.0 us)
Async XLA Ops:
  0.6 1.0 copy-start.1
  1.6 0.9 copy-start.2
  4.0 12.3 %copy-start = (bf16[272,1024]{1,0:T(8,128)(2,1)}, bf16[272,1024]{1,0:T(8,128)(2,1)S(1)}, u32[]{:S(2)}) copy-start(bf16[272,1024]{1,0:T(8,128)(2,1)S(1)} %shard_map.101.refs_0_) | copy-start | bytes 1671172
  4.0 20.5 %collective-permute-start.1 = (bf16[272,1024]{1,0:T(8,128)(2,1)S(1)}, bf16[272,1024]{1,0:T(8,128)(2,1)S(1)}, u32[]{:S(2)}, u32[]{:S(2)}) collective-permute-start(bf16[272,1024]{1,0:T(8,128)(2,1)S(1)} %shard_map.101.refs_0_), channel_id=1, source_target_pairs={{0,2},{1,3},{2,0},{3,1},{4,6},{5,7},{6,4},{7,5},{8,10},{9,11},{10,... | collective-permute-start | bytes 1671176 | tf_op jit(solution)/shard_map/ppermute | solution.py:308
  7.0 17.5 %collective-permute-start = (bf16[272,1024]{1,0:T(8,128)(2,1)S(1)}, bf16[272,1024]{1,0:T(8,128)(2,1)S(1)}, u32[]{:S(2)}, u32[]{:S(2)}) collective-permute-start(bf16[272,1024]{1,0:T(8,128)(2,1)S(1)} %shard_map.101.refs_0_), channel_id=1, source_target_pairs={{0,4},{4,8},{8,12},{12,0},{1,5},{5,9},{9,13},{13,1},{2,6},{6,10},{... | collective-permute-start | bytes 1671176 | tf_op jit(solution)/shard_map/ppermute | solution.py:310
  8.6 7.8 %copy-start.6 = (bf16[1024,4,1536]{2,1,0:T(4,128)(2,1)S(1)}, bf16[1024,4,1536]{2,1,0:T(4,128)(2,1)}, u32[]{:S(2)}) copy-start(bf16[1024,4,1536]{2,1,0:T(4,128)(2,1)} %param.10) | copy-start | bytes 37748740
  24.5 18.6 %copy-start.17 = (bf16[272,1024]{1,0:T(8,128)(2,1)}, bf16[272,1024]{1,0:T(8,128)(2,1)S(1)}, u32[]{:S(2)}) copy-start(bf16[272,1024]{1,0:T(8,128)(2,1)S(1)} %collective-permute-done.1.refs_0_) | copy-start | bytes 1671172
  24.5 2.2 %copy-start.18 = (bf16[272,1024]{1,0:T(8,128)(2,1)}, bf16[272,1024]{1,0:T(8,128)(2,1)S(1)}, u32[]{:S(2)}) copy-start(bf16[272,1024]{1,0:T(8,128)(2,1)S(1)} %collective-permute-done.refs_1_) | copy-start | bytes 1671172
  24.5 21.9 %collective-permute-start.5 = (bf16[272,1024]{1,0:T(8,128)(2,1)S(1)}, bf16[272,1024]{1,0:T(8,128)(2,1)S(1)}, u32[]{:S(2)}, u32[]{:S(2)}) collective-permute-start(bf16[272,1024]{1,0:T(8,128)(2,1)S(1)} %collective-permute-done.refs_1_), channel_id=1, source_target_pairs={{0,2},{1,3},{2,0},{3,1},{4,6},{5,7},{6,4},{7,5},{8,10},{9,11},{10,... | collective-permute-start | bytes 1671176 | tf_op jit(solution)/shard_map/ppermute | solution.py:308
  25.1 19.6 %collective-permute-start.3 = (bf16[272,1024]{1,0:T(8,128)(2,1)S(1)}, bf16[272,1024]{1,0:T(8,128)(2,1)S(1)}, u32[]{:S(2)}, u32[]{:S(2)}) collective-permute-start(bf16[272,1024]{1,0:T(8,128)(2,1)S(1)} %collective-permute-done.refs_1_), channel_id=1, source_target_pairs={{0,4},{4,8},{8,12},{12,0},{1,5},{5,9},{9,13},{13,1},{2,6},{6,10},{... | collective-permute-start | bytes 1671176 | tf_op jit(solution)/shard_map/ppermute | solution.py:310
  43.1 45.2 %collective-permute-start.2 = (bf16[272,1024]{1,0:T(8,128)(2,1)}, bf16[272,1024]{1,0:T(8,128)(2,1)S(1)}, u32[]{:S(2)}, u32[]{:S(2)}) collective-permute-start(bf16[272,1024]{1,0:T(8,128)(2,1)} %get-tuple-element.43), channel_id=1, source_target_pairs={{0,4},{4,8},{8,12},{12,0},{1,5},{5,9},{9,13},{13,1},{2,6},{6,10},{... | collective-permute-start | bytes 1671176 | tf_op jit(solution)/shard_map/ppermute | solution.py:324
  44.7 1.7 %copy-start.19 = (bf16[272,1024]{1,0:T(8,128)(2,1)}, bf16[272,1024]{1,0:T(8,128)(2,1)S(1)}, u32[]{:S(2)}) copy-start(bf16[272,1024]{1,0:T(8,128)(2,1)S(1)} %collective-permute-done.3.refs_5_.refs_0_) | copy-start | bytes 1671172
  44.7 45.1 %collective-permute-start.8 = (bf16[272,1024]{1,0:T(8,128)(2,1)S(1)}, bf16[272,1024]{1,0:T(8,128)(2,1)S(1)}, u32[]{:S(2)}, u32[]{:S(2)}) collective-permute-start(bf16[272,1024]{1,0:T(8,128)(2,1)S(1)} %collective-permute-done.3.refs_5_.refs_0_), channel_id=1, source_target_pairs={{0,2},{1,3},{2,0},{3,1},{4,6},{5,7},{6,4},{7,5},{8,10},{9,11},{10,... | collective-permute-start | bytes 1671176 | tf_op jit(solution)/shard_map/ppermute | solution.py:308
  46.2 24.1 %collective-permute-start.4 = (bf16[272,1024]{1,0:T(8,128)(2,1)S(1)}, bf16[272,1024]{1,0:T(8,128)(2,1)S(1)}, u32[]{:S(2)}, u32[]{:S(2)}) collective-permute-start(bf16[272,1024]{1,0:T(8,128)(2,1)S(1)} %collective-permute-done.3.refs_5_.refs_0_), channel_id=1, source_target_pairs={{0,4},{4,8},{8,12},{12,0},{1,5},{5,9},{9,13},{13,1},{2,6},{6,10},{... | collective-permute-start | bytes 1671176 | tf_op jit(solution)/shard_map/ppermute | solution.py:310
  70.3 1.5 %copy-start.21 = (bf16[272,1024]{1,0:T(8,128)(2,1)}, bf16[272,1024]{1,0:T(8,128)(2,1)S(1)}, u32[]{:S(2)}) copy-start(bf16[272,1024]{1,0:T(8,128)(2,1)S(1)} %collective-permute-done.4.refs_1_) | copy-start | bytes 1671172
  70.3 19.5 %collective-permute-start.9 = (bf16[272,1024]{1,0:T(8,128)(2,1)S(1)}, bf16[272,1024]{1,0:T(8,128)(2,1)S(1)}, u32[]{:S(2)}, u32[]{:S(2)}) collective-permute-start(bf16[272,1024]{1,0:T(8,128)(2,1)S(1)} %collective-permute-done.4.refs_1_), channel_id=1, source_target_pairs={{0,2},{1,3},{2,0},{3,1},{4,6},{5,7},{6,4},{7,5},{8,10},{9,11},{10,... | collective-permute-start | bytes 1671176 | tf_op jit(solution)/shard_map/ppermute | solution.py:308
  89.6 20.1 %collective-permute-start.6 = (bf16[272,1024]{1,0:T(8,128)(2,1)S(1)}, bf16[272,1024]{1,0:T(8,128)(2,1)S(1)}, u32[]{:S(2)}, u32[]{:S(2)}) collective-permute-start(bf16[272,1024]{1,0:T(8,128)(2,1)S(1)} %add_convert_fusion.1.refs_4_), channel_id=1, source_target_pairs={{0,4},{4,8},{8,12},{12,0},{1,5},{5,9},{9,13},{13,1},{2,6},{6,10},{... | collective-permute-start | bytes 1671176 | tf_op jit(solution)/shard_map/ppermute | solution.py:324
  103.2 6.4 %copy-start.8 = (bf16[272,1024]{1,0:T(8,128)(2,1)S(1)}, bf16[272,1024]{1,0:T(8,128)(2,1)}, u32[]{:S(2)}) copy-start(bf16[272,1024]{1,0:T(8,128)(2,1)} %get-tuple-element.48) | copy-start | bytes 1671172
  110.7 6.5 %copy-start.11 = (bf16[2,256,1536]{2,1,0:T(8,128)(2,1)S(1)}, bf16[2,256,1536]{2,1,0:T(8,128)(2,1)}, u32[]{:S(2)}) copy-start(bf16[2,256,1536]{2,1,0:T(8,128)(2,1)} %get-tuple-element.64) | copy-start | bytes 4718596
  110.7 7.1 %copy-start.14 = (bf16[2,192,1024]{2,1,0:T(8,128)(2,1)S(1)}, bf16[2,192,1024]{2,1,0:T(8,128)(2,1)}, u32[]{:S(2)}) copy-start(bf16[2,192,1024]{2,1,0:T(8,128)(2,1)} %get-tuple-element.65) | copy-start | bytes 2359300
  110.7 7.5 %copy-start.7 = (bf16[272,1024]{1,0:T(8,128)(2,1)S(1)}, bf16[272,1024]{1,0:T(8,128)(2,1)}, u32[]{:S(2)}) copy-start(bf16[272,1024]{1,0:T(8,128)(2,1)} %add_convert_fusion.refs_0_) | copy-start | bytes 1671172
  117.2 8.0 %collective-permute-start.12 = (bf16[2,256,1536]{2,1,0:T(8,128)(2,1)}, bf16[2,256,1536]{2,1,0:T(8,128)(2,1)S(1)}, u32[]{:S(2)}, u32[]{:S(2)}) collective-permute-start(bf16[2,256,1536]{2,1,0:T(8,128)(2,1)} %get-tuple-element.67), channel_id=1, source_target_pairs={{0,1},{1,0},{2,3},{3,2},{4,5},{5,4},{6,7},{7,6},{8,9},{9,8},{10,11... | collective-permute-start | bytes 4718600 | tf_op jit(solution)/shard_map/ppermute | solution.py:331
  117.2 7.9 %collective-permute-start.10 = (bf16[2,256,1536]{2,1,0:T(8,128)(2,1)S(1)}, bf16[2,256,1536]{2,1,0:T(8,128)(2,1)S(1)}, u32[]{:S(2)}, u32[]{:S(2)}) collective-permute-start(bf16[2,256,1536]{2,1,0:T(8,128)(2,1)S(1)} %copy-done.11), channel_id=1, source_target_pairs={{0,1},{1,0},{2,3},{3,2},{4,5},{5,4},{6,7},{7,6},{8,9},{9,8},{10,11... | collective-permute-start | bytes 4718600 | tf_op jit(solution)/shard_map/ppermute | solution.py:331
  117.7 6.7 %collective-permute-start.13 = (bf16[2,192,1024]{2,1,0:T(8,128)(2,1)}, bf16[2,192,1024]{2,1,0:T(8,128)(2,1)S(1)}, u32[]{:S(2)}, u32[]{:S(2)}) collective-permute-start(bf16[2,192,1024]{2,1,0:T(8,128)(2,1)} %get-tuple-element.68), channel_id=1, source_target_pairs={{0,1},{1,0},{2,3},{3,2},{4,5},{5,4},{6,7},{7,6},{8,9},{9,8},{10,11... | collective-permute-start | bytes 2359304 | tf_op jit(solution)/shard_map/ppermute | solution.py:332
  117.8 7.3 %collective-permute-start.11 = (bf16[2,192,1024]{2,1,0:T(8,128)(2,1)S(1)}, bf16[2,192,1024]{2,1,0:T(8,128)(2,1)S(1)}, u32[]{:S(2)}, u32[]{:S(2)}) collective-permute-start(bf16[2,192,1024]{2,1,0:T(8,128)(2,1)S(1)} %copy-done.14), channel_id=1, source_target_pairs={{0,1},{1,0},{2,3},{3,2},{4,5},{5,4},{6,7},{7,6},{8,9},{9,8},{10,11... | collective-permute-start | bytes 2359304 | tf_op jit(solution)/shard_map/ppermute | solution.py:332
  118.3 20.8 %collective-permute-start.7 = (bf16[272,1024]{1,0:T(8,128)(2,1)S(1)}, bf16[272,1024]{1,0:T(8,128)(2,1)S(1)}, u32[]{:S(2)}, u32[]{:S(2)}) collective-permute-start(bf16[272,1024]{1,0:T(8,128)(2,1)S(1)} %copy-done.7), channel_id=1, source_target_pairs={{0,4},{4,8},{8,12},{12,0},{1,5},{5,9},{9,13},{13,1},{2,6},{6,10},{... | collective-permute-start | bytes 1671176 | tf_op jit(solution)/shard_map/ppermute | solution.py:335
  124.5 1.6 %copy-start.15 = (bf16[2,192,1024]{2,1,0:T(8,128)(2,1)}, bf16[2,192,1024]{2,1,0:T(8,128)(2,1)S(1)}, u32[]{:S(2)}) copy-start(bf16[2,192,1024]{2,1,0:T(8,128)(2,1)S(1)} %collective-permute-done.13.refs_12_) | copy-start | bytes 2359300
  125.1 0.9 copy-start.16
  125.1 1.5 %copy-start.12 = (bf16[2,256,1536]{2,1,0:T(8,128)(2,1)}, bf16[2,256,1536]{2,1,0:T(8,128)(2,1)S(1)}, u32[]{:S(2)}) copy-start(bf16[2,256,1536]{2,1,0:T(8,128)(2,1)S(1)} %collective-permute-done.12.refs_11_) | copy-start | bytes 4718596
  125.1 1.9 %copy-start.13 = (bf16[2,256,1536]{2,1,0:T(8,128)(2,1)}, bf16[2,256,1536]{2,1,0:T(8,128)(2,1)S(1)}, u32[]{:S(2)}) copy-start(bf16[2,256,1536]{2,1,0:T(8,128)(2,1)S(1)} %collective-permute-done.10.refs_8_) | copy-start | bytes 4718596
  127.0 12.1 %copy-start.10 = (bf16[272,1024]{1,0:T(8,128)(2,1)S(1)}, bf16[272,1024]{1,0:T(8,128)(2,1)}, u32[]{:S(2)}) copy-start(bf16[272,1024]{1,0:T(8,128)(2,1)} %get-tuple-element.45.refs_4_) | copy-start | bytes 1671172
  139.1 1.0 copy-start.4
  (6 other events, 4.7 us)

commit v3 on v2

--- a/solution.py
+++ b/solution.py
@@ -9,7 +9,9 @@
 
 CAP = 64
 HALVES = 2
-VMEM_LIMIT = 56 * 1024 * 1024
+EARLY_VMEM = 34 * 1024 * 1024
+STAGE_VMEM = 34 * 1024 * 1024
+SHARE_VMEM = 16 * 1024 * 1024
 BF = jnp.bfloat16
 F32 = jnp.float32
 
@@ -32,10 +34,6 @@
 
 def per_expert(shape):
     return pl.BlockSpec((1,) + tuple(shape[1:]), lambda e, s: (e,) + (0,) * (len(shape) - 1))
-
-
-def params():
-    return pltpu.CompilerParams(vmem_limit_bytes=VMEM_LIMIT)
 
 
 def pack_kernel(ids_ref, probs_ref, tok_ref, cot_ref, out_ref):
@@ -93,13 +91,14 @@
     ).astype(BF)
 
 
-def stage_kernel(m, local, count, own, after, scal, *refs):
+def stage_kernel(m, own, local, count, after, scal, *refs):
     pays, (wgu, wd) = refs[:m], refs[m : m + 2]
     refs = refs[m + 2 + after :]
     x_ref, h_ref, pg_ref, gs_ref = refs[:4]
-    refs = refs[4:]
+    sums, refs = refs[4 : 4 + own], refs[4 + own :]
+    xs, hs = refs[:2]
     if own:
-        sums, (hit_s, wt_s, cs, o_s, dx_s, dots_s) = refs[:m], refs[m:]
+        hit_s, wt_s, cs, o_s, dx_s, dots_s = refs[2:]
     e = pl.program_id(0)
     here = pl.ds(pl.multiple_of(e * CAP, CAP), CAP)
 
@@ -108,8 +107,8 @@
         for d in range(m):
             hit, weight = masks(pays[d], count, scal[0], local)
             hit_b = hit.astype(BF)
-            scatter_slots(x_ref, mm(hit_b, pays[d][:count, :]).astype(BF), d, local)
-            if own:
+            scatter_slots(xs, mm(hit_b, pays[d][:count, :]).astype(BF), d, local)
+            if d < own:
                 hit_s[d] = hit_b
                 wt_s[d] = weight.astype(BF)
                 slots = mm(hit_b, pays[d][count : 2 * count, :])
@@ -119,17 +118,20 @@
                 slots = mm(weight.astype(BF), pays[d][count : 2 * count, :])
             scatter_slots(gs_ref, slots.astype(BF), d, local)
 
-    pre = mm(x_ref[e], wgu[0])
+    half_d, half_f = x_ref.shape[-1], h_ref.shape[-1]
+    x_ref[0] = xs[e, :, pl.ds(pl.multiple_of(scal[1] * half_d, half_d), half_d)]
+    pre = mm(xs[e], wgu[0])
     middle = pre.shape[-1] // 2
     hidden = (jax.nn.silu(pre[:, :middle]) * pre[:, middle:]).astype(BF)
-    h_ref[0] = hidden
+    hs[...] = hidden
+    h_ref[0] = hs[:, pl.ds(pl.multiple_of(scal[1] * half_f, half_f), half_f)]
     pg = act_gradient(pre, mm_t1(gs_ref[e], wd[0]))
     pg_ref[0] = pg
     if own:
-        out = mm(hidden, wd[0]).astype(BF)
+        out = mm(hidden[: own * CAP], wd[0]).astype(BF)
         dots = jnp.sum(cs[e].astype(F32) * out.astype(F32), axis=1, keepdims=True)
-        dx = mm_t1(pg, wgu[0]).astype(BF)
-        for d in range(m):
+        dx = mm_t1(pg[: own * CAP], wgu[0]).astype(BF)
+        for d in range(own):
             part = slice(d * CAP, (d + 1) * CAP)
             o_s[d, here, :] = out[part]
             dx_s[d, here, :] = dx[part]
@@ -138,7 +140,7 @@
 
         @pl.when(e == local - 1)
         def _():
-            for d in range(m):
+            for d in range(own):
                 sums[d][:count, :] = mm_t0(wt_s[d], o_s[d]).astype(BF)
                 sums[d][count : 2 * count, :] = mm_t0(hit_s[d], dx_s[d]).astype(BF)
                 experts, width = sums[d].shape[0] - 2 * count, sums[d].shape[1]
@@ -151,28 +153,29 @@
                 sums[d][2 * count :, :] = jnp.concatenate([upper, dots - upper, rest], axis=1).astype(BF)
 
 
-def stage(scal, pays, count, wgu, wd, own, after=()):
-    m, (local, width, two_f) = len(pays), wgu.shape
+def stage(scal, limit, mine, others, count, wgu, wd, after=()):
+    pays = (*mine, *others)
+    m, own, (local, width, two_f) = len(pays), len(mine), wgu.shape
     rows, ff = m * CAP, two_f // 2
     outs = [
-        (jax.ShapeDtypeStruct((local, rows, width), BF), full((local, rows, width))),
-        (jax.ShapeDtypeStruct((local, rows, ff), BF), per_expert((local, rows, ff))),
+        (jax.ShapeDtypeStruct((local, rows, width // HALVES), BF), per_expert((local, rows, width // HALVES))),
+        (jax.ShapeDtypeStruct((local, rows, ff // HALVES), BF), per_expert((local, rows, ff // HALVES))),
         (jax.ShapeDtypeStruct((local, rows, two_f), BF), per_expert((local, rows, two_f))),
         (jax.ShapeDtypeStruct((local, rows, width), BF), full((local, rows, width))),
     ]
-    scratch = []
+    outs += [(jax.ShapeDtypeStruct(a.shape, BF), full(a.shape)) for a in mine]
+    scratch = [pltpu.VMEM((local, rows, width), BF), pltpu.VMEM((rows, ff), BF)]
     if own:
-        outs += [(jax.ShapeDtypeStruct(a.shape, BF), full(a.shape)) for a in pays]
-        scratch = [
-            pltpu.VMEM((m, local * CAP, count), BF),
-            pltpu.VMEM((m, local * CAP, count), BF),
-            pltpu.VMEM((local, rows, width), BF),
-            pltpu.VMEM((m, local * CAP, width), BF),
-            pltpu.VMEM((m, local * CAP, width), BF),
-            pltpu.VMEM((m, local, count), F32),
+        scratch += [
+            pltpu.VMEM((own, local * CAP, count), BF),
+            pltpu.VMEM((own, local * CAP, count), BF),
+            pltpu.VMEM((local, own * CAP, width), BF),
+            pltpu.VMEM((own, local * CAP, width), BF),
+            pltpu.VMEM((own, local * CAP, width), BF),
+            pltpu.VMEM((own, local, count), F32),
         ]
     res = pl.pallas_call(
-        functools.partial(stage_kernel, m, local, count, own, len(after)),
+        functools.partial(stage_kernel, m, own, local, count, len(after)),
         grid_spec=pltpu.PrefetchScalarGridSpec(
             num_scalar_prefetch=1,
             grid=(local,),
@@ -183,9 +186,9 @@
             scratch_shapes=scratch,
         ),
         out_shape=[o[0] for o in outs],
-        compiler_params=params(),
+        compiler_params=pltpu.CompilerParams(vmem_limit_bytes=limit),
         cost_estimate=pl.CostEstimate(
-            flops=(48 if own else 34) * local * rows * width * ff, bytes_accessed=24 << 20, transcendentals=local * rows * ff
+            flops=(14 if own else 7) * 1000 * 1000 * 1000, bytes_accessed=24 << 20, transcendentals=local * rows * ff
         ),
     )(scal, *pays, wgu, wd, *after)
     return res[:4], list(res[4:])
@@ -213,10 +216,8 @@
 
 def send_blocks(scal, low, stages, start, local, after=()):
     xs, hs, pgs, gss = zip(*stages)
-    width = xs[0].shape[-1]
-    ff = hs[0].shape[-1]
-    half_d, half_f = width // HALVES, ff // HALVES
-    of_half = lambda a, size: pl.BlockSpec((1, a.shape[1], size), lambda e, s: (e + start, 0, s[1]))
+    width, ff = gss[0].shape[-1], pgs[0].shape[-1] // 2
+    half_d, half_f = xs[0].shape[-1], hs[0].shape[-1]
     whole = lambda a: pl.BlockSpec((1,) + a.shape[1:], lambda e, s: (e + start, 0, 0))
     gate_shape, down_shape = (local, half_d // low, 2 * ff), (local, half_f // low, width)
     outs = [jax.ShapeDtypeStruct(gate_shape, BF)] * (low - 1)
@@ -229,16 +230,14 @@
             num_scalar_prefetch=1,
             grid=(local,),
             in_specs=[pl.BlockSpec(memory_space=pl.ANY)] * k
-            + [of_half(x, half_d) for x in xs]
-            + [of_half(h, half_f) for h in hs]
-            + [whole(a) for a in (*pgs, *gss)],
+            + [whole(a) for a in (*xs, *hs, *pgs, *gss)],
             out_specs=[per_expert(o.shape) for o in outs],
             scratch_shapes=[pltpu.VMEM((half_f, width), F32)],
         ),
         out_shape=outs,
-        compiler_params=params(),
+        compiler_params=pltpu.CompilerParams(vmem_limit_bytes=SHARE_VMEM),
         cost_estimate=pl.CostEstimate(
-            flops=36 * local * xs[0].shape[1] * width * ff, bytes_accessed=24 << 20, transcendentals=0
+            flops=4 * 1000 * 1000 * 1000, bytes_accessed=24 << 20, transcendentals=0
         ),
     )(scal, *after, *xs, *hs, *pgs, *gss)
     return res[: low - 1], res[low - 1 : 2 * low - 2], res[-1]
@@ -262,9 +261,8 @@
 
 def keep_blocks(scal, low, stages, pieces, after=()):
     xs, _, pgs, _ = zip(*stages)
-    local, rows, width = xs[0].shape
-    two_f = pgs[0].shape[-1]
-    half_d = width // HALVES
+    local, rows, half_d = xs[0].shape
+    two_f, width = pgs[0].shape[-1], half_d * HALVES
     steps = 4
     lanes = lambda a: pl.BlockSpec(a.shape[:-1] + (a.shape[-1] // steps,), lambda c, s: (0, 0, c))
     outs = [
@@ -280,14 +278,14 @@
             num_scalar_prefetch=1,
             grid=(steps,),
             in_specs=[pl.BlockSpec(memory_space=pl.ANY)] * k
-            + [pl.BlockSpec((local, rows, half_d), lambda c, s: (0, 0, s[1]))] * len(xs)
+            + [full(x.shape) for x in xs]
             + [lanes(a) for a in (*pgs, *arrived)],
             out_specs=[lanes(o) for o in outs],
         ),
         out_shape=outs,
-        compiler_params=params(),
+        compiler_params=pltpu.CompilerParams(vmem_limit_bytes=SHARE_VMEM),
         cost_estimate=pl.CostEstimate(
-            flops=16 * local * rows * width * two_f, bytes_accessed=24 << 20, transcendentals=0
+            flops=6 * 1000 * 1000 * 1000, bytes_accessed=24 << 20, transcendentals=0
         ),
     )(scal, *after, *xs, *pgs, *arrived)
 
@@ -303,35 +301,39 @@
     pays = [pack(expert_ids, gate_probs, tokens, cotangent, n * local)]
     others = []
     wgu = jnp.transpose(gate_up, (1, 0, 2))
-    wd = jnp.transpose(down_weights, (1, 0, 2))
     for d in range(n):
         others.append(lax.ppermute(pays[d], "replica", across))
         if d < n - 1:
             pays.append(lax.ppermute(pays[d], "expert", ring))
             if d == 0:
-                pays[1], others[0], wgu, wd = lax.optimization_barrier((pays[1], others[0], wgu, wd))
-    near = n // 2
-    own_a, sums_a = stage(scal, pays[:near], count, wgu, wd, True)
-    other_a, _ = stage(scal, others[:near], count, wgu, wd, False, (sums_a[0], pays[near]))
-    own_b, sums_b = stage(scal, pays[near:], count, wgu, wd, True, (other_a[3],))
-    sums = sums_a + sums_b
+                pays[1], others[0], wgu, down_weights = lax.optimization_barrier(
+                    (pays[1], others[0], wgu, down_weights)
+                )
+
+    wd = jnp.transpose(down_weights, (1, 0, 2))
 
     def add(got, mine):
         return (got.astype(F32) + mine.astype(F32)).astype(BF)
 
-    totals = [sums[1]]
-    for d in range(2, n):
-        totals.append(add(lax.ppermute(totals[-1], "expert", ring), sums[d]))
-    other_b, _ = stage(scal, others[near:], count, wgu, wd, False, (totals[n // 2 - 1],))
-    stages = (own_a, other_a, own_b, other_b)
+    step = -(-n // 4)
+    stages, sums, totals, before = [], {}, [], ()
+    for start in range(0, n, step):
+        ready = [d for d in range(start + 1, start + step + 1) if d < n] + ([0] if start == step else [])
+        outs, part = stage(scal, EARLY_VMEM if start <= step else STAGE_VMEM, [pays[d] for d in ready], others[start : start + step], count, wgu, wd, before)
+        stages.append(outs)
+        sums.update(zip(ready, part))
+        before = (outs[3],)
+        for d in ready:
+            if d:
+                totals.append(add(lax.ppermute(totals[-1], "expert", ring), sums[d]) if totals else sums[d])
+                before = (outs[3], totals[-1])
     steps = [[(i, i // low * low + (i % low + j) % low) for i in range(replicas)] for j in range(1, low)]
-    pieces, before = [], ()
+    pieces = []
     for start in range(0, local, -(-local // 2)):
-        gates, downs, own_down = send_blocks(scal, low, stages, start, -(-local // 2), before)
+        gates, downs, own_down = send_blocks(scal, low, stages, start, -(-local // 2))
         gates = [lax.ppermute(b, "replica", s) for b, s in zip(gates, steps)]
         downs = [lax.ppermute(b, "replica", s) for b, s in zip(downs, steps)]
         pieces.append((*gates, *downs, own_down))
-        before = (totals[-1],)
     arrived = lax.ppermute(totals[-1], "expert", ring)
     gate_up_gradient, down_gradient = keep_blocks(scal, low, stages, pieces)
     arrived, gate_up_gradient, down_gradient = lax.optimization_barrier((arrived, gate_up_gradient, down_gradient))

time: 141 us -> 120 us (0.85)
  Pallas kernels: 81.3 us -> 64.3 us
  other arithmetic: 4.53 us -> 2.09 us
  local copies, waits for them, and re-layouts: 22.9 us -> 20.6 us
    unnamed x50 -> x11, local copies, waits for them, and re-layouts: 22.9 us -> 15.7 us
    pallas_call x2, Pallas kernels: 12.8 us -> 5.9 us  [send_blocks(): pl.pallas_call(lambda s, *refs: body(s, *refs[k:]), grid_spec=pltpu.Prefe...]
    pallas_call x4, Pallas kernels: 56.3 us -> 50.1 us  [stage(): pl.pallas_call(functools.partial(stage_kernel, m, own, local, count, len(...]
    optimization_barrier x0 -> x1, local copies, waits for them, and re-layouts: none -> 4.89 us  [on_device(): lax.optimization_barrier((pays[1], others[0], wgu, down_weights))]
    pallas_call x1, Pallas kernels: 12.1 us -> 8.18 us  [keep_blocks(): pl.pallas_call(lambda s, *refs: body(s, *refs[k:]), grid_spec=pltpu.Prefe...]
    ppermute x4, starting transfers between devices: 6.54 us -> 4.07 us  [on_device(): others.append(lax.ppermute(pays[d], 'replica', across))]
    ppermute x2, starting transfers between devices: 1.87 us -> 3.92 us  [on_device(): lax.ppermute(totals[-1], 'expert', ring)]
    convert_element_type x3, other arithmetic: 3.3 us -> 1.4 us  [add(): return (got.astype(F32) + mine.astype(F32)).astype(BF)]
  transfers between devices with their start and end apart: 14 -> 14, of which waited for: 3 -> 5; matrix products, arithmetic and copies ran while one was open for 12% -> 15% of each run, Pallas kernels for 53% -> 42%
where the time goes in v3:
time: 120 us; the launch traced here: 119 us
  Pallas kernels  64.3 us (54%)
  local copies, waits for them, and re-layouts  20.6 us (17%)
  waiting for transfers between devices  18 us (15%)
  starting transfers between devices  13.4 us (11%)
  other arithmetic  2.09 us (2%)
    pallas_call x4, Pallas kernels, stage(): pl.pallas_call(functools.partial(stage_kernel, m, own, local, count, len(...  50.1 us
    unnamed x11, local copies, waits for them, and re-layouts  15.7 us
    ppermute x3, waiting for transfers between devices, on_device(): pays.append(lax.ppermute(pays[d], 'expert', ring))  9.8 us
    pallas_call x1, Pallas kernels, keep_blocks(): pl.pallas_call(lambda s, *refs: body(s, *refs[k:]), grid_spec=pltpu.Prefe...  8.18 us
    ppermute x2, waiting for transfers between devices, on_device(): downs = [lax.ppermute(b, 'replica', s) for b, s in zip(downs, steps)]  6.88 us
    pallas_call x2, Pallas kernels, send_blocks(): pl.pallas_call(lambda s, *refs: body(s, *refs[k:]), grid_spec=pltpu.Prefe...  5.9 us
    optimization_barrier x1, local copies, waits for them, and re-layouts, on_device(): lax.optimization_barrier((pays[1], others[0], wgu, down_weights))  4.89 us
    ppermute x3, starting transfers between devices, on_device(): pays.append(lax.ppermute(pays[d], 'expert', ring))  4.34 us
  transfers between devices with their start and end apart: 14, of which 5 were waited for; matrix products, arithmetic and copies ran while one was open for 15% of the time, Pallas kernels for 42%

profile of v3, /device:TPU:0, one launch (start us, length us, event | category | flops | bytes accessed | tf_op | source)
XLA Modules:
  0.0 119.2 jit_solution(15148206454726026709)
XLA Ops:
  0.6 0.9 copy-done
  1.6 0.9 copy-done.1
  2.5 0.7 copy-done.2
  3.2 0.7 copy-done.4
  4.0 3.0 %collective-permute-start = (bf16[272,1024]{1,0:T(8,128)(2,1)S(1)}, bf16[272,1024]{1,0:T(8,128)(2,1)S(1)}, u32[]{:S(2)}, u32[]{:S(2)}) collective-permute-start(bf16[272,1024]{1,0:T(8,128)(2,1)S(1)} %shard_map.101.refs_1_), channel_id=1, source_target_pairs={{0,4},{4,8},{8,12},{12,0},{1,5},{5,9},{9,13},{13,1},{2,6},{6,10},{... | collective-permute-start | bytes 1671176 | tf_op jit(solution)/shard_map/ppermute | solution.py:307
  7.1 1.5 %collective-permute-start.1 = (bf16[272,1024]{1,0:T(8,128)(2,1)S(1)}, bf16[272,1024]{1,0:T(8,128)(2,1)S(1)}, u32[]{:S(2)}, u32[]{:S(2)}) collective-permute-start(bf16[272,1024]{1,0:T(8,128)(2,1)S(1)} %shard_map.101.refs_1_), channel_id=1, source_target_pairs={{0,2},{1,3},{2,0},{3,1},{4,6},{5,7},{6,4},{7,5},{8,10},{9,11},{10,... | collective-permute-start | bytes 1671176 | tf_op jit(solution)/shard_map/ppermute | solution.py:305
  8.6 12.5 %copy.17 = bf16[1024,4,1536]{2,0,1:T(8,128)(2,1)} copy(bf16[1024,4,1536]{2,1,0:T(4,128)(2,1)} %param.10) | data formatting | bytes 25165824 | tf_op args[4]
  21.1 0.6 collective-permute-done.refs_0_
  21.7 1.0 collective-permute-start.3
  22.7 1.5 %collective-permute-start.4 = (bf16[272,1024]{1,0:T(8,128)(2,1)S(1)}, bf16[272,1024]{1,0:T(8,128)(2,1)S(1)}, u32[]{:S(2)}, u32[]{:S(2)}) collective-permute-start(bf16[272,1024]{1,0:T(8,128)(2,1)S(1)} %collective-permute-done.refs_0_), channel_id=1, source_target_pairs={{0,2},{1,3},{2,0},{3,1},{4,6},{5,7},{6,4},{7,5},{8,10},{9,11},{10,... | collective-permute-start | bytes 1671176 | tf_op jit(solution)/shard_map/ppermute | solution.py:305
  24.2 4.9 %copy.18 = bf16[768,4,1024]{2,0,1:T(8,128)(2,1)S(1)} copy(bf16[768,4,1024]{2,1,0:T(4,128)(2,1)} %param.11) | data formatting | bytes 12582912 | tf_op jit(solution)/shard_map/optimization_barrier | solution.py:309
  29.1 13.1 %shard_map.102 = (bf16[4,128,512]{2,1,0:T(8,128)(2,1)S(1)}, bf16[4,128,384]{2,1,0:T(8,128)(2,1)S(1)}, bf16[4,128,1536]{2,1,0:T(8,128)(2,1)S(1)}, bf16[4,128,1024]{2,1,0:T(8,128)(2,1)S(1)}, bf16[272,1024]{1,0:T(8,128)(2,1)S(1)}) custom-call(s32[3]{0:T(128)S(1)} %pad_add_fusion.scal.s, bf16[272,1024]{1,0:T(8,128)(2,1)S(1)} %collective-permute-done.refs_0_, ...), custom_call_target="tpu_custom_call" | custom-call | flops 14000000000 | bytes 25165824 | tf_op jit(solution)/shard_map/pallas_call | solution.py:177
  42.3 1.6 %collective-permute-start.2 = (bf16[272,1024]{1,0:T(8,128)(2,1)S(1)}, bf16[272,1024]{1,0:T(8,128)(2,1)S(1)}, u32[]{:S(2)}, u32[]{:S(2)}) collective-permute-start(bf16[272,1024]{1,0:T(8,128)(2,1)S(1)} %get-tuple-element.44.refs_6_), channel_id=1, source_target_pairs={{0,4},{4,8},{8,12},{12,0},{1,5},{5,9},{9,13},{13,1},{2,6},{6,10},{... | collective-permute-start | bytes 1671176 | tf_op jit(solution)/shard_map/ppermute | solution.py:328
  43.9 0.3 collective-permute-start.6
  44.2 0.5 collective-permute-start.7
  44.8 15.2 %shard_map.103 = (bf16[4,192,512]{2,1,0:T(8,128)(2,1)S(1)}, bf16[4,192,384]{2,1,0:T(8,128)(2,1)S(1)}, bf16[4,192,1536]{2,1,0:T(8,128)(2,1)S(1)}, bf16[4,192,1024...) custom-call(s32[3]{0:T(128)S(1)} %pad_add_fusion.scal.s, ...), custom_call_target="tpu_custom_call" | custom-call | flops 14000000000 | bytes 25165824 | tf_op jit(solution)/shard_map/pallas_call | solution.py:177
  60.0 0.2 add_convert_fusion.1.refs_5_
  60.2 2.3 %collective-permute-start.5 = (bf16[272,1024]{1,0:T(8,128)(2,1)S(1)}, bf16[272,1024]{1,0:T(8,128)(2,1)S(1)}, u32[]{:S(2)}, u32[]{:S(2)}) collective-permute-start(bf16[272,1024]{1,0:T(8,128)(2,1)S(1)} %add_convert_fusion.1.refs_5_), channel_id=1, source_target_pairs={{0,4},{4,8},{8,12},{12,0},{1,5},{5,9},{9,13},{13,1},{2,6},{6,10},{... | collective-permute-start | bytes 1671176 | tf_op jit(solution)/shard_map/ppermute | solution.py:328
  62.5 9.2 %collective-permute-done.6.refs_0_ = bf16[272,1024]{1,0:T(8,128)(2,1)S(1)} collective-permute-done((bf16[272,1024]{1,0:T(8,128)(2,1)S(1)}, bf16[272,1024]{1,0:T(8,128)(2,1)S(1)}, u32[]{:S(2)}, u32[]{:S(2)}) %collective-permute-start.6) | collective-permute-done | bytes 557088 | tf_op jit(solution)/shard_map/ppermute | solution.py:307
  71.6 0.5 collective-permute-start.9
  72.2 13.2 %shard_map.104 = (bf16[4,128,512]{2,1,0:T(8,128)(2,1)S(1)}, bf16[4,128,384]{2,1,0:T(8,128)(2,1)S(1)}, bf16[4,128,1536]{2,1,0:T(8,128)(2,1)S(1)}, bf16[4,128,1024]{2,1,0:T(8,128)(2,1)S(1)}, bf16[272,1024]{1,0:T(8,128)(2,1)S(1)}) custom-call(s32[3]{0:T(128)S(1)} %pad_add_fusion.scal.s, bf16[272,1024]{1,0:T(8,128)(2,1)S(1)} %collective-permute-done.6.refs_0_, ...), custom_call_target="tpu_custom_call" | custom-call | flops 14000000000 | bytes 25165824 | tf_op jit(solution)/shard_map/pallas_call | solution.py:177
  85.6 8.6 %shard_map.105 = (bf16[4,64,512]{2,1,0:T(8,128)(2,1)S(1)}, bf16[4,64,384]{2,1,0:T(8,128)(2,1)S(1)}, bf16[4,64,1536]{2,1,0:T(8,128)(2,1)S(1)}, bf16[4,64,1024]{2,1,0:T(8,128)(2,1)S(1)}) custom-call(s32[3]{0:T(128)S(1)} %pad_add_fusion.scal.s, bf16[272,1024]{1,0:T(8,128)(2,1)S(1)} %collective-permute-done.9.refs_0_, bf16[4,1024,1536]{2,1,0:T(8,128)(2,1)} %bitcast.22, ...), custom_call_target="tpu_custom_call" | custom-call | flops 7000000000 | bytes 25165824 | tf_op jit(solution)/shard_map/pallas_call | solution.py:177
  94.2 3.0 %shard_map.107 = (bf16[2,256,1536]{2,1,0:T(8,128)(2,1)S(1)}, bf16[2,192,1024]{2,1,0:T(8,128)(2,1)S(1)}, f32[2,192,1024]{2,1,0:T(8,128)S(1)}) custom-call(s32[3]{0:T(128)S(1)} %pad_add_fusion.scal.s, bf16[4,128,512]{2,1,0:T(8,128)(2,1)S(1)} %get-tuple-element.49.refs_0_, bf16[4,192,512]{2,1,0:T(8,128)(2,1)S(1)} %get-tuple-element.50.refs_1_, ...), custom_call_target="tpu_custom_call" | custom-call | flops 4000000000 | bytes 25165824 | tf_op jit(solution)/shard_map/pallas_call | solution.py:227
  97.2 2.9 %shard_map.106 = (bf16[2,256,1536]{2,1,0:T(8,128)(2,1)S(1)}, bf16[2,192,1024]{2,1,0:T(8,128)(2,1)S(1)}, f32[2,192,1024]{2,1,0:T(8,128)S(1)}) custom-call(s32[3]{0:T(128)S(1)} %pad_add_fusion.scal.s, bf16[4,128,512]{2,1,0:T(8,128)(2,1)S(1)} %get-tuple-element.49.refs_0_, bf16[4,192,512]{2,1,0:T(8,128)(2,1)S(1)} %get-tuple-element.50.refs_1_, ...), custom_call_target="tpu_custom_call" | custom-call | flops 4000000000 | bytes 25165824 | tf_op jit(solution)/shard_map/pallas_call | solution.py:227
  100.2 0.5 collective-permute-start.10
  100.8 0.4 collective-permute-start.11
  101.2 5.8 %collective-permute-done.13.refs_12_ = bf16[2,192,1024]{2,1,0:T(8,128)(2,1)S(1)} collective-permute-done((bf16[2,192,1024]{2,1,0:T(8,128)(2,1)S(1)}, bf16[2,192,1024]{2,1,0:T(8,128)(2,1)S(1)}, u32[]{:S(2)}, u32[]{:S(2)}) %collective-permute-start.13) | collective-permute-done | bytes 786464 | tf_op jit(solution)/shard_map/ppermute | solution.py:335
  107.0 1.1 collective-permute-done.11.refs_9_
  108.1 8.2 %shard_map.108 = (f32[256,4,1536]{2,1,0:T(4,128)}, f32[192,4,1024]{2,1,0:T(4,128)}) custom-call(s32[3]{0:T(128)S(1)} %pad_add_fusion.scal.s, bf16[4,128,512]{2,1,0:T(8,128)(2,1)S(1)} %get-tuple-element.49.refs_0_, bf16[4,192,512]{2,1,0:T(8,128)(2,1)S(1)} %get-tuple-element.50.refs_1_, bf16[4,128,512]{2,1,0:T(8,128)(2,1)S(1)} %get-tuple-element.51.refs_2_, ...), custom_call_target="tpu_custom_call" | custom-call | flops 6000000000 | bytes 25165824 | tf_op jit(solution)/shard_map/pallas_call | solution.py:275
  116.3 1.3 %collective-permute-done.8 = bf16[272,1024]{1,0:T(8,128)(2,1)S(1)} collective-permute-done((bf16[272,1024]{1,0:T(8,128)(2,1)S(1)}, bf16[272,1024]{1,0:T(8,128)(2,1)S(1)}, u32[]{:S(2)}, u32[]{:S(2)}) %collective-permute-start.8) | collective-permute-done | bytes 557088 | tf_op jit(solution)/shard_map/ppermute | solution.py:337
  117.6 1.0 add_convert_fusion.2
  118.6 0.6 select_reduce_fusion
  (23 shorter events, 0.6 us)
Async XLA Ops:
  0.6 1.0 copy-start
  1.6 0.9 copy-start.1
  2.5 0.7 copy-start.2
  3.2 0.7 copy-start.4
  4.0 17.7 %collective-permute-start = (bf16[272,1024]{1,0:T(8,128)(2,1)S(1)}, bf16[272,1024]{1,0:T(8,128)(2,1)S(1)}, u32[]{:S(2)}, u32[]{:S(2)}) collective-permute-start(bf16[272,1024]{1,0:T(8,128)(2,1)S(1)} %shard_map.101.refs_1_), channel_id=1, source_target_pairs={{0,4},{4,8},{8,12},{12,0},{1,5},{5,9},{9,13},{13,1},{2,6},{6,10},{... | collective-permute-start | bytes 1671176 | tf_op jit(solution)/shard_map/ppermute | solution.py:307
  7.1 14.7 %collective-permute-start.1 = (bf16[272,1024]{1,0:T(8,128)(2,1)S(1)}, bf16[272,1024]{1,0:T(8,128)(2,1)S(1)}, u32[]{:S(2)}, u32[]{:S(2)}) collective-permute-start(bf16[272,1024]{1,0:T(8,128)(2,1)S(1)} %shard_map.101.refs_1_), channel_id=1, source_target_pairs={{0,2},{1,3},{2,0},{3,1},{4,6},{5,7},{6,4},{7,5},{8,10},{9,11},{10,... | collective-permute-start | bytes 1671176 | tf_op jit(solution)/shard_map/ppermute | solution.py:305
  21.7 22.2 %collective-permute-start.3 = (bf16[272,1024]{1,0:T(8,128)(2,1)S(1)}, bf16[272,1024]{1,0:T(8,128)(2,1)S(1)}, u32[]{:S(2)}, u32[]{:S(2)}) collective-permute-start(bf16[272,1024]{1,0:T(8,128)(2,1)S(1)} %collective-permute-done.refs_0_), channel_id=1, source_target_pairs={{0,4},{4,8},{8,12},{12,0},{1,5},{5,9},{9,13},{13,1},{2,6},{6,10},{... | collective-permute-start | bytes 1671176 | tf_op jit(solution)/shard_map/ppermute | solution.py:307
  22.7 22.0 %collective-permute-start.4 = (bf16[272,1024]{1,0:T(8,128)(2,1)S(1)}, bf16[272,1024]{1,0:T(8,128)(2,1)S(1)}, u32[]{:S(2)}, u32[]{:S(2)}) collective-permute-start(bf16[272,1024]{1,0:T(8,128)(2,1)S(1)} %collective-permute-done.refs_0_), channel_id=1, source_target_pairs={{0,2},{1,3},{2,0},{3,1},{4,6},{5,7},{6,4},{7,5},{8,10},{9,11},{10,... | collective-permute-start | bytes 1671176 | tf_op jit(solution)/shard_map/ppermute | solution.py:305
  42.3 17.7 %collective-permute-start.2 = (bf16[272,1024]{1,0:T(8,128)(2,1)S(1)}, bf16[272,1024]{1,0:T(8,128)(2,1)S(1)}, u32[]{:S(2)}, u32[]{:S(2)}) collective-permute-start(bf16[272,1024]{1,0:T(8,128)(2,1)S(1)} %get-tuple-element.44.refs_6_), channel_id=1, source_target_pairs={{0,4},{4,8},{8,12},{12,0},{1,5},{5,9},{9,13},{13,1},{2,6},{6,10},{... | collective-permute-start | bytes 1671176 | tf_op jit(solution)/shard_map/ppermute | solution.py:328
  43.9 27.7 %collective-permute-start.6 = (bf16[272,1024]{1,0:T(8,128)(2,1)S(1)}, bf16[272,1024]{1,0:T(8,128)(2,1)S(1)}, u32[]{:S(2)}, u32[]{:S(2)}) collective-permute-start(bf16[272,1024]{1,0:T(8,128)(2,1)S(1)} %collective-permute-done.3.refs_0_), channel_id=1, source_target_pairs={{0,4},{4,8},{8,12},{12,0},{1,5},{5,9},{9,13},{13,1},{2,6},{6,10},{... | collective-permute-start | bytes 1671176 | tf_op jit(solution)/shard_map/ppermute | solution.py:307
  44.2 28.0 %collective-permute-start.7 = (bf16[272,1024]{1,0:T(8,128)(2,1)S(1)}, bf16[272,1024]{1,0:T(8,128)(2,1)S(1)}, u32[]{:S(2)}, u32[]{:S(2)}) collective-permute-start(bf16[272,1024]{1,0:T(8,128)(2,1)S(1)} %collective-permute-done.3.refs_0_), channel_id=1, source_target_pairs={{0,2},{1,3},{2,0},{3,1},{4,6},{5,7},{6,4},{7,5},{8,10},{9,11},{10,... | collective-permute-start | bytes 1671176 | tf_op jit(solution)/shard_map/ppermute | solution.py:305
  60.2 25.2 %collective-permute-start.5 = (bf16[272,1024]{1,0:T(8,128)(2,1)S(1)}, bf16[272,1024]{1,0:T(8,128)(2,1)S(1)}, u32[]{:S(2)}, u32[]{:S(2)}) collective-permute-start(bf16[272,1024]{1,0:T(8,128)(2,1)S(1)} %add_convert_fusion.1.refs_5_), channel_id=1, source_target_pairs={{0,4},{4,8},{8,12},{12,0},{1,5},{5,9},{9,13},{13,1},{2,6},{6,10},{... | collective-permute-start | bytes 1671176 | tf_op jit(solution)/shard_map/ppermute | solution.py:328
  71.6 13.9 %collective-permute-start.9 = (bf16[272,1024]{1,0:T(8,128)(2,1)S(1)}, bf16[272,1024]{1,0:T(8,128)(2,1)S(1)}, u32[]{:S(2)}, u32[]{:S(2)}) collective-permute-start(bf16[272,1024]{1,0:T(8,128)(2,1)S(1)} %collective-permute-done.6.refs_0_), channel_id=1, source_target_pairs={{0,2},{1,3},{2,0},{3,1},{4,6},{5,7},{6,4},{7,5},{8,10},{9,11},{10,... | collective-permute-start | bytes 1671176 | tf_op jit(solution)/shard_map/ppermute | solution.py:305
  100.1 8.0 %collective-permute-start.12 = (bf16[2,256,1536]{2,1,0:T(8,128)(2,1)S(1)}, bf16[2,256,1536]{2,1,0:T(8,128)(2,1)S(1)}, u32[]{:S(2)}, u32[]{:S(2)}) collective-permute-start(bf16[2,256,1536]{2,1,0:T(8,128)(2,1)S(1)} %get-tuple-element.66), channel_id=1, source_target_pairs={{0,1},{1,0},{2,3},{3,2},{4,5},{5,4},{6,7},{7,6},{8,9},{9,8},{10,11... | collective-permute-start | bytes 4718600 | tf_op jit(solution)/shard_map/ppermute | solution.py:334
  100.2 7.9 %collective-permute-start.10 = (bf16[2,256,1536]{2,1,0:T(8,128)(2,1)S(1)}, bf16[2,256,1536]{2,1,0:T(8,128)(2,1)S(1)}, u32[]{:S(2)}, u32[]{:S(2)}) collective-permute-start(bf16[2,256,1536]{2,1,0:T(8,128)(2,1)S(1)} %get-tuple-element.63), channel_id=1, source_target_pairs={{0,1},{1,0},{2,3},{3,2},{4,5},{5,4},{6,7},{7,6},{8,9},{9,8},{10,11... | collective-permute-start | bytes 4718600 | tf_op jit(solution)/shard_map/ppermute | solution.py:334
  100.7 6.3 %collective-permute-start.13 = (bf16[2,192,1024]{2,1,0:T(8,128)(2,1)S(1)}, bf16[2,192,1024]{2,1,0:T(8,128)(2,1)S(1)}, u32[]{:S(2)}, u32[]{:S(2)}) collective-permute-start(bf16[2,192,1024]{2,1,0:T(8,128)(2,1)S(1)} %get-tuple-element.67), channel_id=1, source_target_pairs={{0,1},{1,0},{2,3},{3,2},{4,5},{5,4},{6,7},{7,6},{8,9},{9,8},{10,11... | collective-permute-start | bytes 2359304 | tf_op jit(solution)/shard_map/ppermute | solution.py:335
  100.8 7.3 %collective-permute-start.11 = (bf16[2,192,1024]{2,1,0:T(8,128)(2,1)S(1)}, bf16[2,192,1024]{2,1,0:T(8,128)(2,1)S(1)}, u32[]{:S(2)}, u32[]{:S(2)}) collective-permute-start(bf16[2,192,1024]{2,1,0:T(8,128)(2,1)S(1)} %get-tuple-element.64), channel_id=1, source_target_pairs={{0,1},{1,0},{2,3},{3,2},{4,5},{5,4},{6,7},{7,6},{8,9},{9,8},{10,11... | collective-permute-start | bytes 2359304 | tf_op jit(solution)/shard_map/ppermute | solution.py:335
  101.2 16.4 %collective-permute-start.8 = (bf16[272,1024]{1,0:T(8,128)(2,1)S(1)}, bf16[272,1024]{1,0:T(8,128)(2,1)S(1)}, u32[]{:S(2)}, u32[]{:S(2)}) collective-permute-start(bf16[272,1024]{1,0:T(8,128)(2,1)S(1)} %add_convert_fusion.refs_4_), channel_id=1, source_target_pairs={{0,4},{4,8},{8,12},{12,0},{1,5},{5,9},{9,13},{13,1},{2,6},{6,10},{... | collective-permute-start | bytes 1671176 | tf_op jit(solution)/shard_map/ppermute | solution.py:337
  116.3 2.3 %copy-start.3 = (s32[128,6]{0,1:T(8,128)S(1)}, s32[128,6]{0,1:T(8,128)}, u32[]{:S(2)}) copy-start(s32[128,6]{0,1:T(8,128)} %param.7) | copy-start | bytes 9220

commit v4 on v3

--- a/solution.py
+++ b/solution.py
@@ -11,6 +11,7 @@
 HALVES = 2
 EARLY_VMEM = 34 * 1024 * 1024
 STAGE_VMEM = 34 * 1024 * 1024
+PACK_VMEM = 60 * 1024 * 1024
 SHARE_VMEM = 16 * 1024 * 1024
 BF = jnp.bfloat16
 F32 = jnp.float32
@@ -62,7 +63,7 @@
     return pl.pallas_call(
         pack_kernel,
         out_shape=jax.ShapeDtypeStruct((2 * count + experts, width), BF),
-        compiler_params=pltpu.CompilerParams(vmem_limit_bytes=8 * 1024 * 1024),
+        compiler_params=pltpu.CompilerParams(vmem_limit_bytes=PACK_VMEM),
     )(ids.T, probs.T, tokens, cot)
 
 
@@ -237,57 +238,65 @@
         out_shape=outs,
         compiler_params=pltpu.CompilerParams(vmem_limit_bytes=SHARE_VMEM),
         cost_estimate=pl.CostEstimate(
-            flops=4 * 1000 * 1000 * 1000, bytes_accessed=24 << 20, transcendentals=0
+            flops=0, bytes_accessed=1 << 10, transcendentals=0
         ),
     )(scal, *after, *xs, *hs, *pgs, *gss)
     return res[: low - 1], res[low - 1 : 2 * low - 2], res[-1]
 
 
-def keep_kernel(parts, pieces, low, scal, *refs):
-    xs, pgs, refs = refs[:parts], refs[parts : 2 * parts], refs[2 * parts :]
-    gate_ref, down_ref = refs[-2:]
-    each = gate_ref.shape[1] // pieces
-    got = [refs[k * (2 * low - 1) : (k + 1) * (2 * low - 1)] for k in range(pieces)]
+def own_kernel(parts, low, scal, *refs):
+    xs, pgs, out_ref = refs[:parts], refs[parts : 2 * parts], refs[-1]
     size = xs[0].shape[-1] // low
     cols = pl.ds(pl.multiple_of(scal[2] * size, size), size)
-    for e in range(gate_ref.shape[1]):
-        total = mm_t0(
-            jnp.concatenate([x[e, :, cols] for x in xs], axis=0), jnp.concatenate([p[e] for p in pgs], axis=0)
-        )
-        arrived = got[e // each]
-        gate_ref[:, e, :] = total + sum(g[e % each].astype(F32) for g in arrived[: low - 1])
-        down_ref[:, e, :] = arrived[-1][e % each] + sum(g[e % each].astype(F32) for g in arrived[low - 1 : -1])
-
-
-def keep_blocks(scal, low, stages, pieces, after=()):
+    out_ref[0] = mm_t0(
+        jnp.concatenate([x[0, :, cols] for x in xs], axis=0), jnp.concatenate([p[0] for p in pgs], axis=0)
+    )
+
+
+def own_blocks(scal, low, stages, after):
     xs, _, pgs, _ = zip(*stages)
-    local, rows, half_d = xs[0].shape
-    two_f, width = pgs[0].shape[-1], half_d * HALVES
-    steps = 4
-    lanes = lambda a: pl.BlockSpec(a.shape[:-1] + (a.shape[-1] // steps,), lambda c, s: (0, 0, c))
-    outs = [
-        jax.ShapeDtypeStruct((half_d // low, local, two_f), F32),
-        jax.ShapeDtypeStruct((pieces[0][-1].shape[1], local, width), F32),
-    ]
-    k = len(after)
-    body = functools.partial(keep_kernel, len(stages), len(pieces), low)
-    arrived = [a for piece in pieces for a in piece]
+    out = jax.ShapeDtypeStruct((xs[0].shape[0], xs[0].shape[-1] // low, pgs[0].shape[-1]), F32)
     return pl.pallas_call(
-        lambda s, *refs: body(s, *refs[k:]),
+        functools.partial(own_kernel, len(stages), low),
         grid_spec=pltpu.PrefetchScalarGridSpec(
             num_scalar_prefetch=1,
-            grid=(steps,),
-            in_specs=[pl.BlockSpec(memory_space=pl.ANY)] * k
-            + [full(x.shape) for x in xs]
-            + [lanes(a) for a in (*pgs, *arrived)],
-            out_specs=[lanes(o) for o in outs],
-        ),
+            grid=(out.shape[0],),
+            in_specs=[per_expert(a.shape) for a in (*xs, *pgs)] + [pl.BlockSpec(memory_space=pl.ANY)] * len(after),
+            out_specs=per_expert(out.shape),
+        ),
+        out_shape=out,
+        compiler_params=pltpu.CompilerParams(vmem_limit_bytes=SHARE_VMEM),
+        cost_estimate=pl.CostEstimate(flops=0, bytes_accessed=1 << 10, transcendentals=0),
+    )(scal, *xs, *pgs, *after)
+
+
+def join_kernel(pieces, low, own_ref, *refs):
+    gate_ref, down_ref = refs[-2:]
+    e = 0
+    for k in range(pieces):
+        arrived = refs[k * (2 * low - 1) : (k + 1) * (2 * low - 1)]
+        for i in range(arrived[-1].shape[0]):
+            gate_ref[:, e, :] = own_ref[e] + sum(g[i].astype(F32) for g in arrived[: low - 1])
+            down_ref[:, e, :] = arrived[-1][i] + sum(g[i].astype(F32) for g in arrived[low - 1 : -1])
+            e += 1
+
+
+def join_blocks(low, own, pieces):
+    arrived = [a for piece in pieces for a in piece]
+    local, steps = own.shape[0], 4
+    lanes = lambda a: pl.BlockSpec(a.shape[:-1] + (a.shape[-1] // steps,), lambda c: (0, 0, c))
+    outs = [
+        jax.ShapeDtypeStruct((a.shape[1], local, a.shape[-1]), F32) for a in (own, pieces[0][-1])
+    ]
+    return pl.pallas_call(
+        functools.partial(join_kernel, len(pieces), low),
+        grid=(steps,),
+        in_specs=[lanes(a) for a in (own, *arrived)],
+        out_specs=[lanes(o) for o in outs],
         out_shape=outs,
         compiler_params=pltpu.CompilerParams(vmem_limit_bytes=SHARE_VMEM),
-        cost_estimate=pl.CostEstimate(
-            flops=6 * 1000 * 1000 * 1000, bytes_accessed=24 << 20, transcendentals=0
-        ),
-    )(scal, *after, *xs, *pgs, *arrived)
+        cost_estimate=pl.CostEstimate(flops=5 * 1000 * 1000 * 1000, bytes_accessed=16 << 20, transcendentals=0),
+    )(own, *arrived)
 
 
 def on_device(n, replicas, tokens, expert_ids, gate_probs, cotangent, gate_up, down_weights):
@@ -325,18 +334,26 @@
         before = (outs[3],)
         for d in ready:
             if d:
-                totals.append(add(lax.ppermute(totals[-1], "expert", ring), sums[d]) if totals else sums[d])
+                if totals:
+                    send, _ = lax.optimization_barrier((totals[-1], pays[d]))
+                    totals.append(add(lax.ppermute(send, "expert", ring), sums[d]))
+                else:
+                    totals.append(sums[d])
                 before = (outs[3], totals[-1])
     steps = [[(i, i // low * low + (i % low + j) % low) for i in range(replicas)] for j in range(1, low)]
-    pieces = []
-    for start in range(0, local, -(-local // 2)):
-        gates, downs, own_down = send_blocks(scal, low, stages, start, -(-local // 2))
+    arrived = lax.ppermute(totals[-1], "expert", ring)
+    last = local // 2
+    pieces, sent = [], ()
+    for start, size in ((0, last), (last, local - last)) if last else ((0, local),):
+        gates, downs, own_down = send_blocks(scal, low, stages, start, size)
+        sent = (*gates, *downs)
+        if start:
+            gates, downs, arrived = lax.optimization_barrier((gates, downs, arrived))
         gates = [lax.ppermute(b, "replica", s) for b, s in zip(gates, steps)]
         downs = [lax.ppermute(b, "replica", s) for b, s in zip(downs, steps)]
         pieces.append((*gates, *downs, own_down))
-    arrived = lax.ppermute(totals[-1], "expert", ring)
-    gate_up_gradient, down_gradient = keep_blocks(scal, low, stages, pieces)
-    arrived, gate_up_gradient, down_gradient = lax.optimization_barrier((arrived, gate_up_gradient, down_gradient))
+    own = own_blocks(scal, low, stages, sent)
+    gate_up_gradient, down_gradient = join_blocks(low, own, pieces)
     combined, token_gradient = add(arrived[:count], sums[0][:count]), add(arrived[count : 2 * count], sums[0][count : 2 * count])
     dots = arrived[2 * count :, : 2 * count].astype(F32) + sums[0][2 * count :, : 2 * count].astype(F32)
     dots = dots[:, :count] + dots[:, count:]

time: 120 us -> 111 us (0.925)
  waiting for transfers between devices: 18 us -> 11.8 us
  local copies, waits for them, and re-layouts: 20.6 us -> 17.4 us
  Pallas kernels: 64.3 us -> 66.4 us
  starting transfers between devices: 13.4 us -> 11.7 us
    ppermute x2, waiting for transfers between devices: 6.88 us -> 2.23 us  [on_device(): downs = [lax.ppermute(b, 'replica', s) for b, s in zip(downs, steps)]]
    unnamed x11 -> x5, local copies, waits for them, and re-layouts: 15.7 us -> 12.5 us
    ppermute x2, starting transfers between devices: 3.92 us -> 1.63 us  [on_device(): totals.append(add(lax.ppermute(send, 'expert', ring), sums[d]))]
    pallas_call x1, Pallas kernels: 0.15 us -> 2 us  [pack(): pl.pallas_call(pack_kernel, out_shape=jax.ShapeDtypeStruct((2 * count + e...]
    ppermute x1, waiting for transfers between devices: 1.33 us -> 0.01 us  [on_device(): arrived = lax.ppermute(totals[-1], 'expert', ring)]
    pallas_call x1 -> x2, Pallas kernels: 8.18 us -> 8.59 us  [the longest x1 5.63 us: join_blocks(): pl.pallas_call(functools.partial(join_kernel, len(pieces), low), grid=(st...]
  transfers between devices with their start and end apart: 14 -> 14, of which waited for: 5 -> 4; matrix products, arithmetic and copies ran while one was open for 15% -> 18% of each run, Pallas kernels for 42% -> 53%
where the time goes in v4:
time: 111 us; the launch traced here: 110 us
  Pallas kernels  66.4 us (60%)
  local copies, waits for them, and re-layouts  17.4 us (16%)
  waiting for transfers between devices  11.8 us (11%)
  starting transfers between devices  11.7 us (11%)
  other arithmetic  2.09 us (2%)
    pallas_call x4, Pallas kernels, stage(): pl.pallas_call(functools.partial(stage_kernel, m, own, local, count, len(...  49.9 us
    unnamed x5, local copies, waits for them, and re-layouts  12.5 us
    ppermute x3, waiting for transfers between devices, on_device(): pays.append(lax.ppermute(pays[d], 'expert', ring))  9.49 us
    pallas_call x2, Pallas kernels, send_blocks(): pl.pallas_call(lambda s, *refs: body(s, *refs[k:]), grid_spec=pltpu.Prefe...  5.9 us
    pallas_call x1, Pallas kernels, join_blocks(): pl.pallas_call(functools.partial(join_kernel, len(pieces), low), grid=(st...  5.63 us
    optimization_barrier x1, local copies, waits for them, and re-layouts, on_device(): lax.optimization_barrier((pays[1], others[0], wgu, down_weights))  4.89 us
    ppermute x4, starting transfers between devices, on_device(): others.append(lax.ppermute(pays[d], 'replica', across))  4.44 us
    ppermute x3, starting transfers between devices, on_device(): pays.append(lax.ppermute(pays[d], 'expert', ring))  4.32 us
  transfers between devices with their start and end apart: 14, of which 4 were waited for; matrix products, arithmetic and copies ran while one was open for 18% of the time, Pallas kernels for 53%

profile of v4, /device:TPU:0, one launch (start us, length us, event | category | flops | bytes accessed | tf_op | source)
XLA Modules:
  0.0 110.1 jit_solution(8784554477805002194)
XLA Ops:
  0.6 2.0 %shard_map.101.refs_1_ = bf16[272,1024]{1,0:T(8,128)(2,1)} custom-call(s32[6,128]{1,0:T(8,128)} %bitcast.20, bf16[6,128]{1,0:T(8,128)(2,1)} %bitcast.23, bf16[128,1024]{1,0:T(8,128)(2,1)} %tok_ref.1, bf16[128,1024]{1,0:T(8,128)(2,1)} %cot_ref.1), custom_call_target="tpu_custom_call" | custom-call | tf_op jit(solution)/shard_map/pallas_call | solution.py:63
  2.6 3.0 %collective-permute-start = (bf16[272,1024]{1,0:T(8,128)(2,1)}, bf16[272,1024]{1,0:T(8,128)(2,1)S(1)}, u32[]{:S(2)}, u32[]{:S(2)}) collective-permute-start(bf16[272,1024]{1,0:T(8,128)(2,1)} %shard_map.101.refs_1_), channel_id=1, source_target_pairs={{0,4},{4,8},{8,12},{12,0},{1,5},{5,9},{9,13},{13,1},{2,6},{6,10},{... | collective-permute-start | bytes 1671176 | tf_op jit(solution)/shard_map/ppermute | solution.py:316
  5.7 1.5 %collective-permute-start.1 = (bf16[272,1024]{1,0:T(8,128)(2,1)}, bf16[272,1024]{1,0:T(8,128)(2,1)S(1)}, u32[]{:S(2)}, u32[]{:S(2)}) collective-permute-start(bf16[272,1024]{1,0:T(8,128)(2,1)} %shard_map.101.refs_1_), channel_id=1, source_target_pairs={{0,2},{1,3},{2,0},{3,1},{4,6},{5,7},{6,4},{7,5},{8,10},{9,11},{10,... | collective-permute-start | bytes 1671176 | tf_op jit(solution)/shard_map/ppermute | solution.py:314
  7.2 12.5 %copy.17 = bf16[1024,4,1536]{2,0,1:T(8,128)(2,1)} copy(bf16[1024,4,1536]{2,1,0:T(4,128)(2,1)} %param.10) | data formatting | bytes 25165824 | tf_op args[4]
  19.6 0.1 pad_add_fusion.scal.s
  19.7 0.8 collective-permute-done.refs_0_
  20.5 1.0 collective-permute-start.2
  21.5 1.5 %collective-permute-start.3 = (bf16[272,1024]{1,0:T(8,128)(2,1)S(1)}, bf16[272,1024]{1,0:T(8,128)(2,1)S(1)}, u32[]{:S(2)}, u32[]{:S(2)}) collective-permute-start(bf16[272,1024]{1,0:T(8,128)(2,1)S(1)} %collective-permute-done.refs_0_), channel_id=1, source_target_pairs={{0,2},{1,3},{2,0},{3,1},{4,6},{5,7},{6,4},{7,5},{8,10},{9,11},{10,... | collective-permute-start | bytes 1671176 | tf_op jit(solution)/shard_map/ppermute | solution.py:314
  23.0 4.9 %copy.18 = bf16[768,4,1024]{2,0,1:T(8,128)(2,1)S(1)} copy(bf16[768,4,1024]{2,1,0:T(4,128)(2,1)} %param.11) | data formatting | bytes 12582912 | tf_op jit(solution)/shard_map/optimization_barrier | solution.py:318
  27.9 13.1 %shard_map.102 = (bf16[4,128,512]{2,1,0:T(8,128)(2,1)S(1)}, bf16[4,128,384]{2,1,0:T(8,128)(2,1)S(1)}, bf16[4,128,1536]{2,1,0:T(8,128)(2,1)S(1)}, bf16[4,128,1024]{2,1,0:T(8,128)(2,1)S(1)}, bf16[272,1024]{1,0:T(8,128)(2,1)S(1)}) custom-call(s32[3]{0:T(128)S(1)} %pad_add_fusion.scal.s, bf16[272,1024]{1,0:T(8,128)(2,1)S(1)} %collective-permute-done.refs_0_, ...), custom_call_target="tpu_custom_call" | custom-call | flops 14000000000 | bytes 25165824 | tf_op jit(solution)/shard_map/pallas_call | solution.py:178
  41.1 1.6 %collective-permute-start.6 = (bf16[272,1024]{1,0:T(8,128)(2,1)S(1)}, bf16[272,1024]{1,0:T(8,128)(2,1)S(1)}, u32[]{:S(2)}, u32[]{:S(2)}) collective-permute-start(bf16[272,1024]{1,0:T(8,128)(2,1)S(1)} %get-tuple-element.51.refs_6_), channel_id=1, source_target_pairs={{0,4},{4,8},{8,12},{12,0},{1,5},{5,9},{9,13},{13,1},{2,6},{6,10},{... | collective-permute-start | bytes 1671176 | tf_op jit(solution)/shard_map/ppermute | solution.py:339
  42.7 0.3 collective-permute-start.4
  43.0 0.5 collective-permute-start.5
  43.5 15.1 %shard_map.103 = (bf16[4,192,512]{2,1,0:T(8,128)(2,1)S(1)}, bf16[4,192,384]{2,1,0:T(8,128)(2,1)S(1)}, bf16[4,192,1536]{2,1,0:T(8,128)(2,1)S(1)}, bf16[4,192,1024...) custom-call(s32[3]{0:T(128)S(1)} %pad_add_fusion.scal.s, ...), custom_call_target="tpu_custom_call" | custom-call | flops 14000000000 | bytes 25165824 | tf_op jit(solution)/shard_map/pallas_call | solution.py:178
  58.6 0.2 add_convert_fusion.1.refs_5_
  58.8 8.7 %collective-permute-done.4.refs_0_ = bf16[272,1024]{1,0:T(8,128)(2,1)S(1)} collective-permute-done((bf16[272,1024]{1,0:T(8,128)(2,1)S(1)}, bf16[272,1024]{1,0:T(8,128)(2,1)S(1)}, u32[]{:S(2)}, u32[]{:S(2)}) %collective-permute-start.4) | collective-permute-done | bytes 557088 | tf_op jit(solution)/shard_map/ppermute | solution.py:316
  67.5 0.9 collective-permute-start.7
  68.4 13.1 %shard_map.104 = (bf16[4,128,512]{2,1,0:T(8,128)(2,1)S(1)}, bf16[4,128,384]{2,1,0:T(8,128)(2,1)S(1)}, bf16[4,128,1536]{2,1,0:T(8,128)(2,1)S(1)}, bf16[4,128,1024]{2,1,0:T(8,128)(2,1)S(1)}, bf16[272,1024]{1,0:T(8,128)(2,1)S(1)}) custom-call(s32[3]{0:T(128)S(1)} %pad_add_fusion.scal.s, bf16[272,1024]{1,0:T(8,128)(2,1)S(1)} %collective-permute-done.4.refs_0_, ...), custom_call_target="tpu_custom_call" | custom-call | flops 14000000000 | bytes 25165824 | tf_op jit(solution)/shard_map/pallas_call | solution.py:178
  81.5 0.2 add_convert_fusion.refs_4_
  81.7 0.2 collective-permute-start.9
  81.9 8.6 %shard_map.105 = (bf16[4,64,512]{2,1,0:T(8,128)(2,1)S(1)}, bf16[4,64,384]{2,1,0:T(8,128)(2,1)S(1)}, bf16[4,64,1536]{2,1,0:T(8,128)(2,1)S(1)}, bf16[4,64,1024]{2,1,0:T(8,128)(2,1)S(1)}) custom-call(s32[3]{0:T(128)S(1)} %pad_add_fusion.scal.s, bf16[272,1024]{1,0:T(8,128)(2,1)S(1)} %collective-permute-done.7.refs_0_, bf16[4,1024,1536]{2,1,0:T(8,128)(2,1)} %bitcast.19, ...), custom_call_target="tpu_custom_call" | custom-call | flops 7000000000 | bytes 25165824 | tf_op jit(solution)/shard_map/pallas_call | solution.py:178
  90.5 2.9 %shard_map.108 = (bf16[2,256,1536]{2,1,0:T(8,128)(2,1)S(1)}, bf16[2,192,1024]{2,1,0:T(8,128)(2,1)S(1)}, f32[2,192,1024]{2,1,0:T(8,128)S(1)}) custom-call(s32[3]{0:T(128)S(1)} %pad_add_fusion.scal.s, bf16[4,128,512]{2,1,0:T(8,128)(2,1)S(1)} %get-tuple-element.46.refs_0_, bf16[4,192,512]{2,1,0:T(8,128)(2,1)S(1)} %get-tuple-element.49.refs_1_, ...), custom_call_target="tpu_custom_call" | custom-call | bytes 1024 | tf_op jit(solution)/shard_map/pallas_call | solution.py:228
  93.5 3.0 %shard_map.106 = (bf16[2,256,1536]{2,1,0:T(8,128)(2,1)S(1)}, bf16[2,192,1024]{2,1,0:T(8,128)(2,1)S(1)}, f32[2,192,1024]{2,1,0:T(8,128)S(1)}) custom-call(s32[3]{0:T(128)S(1)} %pad_add_fusion.scal.s, bf16[4,128,512]{2,1,0:T(8,128)(2,1)S(1)} %get-tuple-element.46.refs_0_, bf16[4,192,512]{2,1,0:T(8,128)(2,1)S(1)} %get-tuple-element.49.refs_1_, ...), custom_call_target="tpu_custom_call" | custom-call | bytes 1024 | tf_op jit(solution)/shard_map/pallas_call | solution.py:228
  96.5 0.5 collective-permute-start.12
  97.0 3.0 %shard_map.107.own_ref = f32[4,256,1536]{2,1,0:T(8,128)S(1)} custom-call(s32[3]{0:T(128)S(1)} %pad_add_fusion.scal.s, bf16[4,128,512]{2,1,0:T(8,128)(2,1)S(1)} %get-tuple-element.46.refs_0_, bf16[4,192,512]{2,1,0:T(8,128)(2,1)S(1)} %get-tuple-element.49.refs_1_, bf16[4,128,512]{2,1,0:T(8,128)(2,1)S(1)} %get-tuple-element.53.refs_2_, ...), custom_call_target="tpu_custom_call" | custom-call | bytes 1024 | tf_op jit(solution)/shard_map/pallas_call | solution.py:259
  100.0 0.2 collective-permute-start.11
  100.2 0.4 collective-permute-start.13
  100.6 0.6 select_reduce_fusion
  101.2 1.0 add_convert_fusion.2
  102.2 1.1 %collective-permute-done.11.refs_1_ = bf16[2,192,1024]{2,1,0:T(8,128)(2,1)S(1)} collective-permute-done((bf16[2,192,1024]{2,1,0:T(8,128)(2,1)S(1)}, bf16[2,192,1024]{2,1,0:T(8,128)(2,1)S(1)}, u32[]{:S(2)}, u32[]{:S(2)}) %collective-permute-start.11) | collective-permute-done | bytes 786464 | tf_op jit(solution)/shard_map/ppermute | solution.py:353
  103.3 1.1 %collective-permute-done.13.refs_4_ = bf16[2,192,1024]{2,1,0:T(8,128)(2,1)S(1)} collective-permute-done((bf16[2,192,1024]{2,1,0:T(8,128)(2,1)S(1)}, bf16[2,192,1024]{2,1,0:T(8,128)(2,1)S(1)}, u32[]{:S(2)}, u32[]{:S(2)}) %collective-permute-start.13) | collective-permute-done | bytes 786464 | tf_op jit(solution)/shard_map/ppermute | solution.py:353
  104.4 5.6 %shard_map.109 = (f32[256,4,1536]{2,1,0:T(4,128)}, f32[192,4,1024]{2,1,0:T(4,128)}) custom-call(f32[4,256,1536]{2,1,0:T(8,128)S(1)} %shard_map.107.own_ref, bf16[2,256,1536]{2,1,0:T(8,128)(2,1)S(1)} %collective-permute-done.10.refs_0_, bf16[2,192,1024]{2,1,0:T(8,128)(2,1)S(1)} %collective-permute-done.11.refs_1_, ...), custom_call_target="tpu_custom_call" | custom-call | flops 5000000000 | bytes 16777216 | tf_op jit(solution)/shard_map/pallas_call | solution.py:291
  (18 shorter events, 0.1 us)
Async XLA Ops:
  2.6 17.9 %collective-permute-start = (bf16[272,1024]{1,0:T(8,128)(2,1)}, bf16[272,1024]{1,0:T(8,128)(2,1)S(1)}, u32[]{:S(2)}, u32[]{:S(2)}) collective-permute-start(bf16[272,1024]{1,0:T(8,128)(2,1)} %shard_map.101.refs_1_), channel_id=1, source_target_pairs={{0,4},{4,8},{8,12},{12,0},{1,5},{5,9},{9,13},{13,1},{2,6},{6,10},{... | collective-permute-start | bytes 1671176 | tf_op jit(solution)/shard_map/ppermute | solution.py:316
  5.7 14.9 %collective-permute-start.1 = (bf16[272,1024]{1,0:T(8,128)(2,1)}, bf16[272,1024]{1,0:T(8,128)(2,1)S(1)}, u32[]{:S(2)}, u32[]{:S(2)}) collective-permute-start(bf16[272,1024]{1,0:T(8,128)(2,1)} %shard_map.101.refs_1_), channel_id=1, source_target_pairs={{0,2},{1,3},{2,0},{3,1},{4,6},{5,7},{6,4},{7,5},{8,10},{9,11},{10,... | collective-permute-start | bytes 1671176 | tf_op jit(solution)/shard_map/ppermute | solution.py:314
  20.5 20.5 %collective-permute-start.2 = (bf16[272,1024]{1,0:T(8,128)(2,1)S(1)}, bf16[272,1024]{1,0:T(8,128)(2,1)S(1)}, u32[]{:S(2)}, u32[]{:S(2)}) collective-permute-start(bf16[272,1024]{1,0:T(8,128)(2,1)S(1)} %collective-permute-done.refs_0_), channel_id=1, source_target_pairs={{0,4},{4,8},{8,12},{12,0},{1,5},{5,9},{9,13},{13,1},{2,6},{6,10},{... | collective-permute-start | bytes 1671176 | tf_op jit(solution)/shard_map/ppermute | solution.py:316
  21.5 22.0 %collective-permute-start.3 = (bf16[272,1024]{1,0:T(8,128)(2,1)S(1)}, bf16[272,1024]{1,0:T(8,128)(2,1)S(1)}, u32[]{:S(2)}, u32[]{:S(2)}) collective-permute-start(bf16[272,1024]{1,0:T(8,128)(2,1)S(1)} %collective-permute-done.refs_0_), channel_id=1, source_target_pairs={{0,2},{1,3},{2,0},{3,1},{4,6},{5,7},{6,4},{7,5},{8,10},{9,11},{10,... | collective-permute-start | bytes 1671176 | tf_op jit(solution)/shard_map/ppermute | solution.py:314
  27.9 15.6 %copy-start = (bf16[272,1024]{1,0:T(8,128)(2,1)S(1)}, bf16[272,1024]{1,0:T(8,128)(2,1)}, u32[]{:S(2)}) copy-start(bf16[272,1024]{1,0:T(8,128)(2,1)} %shard_map.101.refs_1_) | copy-start | bytes 1671172
  41.1 17.5 %collective-permute-start.6 = (bf16[272,1024]{1,0:T(8,128)(2,1)S(1)}, bf16[272,1024]{1,0:T(8,128)(2,1)S(1)}, u32[]{:S(2)}, u32[]{:S(2)}) collective-permute-start(bf16[272,1024]{1,0:T(8,128)(2,1)S(1)} %get-tuple-element.51.refs_6_), channel_id=1, source_target_pairs={{0,4},{4,8},{8,12},{12,0},{1,5},{5,9},{9,13},{13,1},{2,6},{6,10},{... | collective-permute-start | bytes 1671176 | tf_op jit(solution)/shard_map/ppermute | solution.py:339
  42.7 24.8 %collective-permute-start.4 = (bf16[272,1024]{1,0:T(8,128)(2,1)S(1)}, bf16[272,1024]{1,0:T(8,128)(2,1)S(1)}, u32[]{:S(2)}, u32[]{:S(2)}) collective-permute-start(bf16[272,1024]{1,0:T(8,128)(2,1)S(1)} %collective-permute-done.2.refs_0_), channel_id=1, source_target_pairs={{0,4},{4,8},{8,12},{12,0},{1,5},{5,9},{9,13},{13,1},{2,6},{6,10},{... | collective-permute-start | bytes 1671176 | tf_op jit(solution)/shard_map/ppermute | solution.py:316
  43.0 25.4 %collective-permute-start.5 = (bf16[272,1024]{1,0:T(8,128)(2,1)S(1)}, bf16[272,1024]{1,0:T(8,128)(2,1)S(1)}, u32[]{:S(2)}, u32[]{:S(2)}) collective-permute-start(bf16[272,1024]{1,0:T(8,128)(2,1)S(1)} %collective-permute-done.2.refs_0_), channel_id=1, source_target_pairs={{0,2},{1,3},{2,0},{3,1},{4,6},{5,7},{6,4},{7,5},{8,10},{9,11},{10,... | collective-permute-start | bytes 1671176 | tf_op jit(solution)/shard_map/ppermute | solution.py:314
  67.5 14.1 %collective-permute-start.8 = (bf16[272,1024]{1,0:T(8,128)(2,1)S(1)}, bf16[272,1024]{1,0:T(8,128)(2,1)S(1)}, u32[]{:S(2)}, u32[]{:S(2)}) collective-permute-start(bf16[272,1024]{1,0:T(8,128)(2,1)S(1)} %add_convert_fusion.1.refs_5_), channel_id=1, source_target_pairs={{0,4},{4,8},{8,12},{12,0},{1,5},{5,9},{9,13},{13,1},{2,6},{6,10},{... | collective-permute-start | bytes 1671176 | tf_op jit(solution)/shard_map/ppermute | solution.py:339
  67.5 14.5 %collective-permute-start.7 = (bf16[272,1024]{1,0:T(8,128)(2,1)S(1)}, bf16[272,1024]{1,0:T(8,128)(2,1)S(1)}, u32[]{:S(2)}, u32[]{:S(2)}) collective-permute-start(bf16[272,1024]{1,0:T(8,128)(2,1)S(1)} %collective-permute-done.4.refs_0_), channel_id=1, source_target_pairs={{0,2},{1,3},{2,0},{3,1},{4,6},{5,7},{6,4},{7,5},{8,10},{9,11},{10,... | collective-permute-start | bytes 1671176 | tf_op jit(solution)/shard_map/ppermute | solution.py:314
  81.7 14.8 %collective-permute-start.9 = (bf16[272,1024]{1,0:T(8,128)(2,1)S(1)}, bf16[272,1024]{1,0:T(8,128)(2,1)S(1)}, u32[]{:S(2)}, u32[]{:S(2)}) collective-permute-start(bf16[272,1024]{1,0:T(8,128)(2,1)S(1)} %add_convert_fusion.refs_4_), channel_id=1, source_target_pairs={{0,4},{4,8},{8,12},{12,0},{1,5},{5,9},{9,13},{13,1},{2,6},{6,10},{... | collective-permute-start | bytes 1671176 | tf_op jit(solution)/shard_map/ppermute | solution.py:344
  96.4 8.0 %collective-permute-start.10 = (bf16[2,256,1536]{2,1,0:T(8,128)(2,1)S(1)}, bf16[2,256,1536]{2,1,0:T(8,128)(2,1)S(1)}, u32[]{:S(2)}, u32[]{:S(2)}) collective-permute-start(bf16[2,256,1536]{2,1,0:T(8,128)(2,1)S(1)} %get-tuple-element.71), channel_id=1, source_target_pairs={{0,1},{1,0},{2,3},{3,2},{4,5},{5,4},{6,7},{7,6},{8,9},{9,8},{10,11... | collective-permute-start | bytes 4718600 | tf_op jit(solution)/shard_map/ppermute | solution.py:352
  96.5 4.0 %copy-start.1 = (s32[128,6]{0,1:T(8,128)S(1)}, s32[128,6]{0,1:T(8,128)}, u32[]{:S(2)}) copy-start(s32[128,6]{0,1:T(8,128)} %param.7) | copy-start | bytes 9220
  96.5 7.9 %collective-permute-start.12 = (bf16[2,256,1536]{2,1,0:T(8,128)(2,1)S(1)}, bf16[2,256,1536]{2,1,0:T(8,128)(2,1)S(1)}, u32[]{:S(2)}, u32[]{:S(2)}) collective-permute-start(bf16[2,256,1536]{2,1,0:T(8,128)(2,1)S(1)} %get-tuple-element.74.refs_8_), channel_id=1, source_target_pairs={{0,1},{1,0},{2,3},{3,2},{4,5},{5,4},{6,7},{7,6},{8,9},{9,8},{10,11... | collective-permute-start | bytes 4718600 | tf_op jit(solution)/shard_map/ppermute | solution.py:352
  100.0 3.3 %collective-permute-start.11 = (bf16[2,192,1024]{2,1,0:T(8,128)(2,1)S(1)}, bf16[2,192,1024]{2,1,0:T(8,128)(2,1)S(1)}, u32[]{:S(2)}, u32[]{:S(2)}) collective-permute-start(bf16[2,192,1024]{2,1,0:T(8,128)(2,1)S(1)} %get-tuple-element.72), channel_id=1, source_target_pairs={{0,1},{1,0},{2,3},{3,2},{4,5},{5,4},{6,7},{7,6},{8,9},{9,8},{10,11... | collective-permute-start | bytes 2359304 | tf_op jit(solution)/shard_map/ppermute | solution.py:353
  100.2 4.2 %collective-permute-start.13 = (bf16[2,192,1024]{2,1,0:T(8,128)(2,1)S(1)}, bf16[2,192,1024]{2,1,0:T(8,128)(2,1)S(1)}, u32[]{:S(2)}, u32[]{:S(2)}) collective-permute-start(bf16[2,192,1024]{2,1,0:T(8,128)(2,1)S(1)} %get-tuple-element.75.refs_9_), channel_id=1, source_target_pairs={{0,1},{1,0},{2,3},{3,2},{4,5},{5,4},{6,7},{7,6},{8,9},{9,8},{10,11... | collective-permute-start | bytes 2359304 | tf_op jit(solution)/shard_map/ppermute | solution.py:353

commit v5 on v4

--- a/solution.py
+++ b/solution.py
@@ -97,11 +97,28 @@
     refs = refs[m + 2 + after :]
     x_ref, h_ref, pg_ref, gs_ref = refs[:4]
     sums, refs = refs[4 : 4 + own], refs[4 + own :]
-    xs, hs = refs[:2]
+    xs, hs, gu_s, d_s, sem = refs[:5]
     if own:
-        hit_s, wt_s, cs, o_s, dx_s, dots_s = refs[2:]
+        hit_s, wt_s, cs, o_s, dx_s, dots_s = refs[5:]
     e = pl.program_id(0)
     here = pl.ds(pl.multiple_of(e * CAP, CAP), CAP)
+
+    def fetch(k):
+        slot = lax.rem(k, 2)
+        return (
+            pltpu.make_async_copy(wgu.at[k], gu_s.at[slot], sem.at[0, slot]),
+            pltpu.make_async_copy(wd.at[k], d_s.at[slot], sem.at[1, slot]),
+        )
+
+    @pl.when(e == 0)
+    def _():
+        for copy in fetch(e):
+            copy.start()
+
+    @pl.when(e + 1 < local)
+    def _():
+        for copy in fetch(e + 1):
+            copy.start()
 
     @pl.when(e == 0)
     def _():
@@ -121,17 +138,20 @@
 
     half_d, half_f = x_ref.shape[-1], h_ref.shape[-1]
     x_ref[0] = xs[e, :, pl.ds(pl.multiple_of(scal[1] * half_d, half_d), half_d)]
-    pre = mm(xs[e], wgu[0])
+    for copy in fetch(e):
+        copy.wait()
+    slot = lax.rem(e, 2)
+    pre = mm(xs[e], gu_s[slot])
     middle = pre.shape[-1] // 2
     hidden = (jax.nn.silu(pre[:, :middle]) * pre[:, middle:]).astype(BF)
     hs[...] = hidden
     h_ref[0] = hs[:, pl.ds(pl.multiple_of(scal[1] * half_f, half_f), half_f)]
-    pg = act_gradient(pre, mm_t1(gs_ref[e], wd[0]))
+    pg = act_gradient(pre, mm_t1(gs_ref[e], d_s[slot]))
     pg_ref[0] = pg
     if own:
-        out = mm(hidden[: own * CAP], wd[0]).astype(BF)
+        out = mm(hidden[: own * CAP], d_s[slot]).astype(BF)
         dots = jnp.sum(cs[e].astype(F32) * out.astype(F32), axis=1, keepdims=True)
-        dx = mm_t1(pg[: own * CAP], wgu[0]).astype(BF)
+        dx = mm_t1(pg[: own * CAP], gu_s[slot]).astype(BF)
         for d in range(own):
             part = slice(d * CAP, (d + 1) * CAP)
             o_s[d, here, :] = out[part]
@@ -165,7 +185,13 @@
         (jax.ShapeDtypeStruct((local, rows, width), BF), full((local, rows, width))),
     ]
     outs += [(jax.ShapeDtypeStruct(a.shape, BF), full(a.shape)) for a in mine]
-    scratch = [pltpu.VMEM((local, rows, width), BF), pltpu.VMEM((rows, ff), BF)]
+    scratch = [
+        pltpu.VMEM((local, rows, width), BF),
+        pltpu.VMEM((rows, ff), BF),
+        pltpu.VMEM((2,) + wgu.shape[1:], BF),
+        pltpu.VMEM((2,) + wd.shape[1:], BF),
+        pltpu.SemaphoreType.DMA((2, 2)),
+    ]
     if own:
         scratch += [
             pltpu.VMEM((own, local * CAP, count), BF),
@@ -181,8 +207,7 @@
             num_scalar_prefetch=1,
             grid=(local,),
             in_specs=[full(a.shape) for a in pays]
-            + [per_expert(wgu.shape), per_expert(wd.shape)]
-            + [pl.BlockSpec(memory_space=pl.ANY)] * len(after),
+            + [pl.BlockSpec(memory_space=pl.ANY)] * (2 + len(after)),
             out_specs=[o[1] for o in outs],
             scratch_shapes=scratch,
         ),

time: 111 us -> 109 us (0.982)
  Pallas kernels: 66.4 us -> 63.2 us
  waiting for transfers between devices: 11.8 us -> 13.1 us
    pallas_call x4, Pallas kernels: 49.9 us -> 46.7 us  [stage(): pl.pallas_call(functools.partial(stage_kernel, m, own, local, count, len(...]
    ppermute x2, waiting for transfers between devices: 0.01 us -> 1.26 us  [on_device(): totals.append(add(lax.ppermute(send, 'expert', ring), sums[d]))]
  transfers between devices with their start and end apart: 14 -> 14, of which waited for: 4 -> 6; matrix products, arithmetic and copies ran while one was open for 18% -> 18% of each run, Pallas kernels for 53% -> 51%
where the time goes in v5:
time: 109 us; the launch traced here: 108 us
  Pallas kernels  63.2 us (58%)
  local copies, waits for them, and re-layouts  17.4 us (16%)
  waiting for transfers between devices  13.1 us (12%)
  starting transfers between devices  11.6 us (11%)
  other arithmetic  2.09 us (2%)
    pallas_call x4, Pallas kernels, stage(): pl.pallas_call(functools.partial(stage_kernel, m, own, local, count, len(...  46.7 us
    unnamed x5, local copies, waits for them, and re-layouts  12.5 us
    ppermute x3, waiting for transfers between devices, on_device(): pays.append(lax.ppermute(pays[d], 'expert', ring))  9.62 us
    pallas_call x2, Pallas kernels, send_blocks(): pl.pallas_call(lambda s, *refs: body(s, *refs[k:]), grid_spec=pltpu.Prefe...  5.9 us
    pallas_call x1, Pallas kernels, join_blocks(): pl.pallas_call(functools.partial(join_kernel, len(pieces), low), grid=(st...  5.63 us
    optimization_barrier x1, local copies, waits for them, and re-layouts, on_device(): lax.optimization_barrier((pays[1], others[0], wgu, down_weights))  4.89 us
    ppermute x4, starting transfers between devices, on_device(): others.append(lax.ppermute(pays[d], 'replica', across))  4.47 us
    ppermute x3, starting transfers between devices, on_device(): pays.append(lax.ppermute(pays[d], 'expert', ring))  4.32 us
  transfers between devices with their start and end apart: 14, of which 6 were waited for; matrix products, arithmetic and copies ran while one was open for 18% of the time, Pallas kernels for 51%

profile of v5, /device:TPU:0, one launch (start us, length us, event | category | flops | bytes accessed | tf_op | source)
XLA Modules:
  0.0 108.2 jit_solution(6301372477383796976)
XLA Ops:
  0.6 2.0 %shard_map.101.refs_1_ = bf16[272,1024]{1,0:T(8,128)(2,1)} custom-call(s32[6,128]{1,0:T(8,128)} %bitcast.20, bf16[6,128]{1,0:T(8,128)(2,1)} %bitcast.23, bf16[128,1024]{1,0:T(8,128)(2,1)} %tok_ref.1, bf16[128,1024]{1,0:T(8,128)(2,1)} %cot_ref.1), custom_call_target="tpu_custom_call" | custom-call | tf_op jit(solution)/shard_map/pallas_call | solution.py:63
  2.6 3.0 %collective-permute-start = (bf16[272,1024]{1,0:T(8,128)(2,1)}, bf16[272,1024]{1,0:T(8,128)(2,1)S(1)}, u32[]{:S(2)}, u32[]{:S(2)}) collective-permute-start(bf16[272,1024]{1,0:T(8,128)(2,1)} %shard_map.101.refs_1_), channel_id=1, source_target_pairs={{0,4},{4,8},{8,12},{12,0},{1,5},{5,9},{9,13},{13,1},{2,6},{6,10},{... | collective-permute-start | bytes 1671176 | tf_op jit(solution)/shard_map/ppermute | solution.py:341
  5.7 1.5 %collective-permute-start.1 = (bf16[272,1024]{1,0:T(8,128)(2,1)}, bf16[272,1024]{1,0:T(8,128)(2,1)S(1)}, u32[]{:S(2)}, u32[]{:S(2)}) collective-permute-start(bf16[272,1024]{1,0:T(8,128)(2,1)} %shard_map.101.refs_1_), channel_id=1, source_target_pairs={{0,2},{1,3},{2,0},{3,1},{4,6},{5,7},{6,4},{7,5},{8,10},{9,11},{10,... | collective-permute-start | bytes 1671176 | tf_op jit(solution)/shard_map/ppermute | solution.py:339
  7.2 12.5 %copy.17 = bf16[1024,4,1536]{2,0,1:T(8,128)(2,1)} copy(bf16[1024,4,1536]{2,1,0:T(4,128)(2,1)} %param.10) | data formatting | bytes 25165824 | tf_op args[4]
  19.7 0.8 collective-permute-done.refs_0_
  20.5 1.0 collective-permute-start.2
  21.5 1.5 %collective-permute-start.3 = (bf16[272,1024]{1,0:T(8,128)(2,1)S(1)}, bf16[272,1024]{1,0:T(8,128)(2,1)S(1)}, u32[]{:S(2)}, u32[]{:S(2)}) collective-permute-start(bf16[272,1024]{1,0:T(8,128)(2,1)S(1)} %collective-permute-done.refs_0_), channel_id=1, source_target_pairs={{0,2},{1,3},{2,0},{3,1},{4,6},{5,7},{6,4},{7,5},{8,10},{9,11},{10,... | collective-permute-start | bytes 1671176 | tf_op jit(solution)/shard_map/ppermute | solution.py:339
  23.0 4.9 %copy.18 = bf16[768,4,1024]{2,0,1:T(8,128)(2,1)S(1)} copy(bf16[768,4,1024]{2,1,0:T(4,128)(2,1)} %param.11) | data formatting | bytes 12582912 | tf_op jit(solution)/shard_map/optimization_barrier | solution.py:343
  27.9 12.3 %shard_map.102 = (bf16[4,128,512]{2,1,0:T(8,128)(2,1)S(1)}, bf16[4,128,384]{2,1,0:T(8,128)(2,1)S(1)}, bf16[4,128,1536]{2,1,0:T(8,128)(2,1)S(1)}, bf16[4,128,1024]{2,1,0:T(8,128)(2,1)S(1)}, bf16[272,1024]{1,0:T(8,128)(2,1)S(1)}) custom-call(s32[3]{0:T(128)S(1)} %pad_add_fusion.scal.s, bf16[272,1024]{1,0:T(8,128)(2,1)S(1)} %collective-permute-done.refs_0_, ...), custom_call_target="tpu_custom_call" | custom-call | flops 14000000000 | bytes 25165824 | tf_op jit(solution)/shard_map/pallas_call | solution.py:204
  40.3 1.6 %collective-permute-start.6 = (bf16[272,1024]{1,0:T(8,128)(2,1)S(1)}, bf16[272,1024]{1,0:T(8,128)(2,1)S(1)}, u32[]{:S(2)}, u32[]{:S(2)}) collective-permute-start(bf16[272,1024]{1,0:T(8,128)(2,1)S(1)} %get-tuple-element.51.refs_6_), channel_id=1, source_target_pairs={{0,4},{4,8},{8,12},{12,0},{1,5},{5,9},{9,13},{13,1},{2,6},{6,10},{... | collective-permute-start | bytes 1671176 | tf_op jit(solution)/shard_map/ppermute | solution.py:364
  41.9 0.3 collective-permute-start.4
  42.2 0.5 collective-permute-start.5
  42.7 13.9 %shard_map.103 = (bf16[4,192,512]{2,1,0:T(8,128)(2,1)S(1)}, bf16[4,192,384]{2,1,0:T(8,128)(2,1)S(1)}, bf16[4,192,1536]{2,1,0:T(8,128)(2,1)S(1)}, bf16[4,192,1024...) custom-call(s32[3]{0:T(128)S(1)} %pad_add_fusion.scal.s, ...), custom_call_target="tpu_custom_call" | custom-call | flops 14000000000 | bytes 25165824 | tf_op jit(solution)/shard_map/pallas_call | solution.py:204
  56.6 1.1 collective-permute-done.6
  57.7 0.2 add_convert_fusion.1.refs_5_
  57.9 8.8 %collective-permute-done.4.refs_0_ = bf16[272,1024]{1,0:T(8,128)(2,1)S(1)} collective-permute-done((bf16[272,1024]{1,0:T(8,128)(2,1)S(1)}, bf16[272,1024]{1,0:T(8,128)(2,1)S(1)}, u32[]{:S(2)}, u32[]{:S(2)}) %collective-permute-start.4) | collective-permute-done | bytes 557088 | tf_op jit(solution)/shard_map/ppermute | solution.py:341
  66.7 0.9 collective-permute-start.7
  67.6 12.3 %shard_map.104 = (bf16[4,128,512]{2,1,0:T(8,128)(2,1)S(1)}, bf16[4,128,384]{2,1,0:T(8,128)(2,1)S(1)}, bf16[4,128,1536]{2,1,0:T(8,128)(2,1)S(1)}, bf16[4,128,1024]{2,1,0:T(8,128)(2,1)S(1)}, bf16[272,1024]{1,0:T(8,128)(2,1)S(1)}) custom-call(s32[3]{0:T(128)S(1)} %pad_add_fusion.scal.s, bf16[272,1024]{1,0:T(8,128)(2,1)S(1)} %collective-permute-done.4.refs_0_, ...), custom_call_target="tpu_custom_call" | custom-call | flops 14000000000 | bytes 25165824 | tf_op jit(solution)/shard_map/pallas_call | solution.py:204
  80.0 0.2 collective-permute-done.8
  80.2 0.2 add_convert_fusion.refs_4_
  80.5 8.2 %shard_map.105 = (bf16[4,64,512]{2,1,0:T(8,128)(2,1)S(1)}, bf16[4,64,384]{2,1,0:T(8,128)(2,1)S(1)}, bf16[4,64,1536]{2,1,0:T(8,128)(2,1)S(1)}, bf16[4,64,1024]{2,1,0:T(8,128)(2,1)S(1)}) custom-call(s32[3]{0:T(128)S(1)} %pad_add_fusion.scal.s, bf16[272,1024]{1,0:T(8,128)(2,1)S(1)} %collective-permute-done.7.refs_0_, bf16[4,1024,1536]{2,1,0:T(8,128)(2,1)} %bitcast.19, ...), custom_call_target="tpu_custom_call" | custom-call | flops 7000000000 | bytes 25165824 | tf_op jit(solution)/shard_map/pallas_call | solution.py:204
  88.7 2.9 %shard_map.108 = (bf16[2,256,1536]{2,1,0:T(8,128)(2,1)S(1)}, bf16[2,192,1024]{2,1,0:T(8,128)(2,1)S(1)}, f32[2,192,1024]{2,1,0:T(8,128)S(1)}) custom-call(s32[3]{0:T(128)S(1)} %pad_add_fusion.scal.s, bf16[4,128,512]{2,1,0:T(8,128)(2,1)S(1)} %get-tuple-element.46.refs_0_, bf16[4,192,512]{2,1,0:T(8,128)(2,1)S(1)} %get-tuple-element.49.refs_1_, ...), custom_call_target="tpu_custom_call" | custom-call | bytes 1024 | tf_op jit(solution)/shard_map/pallas_call | solution.py:253
  91.6 3.0 %shard_map.106 = (bf16[2,256,1536]{2,1,0:T(8,128)(2,1)S(1)}, bf16[2,192,1024]{2,1,0:T(8,128)(2,1)S(1)}, f32[2,192,1024]{2,1,0:T(8,128)S(1)}) custom-call(s32[3]{0:T(128)S(1)} %pad_add_fusion.scal.s, bf16[4,128,512]{2,1,0:T(8,128)(2,1)S(1)} %get-tuple-element.46.refs_0_, bf16[4,192,512]{2,1,0:T(8,128)(2,1)S(1)} %get-tuple-element.49.refs_1_, ...), custom_call_target="tpu_custom_call" | custom-call | bytes 1024 | tf_op jit(solution)/shard_map/pallas_call | solution.py:253
  94.7 0.5 collective-permute-start.12
  95.2 3.0 %shard_map.107.own_ref = f32[4,256,1536]{2,1,0:T(8,128)S(1)} custom-call(s32[3]{0:T(128)S(1)} %pad_add_fusion.scal.s, bf16[4,128,512]{2,1,0:T(8,128)(2,1)S(1)} %get-tuple-element.46.refs_0_, bf16[4,192,512]{2,1,0:T(8,128)(2,1)S(1)} %get-tuple-element.49.refs_1_, bf16[4,128,512]{2,1,0:T(8,128)(2,1)S(1)} %get-tuple-element.53.refs_2_, ...), custom_call_target="tpu_custom_call" | custom-call | bytes 1024 | tf_op jit(solution)/shard_map/pallas_call | solution.py:284
  98.1 0.2 collective-permute-start.11
  98.3 0.4 collective-permute-start.13
  98.7 0.6 select_reduce_fusion
  99.3 1.0 add_convert_fusion.2
  100.3 1.1 %collective-permute-done.11.refs_1_ = bf16[2,192,1024]{2,1,0:T(8,128)(2,1)S(1)} collective-permute-done((bf16[2,192,1024]{2,1,0:T(8,128)(2,1)S(1)}, bf16[2,192,1024]{2,1,0:T(8,128)(2,1)S(1)}, u32[]{:S(2)}, u32[]{:S(2)}) %collective-permute-start.11) | collective-permute-done | bytes 786464 | tf_op jit(solution)/shard_map/ppermute | solution.py:378
  101.4 1.1 %collective-permute-done.13.refs_4_ = bf16[2,192,1024]{2,1,0:T(8,128)(2,1)S(1)} collective-permute-done((bf16[2,192,1024]{2,1,0:T(8,128)(2,1)S(1)}, bf16[2,192,1024]{2,1,0:T(8,128)(2,1)S(1)}, u32[]{:S(2)}, u32[]{:S(2)}) %collective-permute-start.13) | collective-permute-done | bytes 786464 | tf_op jit(solution)/shard_map/ppermute | solution.py:378
  102.6 5.6 %shard_map.109 = (f32[256,4,1536]{2,1,0:T(4,128)}, f32[192,4,1024]{2,1,0:T(4,128)}) custom-call(f32[4,256,1536]{2,1,0:T(8,128)S(1)} %shard_map.107.own_ref, bf16[2,256,1536]{2,1,0:T(8,128)(2,1)S(1)} %collective-permute-done.10.refs_0_, bf16[2,192,1024]{2,1,0:T(8,128)(2,1)S(1)} %collective-permute-done.11.refs_1_, ...), custom_call_target="tpu_custom_call" | custom-call | flops 5000000000 | bytes 16777216 | tf_op jit(solution)/shard_map/pallas_call | solution.py:316
  (18 shorter events, 0.3 us)
Async XLA Ops:
  2.6 17.9 %collective-permute-start = (bf16[272,1024]{1,0:T(8,128)(2,1)}, bf16[272,1024]{1,0:T(8,128)(2,1)S(1)}, u32[]{:S(2)}, u32[]{:S(2)}) collective-permute-start(bf16[272,1024]{1,0:T(8,128)(2,1)} %shard_map.101.refs_1_), channel_id=1, source_target_pairs={{0,4},{4,8},{8,12},{12,0},{1,5},{5,9},{9,13},{13,1},{2,6},{6,10},{... | collective-permute-start | bytes 1671176 | tf_op jit(solution)/shard_map/ppermute | solution.py:341
  5.7 14.9 %collective-permute-start.1 = (bf16[272,1024]{1,0:T(8,128)(2,1)}, bf16[272,1024]{1,0:T(8,128)(2,1)S(1)}, u32[]{:S(2)}, u32[]{:S(2)}) collective-permute-start(bf16[272,1024]{1,0:T(8,128)(2,1)} %shard_map.101.refs_1_), channel_id=1, source_target_pairs={{0,2},{1,3},{2,0},{3,1},{4,6},{5,7},{6,4},{7,5},{8,10},{9,11},{10,... | collective-permute-start | bytes 1671176 | tf_op jit(solution)/shard_map/ppermute | solution.py:339
  20.5 19.8 %collective-permute-start.2 = (bf16[272,1024]{1,0:T(8,128)(2,1)S(1)}, bf16[272,1024]{1,0:T(8,128)(2,1)S(1)}, u32[]{:S(2)}, u32[]{:S(2)}) collective-permute-start(bf16[272,1024]{1,0:T(8,128)(2,1)S(1)} %collective-permute-done.refs_0_), channel_id=1, source_target_pairs={{0,4},{4,8},{8,12},{12,0},{1,5},{5,9},{9,13},{13,1},{2,6},{6,10},{... | collective-permute-start | bytes 1671176 | tf_op jit(solution)/shard_map/ppermute | solution.py:341
  21.5 21.2 %collective-permute-start.3 = (bf16[272,1024]{1,0:T(8,128)(2,1)S(1)}, bf16[272,1024]{1,0:T(8,128)(2,1)S(1)}, u32[]{:S(2)}, u32[]{:S(2)}) collective-permute-start(bf16[272,1024]{1,0:T(8,128)(2,1)S(1)} %collective-permute-done.refs_0_), channel_id=1, source_target_pairs={{0,2},{1,3},{2,0},{3,1},{4,6},{5,7},{6,4},{7,5},{8,10},{9,11},{10,... | collective-permute-start | bytes 1671176 | tf_op jit(solution)/shard_map/ppermute | solution.py:339
  27.9 14.8 %copy-start = (bf16[272,1024]{1,0:T(8,128)(2,1)S(1)}, bf16[272,1024]{1,0:T(8,128)(2,1)}, u32[]{:S(2)}) copy-start(bf16[272,1024]{1,0:T(8,128)(2,1)} %shard_map.101.refs_1_) | copy-start | bytes 1671172
  40.3 17.4 %collective-permute-start.6 = (bf16[272,1024]{1,0:T(8,128)(2,1)S(1)}, bf16[272,1024]{1,0:T(8,128)(2,1)S(1)}, u32[]{:S(2)}, u32[]{:S(2)}) collective-permute-start(bf16[272,1024]{1,0:T(8,128)(2,1)S(1)} %get-tuple-element.51.refs_6_), channel_id=1, source_target_pairs={{0,4},{4,8},{8,12},{12,0},{1,5},{5,9},{9,13},{13,1},{2,6},{6,10},{... | collective-permute-start | bytes 1671176 | tf_op jit(solution)/shard_map/ppermute | solution.py:364
  41.9 24.8 %collective-permute-start.4 = (bf16[272,1024]{1,0:T(8,128)(2,1)S(1)}, bf16[272,1024]{1,0:T(8,128)(2,1)S(1)}, u32[]{:S(2)}, u32[]{:S(2)}) collective-permute-start(bf16[272,1024]{1,0:T(8,128)(2,1)S(1)} %collective-permute-done.2.refs_0_), channel_id=1, source_target_pairs={{0,4},{4,8},{8,12},{12,0},{1,5},{5,9},{9,13},{13,1},{2,6},{6,10},{... | collective-permute-start | bytes 1671176 | tf_op jit(solution)/shard_map/ppermute | solution.py:341
  42.2 25.4 %collective-permute-start.5 = (bf16[272,1024]{1,0:T(8,128)(2,1)S(1)}, bf16[272,1024]{1,0:T(8,128)(2,1)S(1)}, u32[]{:S(2)}, u32[]{:S(2)}) collective-permute-start(bf16[272,1024]{1,0:T(8,128)(2,1)S(1)} %collective-permute-done.2.refs_0_), channel_id=1, source_target_pairs={{0,2},{1,3},{2,0},{3,1},{4,6},{5,7},{6,4},{7,5},{8,10},{9,11},{10,... | collective-permute-start | bytes 1671176 | tf_op jit(solution)/shard_map/ppermute | solution.py:339
  66.7 13.5 %collective-permute-start.8 = (bf16[272,1024]{1,0:T(8,128)(2,1)S(1)}, bf16[272,1024]{1,0:T(8,128)(2,1)S(1)}, u32[]{:S(2)}, u32[]{:S(2)}) collective-permute-start(bf16[272,1024]{1,0:T(8,128)(2,1)S(1)} %add_convert_fusion.1.refs_5_), channel_id=1, source_target_pairs={{0,4},{4,8},{8,12},{12,0},{1,5},{5,9},{9,13},{13,1},{2,6},{6,10},{... | collective-permute-start | bytes 1671176 | tf_op jit(solution)/shard_map/ppermute | solution.py:364
  66.7 13.8 %collective-permute-start.7 = (bf16[272,1024]{1,0:T(8,128)(2,1)S(1)}, bf16[272,1024]{1,0:T(8,128)(2,1)S(1)}, u32[]{:S(2)}, u32[]{:S(2)}) collective-permute-start(bf16[272,1024]{1,0:T(8,128)(2,1)S(1)} %collective-permute-done.4.refs_0_), channel_id=1, source_target_pairs={{0,2},{1,3},{2,0},{3,1},{4,6},{5,7},{6,4},{7,5},{8,10},{9,11},{10,... | collective-permute-start | bytes 1671176 | tf_op jit(solution)/shard_map/ppermute | solution.py:339
  80.4 14.3 %collective-permute-start.9 = (bf16[272,1024]{1,0:T(8,128)(2,1)S(1)}, bf16[272,1024]{1,0:T(8,128)(2,1)S(1)}, u32[]{:S(2)}, u32[]{:S(2)}) collective-permute-start(bf16[272,1024]{1,0:T(8,128)(2,1)S(1)} %add_convert_fusion.refs_4_), channel_id=1, source_target_pairs={{0,4},{4,8},{8,12},{12,0},{1,5},{5,9},{9,13},{13,1},{2,6},{6,10},{... | collective-permute-start | bytes 1671176 | tf_op jit(solution)/shard_map/ppermute | solution.py:369
  94.6 8.0 %collective-permute-start.10 = (bf16[2,256,1536]{2,1,0:T(8,128)(2,1)S(1)}, bf16[2,256,1536]{2,1,0:T(8,128)(2,1)S(1)}, u32[]{:S(2)}, u32[]{:S(2)}) collective-permute-start(bf16[2,256,1536]{2,1,0:T(8,128)(2,1)S(1)} %get-tuple-element.71), channel_id=1, source_target_pairs={{0,1},{1,0},{2,3},{3,2},{4,5},{5,4},{6,7},{7,6},{8,9},{9,8},{10,11... | collective-permute-start | bytes 4718600 | tf_op jit(solution)/shard_map/ppermute | solution.py:377
  94.7 4.0 %copy-start.1 = (s32[128,6]{0,1:T(8,128)S(1)}, s32[128,6]{0,1:T(8,128)}, u32[]{:S(2)}) copy-start(s32[128,6]{0,1:T(8,128)} %param.7) | copy-start | bytes 9220
  94.7 7.9 %collective-permute-start.12 = (bf16[2,256,1536]{2,1,0:T(8,128)(2,1)S(1)}, bf16[2,256,1536]{2,1,0:T(8,128)(2,1)S(1)}, u32[]{:S(2)}, u32[]{:S(2)}) collective-permute-start(bf16[2,256,1536]{2,1,0:T(8,128)(2,1)S(1)} %get-tuple-element.74.refs_8_), channel_id=1, source_target_pairs={{0,1},{1,0},{2,3},{3,2},{4,5},{5,4},{6,7},{7,6},{8,9},{9,8},{10,11... | collective-permute-start | bytes 4718600 | tf_op jit(solution)/shard_map/ppermute | solution.py:377
  98.1 3.3 %collective-permute-start.11 = (bf16[2,192,1024]{2,1,0:T(8,128)(2,1)S(1)}, bf16[2,192,1024]{2,1,0:T(8,128)(2,1)S(1)}, u32[]{:S(2)}, u32[]{:S(2)}) collective-permute-start(bf16[2,192,1024]{2,1,0:T(8,128)(2,1)S(1)} %get-tuple-element.72), channel_id=1, source_target_pairs={{0,1},{1,0},{2,3},{3,2},{4,5},{5,4},{6,7},{7,6},{8,9},{9,8},{10,11... | collective-permute-start | bytes 2359304 | tf_op jit(solution)/shard_map/ppermute | solution.py:378
  98.3 4.2 %collective-permute-start.13 = (bf16[2,192,1024]{2,1,0:T(8,128)(2,1)S(1)}, bf16[2,192,1024]{2,1,0:T(8,128)(2,1)S(1)}, u32[]{:S(2)}, u32[]{:S(2)}) collective-permute-start(bf16[2,192,1024]{2,1,0:T(8,128)(2,1)S(1)} %get-tuple-element.75.refs_9_), channel_id=1, source_target_pairs={{0,1},{1,0},{2,3},{3,2},{4,5},{5,4},{6,7},{7,6},{8,9},{9,8},{10,11... | collective-permute-start | bytes 2359304 | tf_op jit(solution)/shard_map/ppermute | solution.py:378

commit v6 on v5

--- a/solution.py
+++ b/solution.py
@@ -12,7 +12,7 @@
 EARLY_VMEM = 34 * 1024 * 1024
 STAGE_VMEM = 34 * 1024 * 1024
 PACK_VMEM = 60 * 1024 * 1024
-SHARE_VMEM = 16 * 1024 * 1024
+SHARE_VMEM = 24 * 1024 * 1024
 BF = jnp.bfloat16
 F32 = jnp.float32
 

time: 109 us -> 109 us (level)
  no operation moved by 1% of the time
where the time goes in v6:
time: 109 us; the launch traced here: 108 us
  Pallas kernels  63.2 us (58%)
  local copies, waits for them, and re-layouts  17.4 us (16%)
  waiting for transfers between devices  13.1 us (12%)
  starting transfers between devices  11.6 us (11%)
  other arithmetic  2.09 us (2%)
    pallas_call x4, Pallas kernels, stage(): pl.pallas_call(functools.partial(stage_kernel, m, own, local, count, len(...  46.7 us
    unnamed x5, local copies, waits for them, and re-layouts  12.5 us
    ppermute x3, waiting for transfers between devices, on_device(): pays.append(lax.ppermute(pays[d], 'expert', ring))  9.62 us
    pallas_call x2, Pallas kernels, send_blocks(): pl.pallas_call(lambda s, *refs: body(s, *refs[k:]), grid_spec=pltpu.Prefe...  5.9 us
    pallas_call x1, Pallas kernels, join_blocks(): pl.pallas_call(functools.partial(join_kernel, len(pieces), low), grid=(st...  5.63 us
    optimization_barrier x1, local copies, waits for them, and re-layouts, on_device(): lax.optimization_barrier((pays[1], others[0], wgu, down_weights))  4.89 us
    ppermute x4, starting transfers between devices, on_device(): others.append(lax.ppermute(pays[d], 'replica', across))  4.47 us
    ppermute x3, starting transfers between devices, on_device(): pays.append(lax.ppermute(pays[d], 'expert', ring))  4.32 us
  transfers between devices with their start and end apart: 14, of which 6 were waited for; matrix products, arithmetic and copies ran while one was open for 18% of the time, Pallas kernels for 51%

profile of v6, /device:TPU:0, one launch (start us, length us, event | category | flops | bytes accessed | tf_op | source)
XLA Modules:
  0.0 108.2 jit_solution(3912821310192719600)
XLA Ops:
  0.6 2.0 %shard_map.101.refs_1_ = bf16[272,1024]{1,0:T(8,128)(2,1)} custom-call(s32[6,128]{1,0:T(8,128)} %bitcast.20, bf16[6,128]{1,0:T(8,128)(2,1)} %bitcast.23, bf16[128,1024]{1,0:T(8,128)(2,1)} %tok_ref.1, bf16[128,1024]{1,0:T(8,128)(2,1)} %cot_ref.1), custom_call_target="tpu_custom_call" | custom-call | tf_op jit(solution)/shard_map/pallas_call | solution.py:63
  2.6 3.0 %collective-permute-start = (bf16[272,1024]{1,0:T(8,128)(2,1)}, bf16[272,1024]{1,0:T(8,128)(2,1)S(1)}, u32[]{:S(2)}, u32[]{:S(2)}) collective-permute-start(bf16[272,1024]{1,0:T(8,128)(2,1)} %shard_map.101.refs_1_), channel_id=1, source_target_pairs={{0,4},{4,8},{8,12},{12,0},{1,5},{5,9},{9,13},{13,1},{2,6},{6,10},{... | collective-permute-start | bytes 1671176 | tf_op jit(solution)/shard_map/ppermute | solution.py:341
  5.7 1.5 %collective-permute-start.1 = (bf16[272,1024]{1,0:T(8,128)(2,1)}, bf16[272,1024]{1,0:T(8,128)(2,1)S(1)}, u32[]{:S(2)}, u32[]{:S(2)}) collective-permute-start(bf16[272,1024]{1,0:T(8,128)(2,1)} %shard_map.101.refs_1_), channel_id=1, source_target_pairs={{0,2},{1,3},{2,0},{3,1},{4,6},{5,7},{6,4},{7,5},{8,10},{9,11},{10,... | collective-permute-start | bytes 1671176 | tf_op jit(solution)/shard_map/ppermute | solution.py:339
  7.2 12.5 %copy.17 = bf16[1024,4,1536]{2,0,1:T(8,128)(2,1)} copy(bf16[1024,4,1536]{2,1,0:T(4,128)(2,1)} %param.10) | data formatting | bytes 25165824 | tf_op args[4]
  19.7 0.8 collective-permute-done.refs_0_
  20.5 1.0 collective-permute-start.2
  21.5 1.5 %collective-permute-start.3 = (bf16[272,1024]{1,0:T(8,128)(2,1)S(1)}, bf16[272,1024]{1,0:T(8,128)(2,1)S(1)}, u32[]{:S(2)}, u32[]{:S(2)}) collective-permute-start(bf16[272,1024]{1,0:T(8,128)(2,1)S(1)} %collective-permute-done.refs_0_), channel_id=1, source_target_pairs={{0,2},{1,3},{2,0},{3,1},{4,6},{5,7},{6,4},{7,5},{8,10},{9,11},{10,... | collective-permute-start | bytes 1671176 | tf_op jit(solution)/shard_map/ppermute | solution.py:339
  23.0 4.9 %copy.18 = bf16[768,4,1024]{2,0,1:T(8,128)(2,1)S(1)} copy(bf16[768,4,1024]{2,1,0:T(4,128)(2,1)} %param.11) | data formatting | bytes 12582912 | tf_op jit(solution)/shard_map/optimization_barrier | solution.py:343
  27.9 12.3 %shard_map.102 = (bf16[4,128,512]{2,1,0:T(8,128)(2,1)S(1)}, bf16[4,128,384]{2,1,0:T(8,128)(2,1)S(1)}, bf16[4,128,1536]{2,1,0:T(8,128)(2,1)S(1)}, bf16[4,128,1024]{2,1,0:T(8,128)(2,1)S(1)}, bf16[272,1024]{1,0:T(8,128)(2,1)S(1)}) custom-call(s32[3]{0:T(128)S(1)} %pad_add_fusion.scal.s, bf16[272,1024]{1,0:T(8,128)(2,1)S(1)} %collective-permute-done.refs_0_, ...), custom_call_target="tpu_custom_call" | custom-call | flops 14000000000 | bytes 25165824 | tf_op jit(solution)/shard_map/pallas_call | solution.py:204
  40.3 1.6 %collective-permute-start.6 = (bf16[272,1024]{1,0:T(8,128)(2,1)S(1)}, bf16[272,1024]{1,0:T(8,128)(2,1)S(1)}, u32[]{:S(2)}, u32[]{:S(2)}) collective-permute-start(bf16[272,1024]{1,0:T(8,128)(2,1)S(1)} %get-tuple-element.51.refs_6_), channel_id=1, source_target_pairs={{0,4},{4,8},{8,12},{12,0},{1,5},{5,9},{9,13},{13,1},{2,6},{6,10},{... | collective-permute-start | bytes 1671176 | tf_op jit(solution)/shard_map/ppermute | solution.py:364
  41.9 0.3 collective-permute-start.4
  42.2 0.5 collective-permute-start.5
  42.7 13.9 %shard_map.103 = (bf16[4,192,512]{2,1,0:T(8,128)(2,1)S(1)}, bf16[4,192,384]{2,1,0:T(8,128)(2,1)S(1)}, bf16[4,192,1536]{2,1,0:T(8,128)(2,1)S(1)}, bf16[4,192,1024...) custom-call(s32[3]{0:T(128)S(1)} %pad_add_fusion.scal.s, ...), custom_call_target="tpu_custom_call" | custom-call | flops 14000000000 | bytes 25165824 | tf_op jit(solution)/shard_map/pallas_call | solution.py:204
  56.6 1.1 collective-permute-done.6
  57.7 0.2 add_convert_fusion.1.refs_5_
  57.9 8.8 %collective-permute-done.4.refs_0_ = bf16[272,1024]{1,0:T(8,128)(2,1)S(1)} collective-permute-done((bf16[272,1024]{1,0:T(8,128)(2,1)S(1)}, bf16[272,1024]{1,0:T(8,128)(2,1)S(1)}, u32[]{:S(2)}, u32[]{:S(2)}) %collective-permute-start.4) | collective-permute-done | bytes 557088 | tf_op jit(solution)/shard_map/ppermute | solution.py:341
  66.7 0.9 collective-permute-start.7
  67.6 12.3 %shard_map.104 = (bf16[4,128,512]{2,1,0:T(8,128)(2,1)S(1)}, bf16[4,128,384]{2,1,0:T(8,128)(2,1)S(1)}, bf16[4,128,1536]{2,1,0:T(8,128)(2,1)S(1)}, bf16[4,128,1024]{2,1,0:T(8,128)(2,1)S(1)}, bf16[272,1024]{1,0:T(8,128)(2,1)S(1)}) custom-call(s32[3]{0:T(128)S(1)} %pad_add_fusion.scal.s, bf16[272,1024]{1,0:T(8,128)(2,1)S(1)} %collective-permute-done.4.refs_0_, ...), custom_call_target="tpu_custom_call" | custom-call | flops 14000000000 | bytes 25165824 | tf_op jit(solution)/shard_map/pallas_call | solution.py:204
  80.0 0.2 collective-permute-done.8
  80.2 0.2 add_convert_fusion.refs_4_
  80.5 8.2 %shard_map.105 = (bf16[4,64,512]{2,1,0:T(8,128)(2,1)S(1)}, bf16[4,64,384]{2,1,0:T(8,128)(2,1)S(1)}, bf16[4,64,1536]{2,1,0:T(8,128)(2,1)S(1)}, bf16[4,64,1024]{2,1,0:T(8,128)(2,1)S(1)}) custom-call(s32[3]{0:T(128)S(1)} %pad_add_fusion.scal.s, bf16[272,1024]{1,0:T(8,128)(2,1)S(1)} %collective-permute-done.7.refs_0_, bf16[4,1024,1536]{2,1,0:T(8,128)(2,1)} %bitcast.19, ...), custom_call_target="tpu_custom_call" | custom-call | flops 7000000000 | bytes 25165824 | tf_op jit(solution)/shard_map/pallas_call | solution.py:204
  88.7 2.9 %shard_map.108 = (bf16[2,256,1536]{2,1,0:T(8,128)(2,1)S(1)}, bf16[2,192,1024]{2,1,0:T(8,128)(2,1)S(1)}, f32[2,192,1024]{2,1,0:T(8,128)S(1)}) custom-call(s32[3]{0:T(128)S(1)} %pad_add_fusion.scal.s, bf16[4,128,512]{2,1,0:T(8,128)(2,1)S(1)} %get-tuple-element.46.refs_0_, bf16[4,192,512]{2,1,0:T(8,128)(2,1)S(1)} %get-tuple-element.49.refs_1_, ...), custom_call_target="tpu_custom_call" | custom-call | bytes 1024 | tf_op jit(solution)/shard_map/pallas_call | solution.py:253
  91.6 3.0 %shard_map.106 = (bf16[2,256,1536]{2,1,0:T(8,128)(2,1)S(1)}, bf16[2,192,1024]{2,1,0:T(8,128)(2,1)S(1)}, f32[2,192,1024]{2,1,0:T(8,128)S(1)}) custom-call(s32[3]{0:T(128)S(1)} %pad_add_fusion.scal.s, bf16[4,128,512]{2,1,0:T(8,128)(2,1)S(1)} %get-tuple-element.46.refs_0_, bf16[4,192,512]{2,1,0:T(8,128)(2,1)S(1)} %get-tuple-element.49.refs_1_, ...), custom_call_target="tpu_custom_call" | custom-call | bytes 1024 | tf_op jit(solution)/shard_map/pallas_call | solution.py:253
  94.7 0.5 collective-permute-start.12
  95.2 3.0 %shard_map.107.own_ref = f32[4,256,1536]{2,1,0:T(8,128)S(1)} custom-call(s32[3]{0:T(128)S(1)} %pad_add_fusion.scal.s, bf16[4,128,512]{2,1,0:T(8,128)(2,1)S(1)} %get-tuple-element.46.refs_0_, bf16[4,192,512]{2,1,0:T(8,128)(2,1)S(1)} %get-tuple-element.49.refs_1_, bf16[4,128,512]{2,1,0:T(8,128)(2,1)S(1)} %get-tuple-element.53.refs_2_, ...), custom_call_target="tpu_custom_call" | custom-call | bytes 1024 | tf_op jit(solution)/shard_map/pallas_call | solution.py:284
  98.1 0.2 collective-permute-start.11
  98.3 0.4 collective-permute-start.13
  98.7 0.6 select_reduce_fusion
  99.3 1.0 add_convert_fusion.2
  100.3 1.1 %collective-permute-done.11.refs_1_ = bf16[2,192,1024]{2,1,0:T(8,128)(2,1)S(1)} collective-permute-done((bf16[2,192,1024]{2,1,0:T(8,128)(2,1)S(1)}, bf16[2,192,1024]{2,1,0:T(8,128)(2,1)S(1)}, u32[]{:S(2)}, u32[]{:S(2)}) %collective-permute-start.11) | collective-permute-done | bytes 786464 | tf_op jit(solution)/shard_map/ppermute | solution.py:378
  101.4 1.1 %collective-permute-done.13.refs_4_ = bf16[2,192,1024]{2,1,0:T(8,128)(2,1)S(1)} collective-permute-done((bf16[2,192,1024]{2,1,0:T(8,128)(2,1)S(1)}, bf16[2,192,1024]{2,1,0:T(8,128)(2,1)S(1)}, u32[]{:S(2)}, u32[]{:S(2)}) %collective-permute-start.13) | collective-permute-done | bytes 786464 | tf_op jit(solution)/shard_map/ppermute | solution.py:378
  102.6 5.6 %shard_map.109 = (f32[256,4,1536]{2,1,0:T(4,128)}, f32[192,4,1024]{2,1,0:T(4,128)}) custom-call(f32[4,256,1536]{2,1,0:T(8,128)S(1)} %shard_map.107.own_ref, bf16[2,256,1536]{2,1,0:T(8,128)(2,1)S(1)} %collective-permute-done.10.refs_0_, bf16[2,192,1024]{2,1,0:T(8,128)(2,1)S(1)} %collective-permute-done.11.refs_1_, ...), custom_call_target="tpu_custom_call" | custom-call | flops 5000000000 | bytes 16777216 | tf_op jit(solution)/shard_map/pallas_call | solution.py:316
  (18 shorter events, 0.3 us)
Async XLA Ops:
  2.6 17.9 %collective-permute-start = (bf16[272,1024]{1,0:T(8,128)(2,1)}, bf16[272,1024]{1,0:T(8,128)(2,1)S(1)}, u32[]{:S(2)}, u32[]{:S(2)}) collective-permute-start(bf16[272,1024]{1,0:T(8,128)(2,1)} %shard_map.101.refs_1_), channel_id=1, source_target_pairs={{0,4},{4,8},{8,12},{12,0},{1,5},{5,9},{9,13},{13,1},{2,6},{6,10},{... | collective-permute-start | bytes 1671176 | tf_op jit(solution)/shard_map/ppermute | solution.py:341
  5.7 14.9 %collective-permute-start.1 = (bf16[272,1024]{1,0:T(8,128)(2,1)}, bf16[272,1024]{1,0:T(8,128)(2,1)S(1)}, u32[]{:S(2)}, u32[]{:S(2)}) collective-permute-start(bf16[272,1024]{1,0:T(8,128)(2,1)} %shard_map.101.refs_1_), channel_id=1, source_target_pairs={{0,2},{1,3},{2,0},{3,1},{4,6},{5,7},{6,4},{7,5},{8,10},{9,11},{10,... | collective-permute-start | bytes 1671176 | tf_op jit(solution)/shard_map/ppermute | solution.py:339
  20.5 19.8 %collective-permute-start.2 = (bf16[272,1024]{1,0:T(8,128)(2,1)S(1)}, bf16[272,1024]{1,0:T(8,128)(2,1)S(1)}, u32[]{:S(2)}, u32[]{:S(2)}) collective-permute-start(bf16[272,1024]{1,0:T(8,128)(2,1)S(1)} %collective-permute-done.refs_0_), channel_id=1, source_target_pairs={{0,4},{4,8},{8,12},{12,0},{1,5},{5,9},{9,13},{13,1},{2,6},{6,10},{... | collective-permute-start | bytes 1671176 | tf_op jit(solution)/shard_map/ppermute | solution.py:341
  21.5 21.2 %collective-permute-start.3 = (bf16[272,1024]{1,0:T(8,128)(2,1)S(1)}, bf16[272,1024]{1,0:T(8,128)(2,1)S(1)}, u32[]{:S(2)}, u32[]{:S(2)}) collective-permute-start(bf16[272,1024]{1,0:T(8,128)(2,1)S(1)} %collective-permute-done.refs_0_), channel_id=1, source_target_pairs={{0,2},{1,3},{2,0},{3,1},{4,6},{5,7},{6,4},{7,5},{8,10},{9,11},{10,... | collective-permute-start | bytes 1671176 | tf_op jit(solution)/shard_map/ppermute | solution.py:339
  27.9 14.8 %copy-start = (bf16[272,1024]{1,0:T(8,128)(2,1)S(1)}, bf16[272,1024]{1,0:T(8,128)(2,1)}, u32[]{:S(2)}) copy-start(bf16[272,1024]{1,0:T(8,128)(2,1)} %shard_map.101.refs_1_) | copy-start | bytes 1671172
  40.3 17.4 %collective-permute-start.6 = (bf16[272,1024]{1,0:T(8,128)(2,1)S(1)}, bf16[272,1024]{1,0:T(8,128)(2,1)S(1)}, u32[]{:S(2)}, u32[]{:S(2)}) collective-permute-start(bf16[272,1024]{1,0:T(8,128)(2,1)S(1)} %get-tuple-element.51.refs_6_), channel_id=1, source_target_pairs={{0,4},{4,8},{8,12},{12,0},{1,5},{5,9},{9,13},{13,1},{2,6},{6,10},{... | collective-permute-start | bytes 1671176 | tf_op jit(solution)/shard_map/ppermute | solution.py:364
  41.9 24.8 %collective-permute-start.4 = (bf16[272,1024]{1,0:T(8,128)(2,1)S(1)}, bf16[272,1024]{1,0:T(8,128)(2,1)S(1)}, u32[]{:S(2)}, u32[]{:S(2)}) collective-permute-start(bf16[272,1024]{1,0:T(8,128)(2,1)S(1)} %collective-permute-done.2.refs_0_), channel_id=1, source_target_pairs={{0,4},{4,8},{8,12},{12,0},{1,5},{5,9},{9,13},{13,1},{2,6},{6,10},{... | collective-permute-start | bytes 1671176 | tf_op jit(solution)/shard_map/ppermute | solution.py:341
  42.2 25.4 %collective-permute-start.5 = (bf16[272,1024]{1,0:T(8,128)(2,1)S(1)}, bf16[272,1024]{1,0:T(8,128)(2,1)S(1)}, u32[]{:S(2)}, u32[]{:S(2)}) collective-permute-start(bf16[272,1024]{1,0:T(8,128)(2,1)S(1)} %collective-permute-done.2.refs_0_), channel_id=1, source_target_pairs={{0,2},{1,3},{2,0},{3,1},{4,6},{5,7},{6,4},{7,5},{8,10},{9,11},{10,... | collective-permute-start | bytes 1671176 | tf_op jit(solution)/shard_map/ppermute | solution.py:339
  66.7 13.5 %collective-permute-start.8 = (bf16[272,1024]{1,0:T(8,128)(2,1)S(1)}, bf16[272,1024]{1,0:T(8,128)(2,1)S(1)}, u32[]{:S(2)}, u32[]{:S(2)}) collective-permute-start(bf16[272,1024]{1,0:T(8,128)(2,1)S(1)} %add_convert_fusion.1.refs_5_), channel_id=1, source_target_pairs={{0,4},{4,8},{8,12},{12,0},{1,5},{5,9},{9,13},{13,1},{2,6},{6,10},{... | collective-permute-start | bytes 1671176 | tf_op jit(solution)/shard_map/ppermute | solution.py:364
  66.7 13.8 %collective-permute-start.7 = (bf16[272,1024]{1,0:T(8,128)(2,1)S(1)}, bf16[272,1024]{1,0:T(8,128)(2,1)S(1)}, u32[]{:S(2)}, u32[]{:S(2)}) collective-permute-start(bf16[272,1024]{1,0:T(8,128)(2,1)S(1)} %collective-permute-done.4.refs_0_), channel_id=1, source_target_pairs={{0,2},{1,3},{2,0},{3,1},{4,6},{5,7},{6,4},{7,5},{8,10},{9,11},{10,... | collective-permute-start | bytes 1671176 | tf_op jit(solution)/shard_map/ppermute | solution.py:339
  80.4 14.3 %collective-permute-start.9 = (bf16[272,1024]{1,0:T(8,128)(2,1)S(1)}, bf16[272,1024]{1,0:T(8,128)(2,1)S(1)}, u32[]{:S(2)}, u32[]{:S(2)}) collective-permute-start(bf16[272,1024]{1,0:T(8,128)(2,1)S(1)} %add_convert_fusion.refs_4_), channel_id=1, source_target_pairs={{0,4},{4,8},{8,12},{12,0},{1,5},{5,9},{9,13},{13,1},{2,6},{6,10},{... | collective-permute-start | bytes 1671176 | tf_op jit(solution)/shard_map/ppermute | solution.py:369
  94.6 8.0 %collective-permute-start.10 = (bf16[2,256,1536]{2,1,0:T(8,128)(2,1)S(1)}, bf16[2,256,1536]{2,1,0:T(8,128)(2,1)S(1)}, u32[]{:S(2)}, u32[]{:S(2)}) collective-permute-start(bf16[2,256,1536]{2,1,0:T(8,128)(2,1)S(1)} %get-tuple-element.71), channel_id=1, source_target_pairs={{0,1},{1,0},{2,3},{3,2},{4,5},{5,4},{6,7},{7,6},{8,9},{9,8},{10,11... | collective-permute-start | bytes 4718600 | tf_op jit(solution)/shard_map/ppermute | solution.py:377
  94.7 4.0 %copy-start.1 = (s32[128,6]{0,1:T(8,128)S(1)}, s32[128,6]{0,1:T(8,128)}, u32[]{:S(2)}) copy-start(s32[128,6]{0,1:T(8,128)} %param.7) | copy-start | bytes 9220
  94.7 7.9 %collective-permute-start.12 = (bf16[2,256,1536]{2,1,0:T(8,128)(2,1)S(1)}, bf16[2,256,1536]{2,1,0:T(8,128)(2,1)S(1)}, u32[]{:S(2)}, u32[]{:S(2)}) collective-permute-start(bf16[2,256,1536]{2,1,0:T(8,128)(2,1)S(1)} %get-tuple-element.74.refs_8_), channel_id=1, source_target_pairs={{0,1},{1,0},{2,3},{3,2},{4,5},{5,4},{6,7},{7,6},{8,9},{9,8},{10,11... | collective-permute-start | bytes 4718600 | tf_op jit(solution)/shard_map/ppermute | solution.py:377
  98.1 3.3 %collective-permute-start.11 = (bf16[2,192,1024]{2,1,0:T(8,128)(2,1)S(1)}, bf16[2,192,1024]{2,1,0:T(8,128)(2,1)S(1)}, u32[]{:S(2)}, u32[]{:S(2)}) collective-permute-start(bf16[2,192,1024]{2,1,0:T(8,128)(2,1)S(1)} %get-tuple-element.72), channel_id=1, source_target_pairs={{0,1},{1,0},{2,3},{3,2},{4,5},{5,4},{6,7},{7,6},{8,9},{9,8},{10,11... | collective-permute-start | bytes 2359304 | tf_op jit(solution)/shard_map/ppermute | solution.py:378
  98.3 4.2 %collective-permute-start.13 = (bf16[2,192,1024]{2,1,0:T(8,128)(2,1)S(1)}, bf16[2,192,1024]{2,1,0:T(8,128)(2,1)S(1)}, u32[]{:S(2)}, u32[]{:S(2)}) collective-permute-start(bf16[2,192,1024]{2,1,0:T(8,128)(2,1)S(1)} %get-tuple-element.75.refs_9_), channel_id=1, source_target_pairs={{0,1},{1,0},{2,3},{3,2},{4,5},{5,4},{6,7},{7,6},{8,9},{9,8},{10,11... | collective-permute-start | bytes 2359304 | tf_op jit(solution)/shard_map/ppermute | solution.py:378
